TPU v7x, 32 devices: a whole 2x2x4 slice. The times are simulated.
32 devices in a mesh: fsdp: 8 (over z, y), rep: 4 (over x, core).
Axes of the slice: x: 2, y: 2, z: 4, core: 2. Of those that a mesh axis runs over, the one named last changes fastest.
Arguments:
- clips_in: bfloat16 [96, 392, 2048], P(('fsdp', 'rep')), may hold values from -6 to 6
- view_ids: int32 [96], P(('fsdp', 'rep')), may hold values from 0 to 32, as said below
- seg_order: int32 [96, 8], P(('fsdp', 'rep')), may hold values from 0 to 7, each once within a row
- reduce_weight: bfloat16 [2048, 512], P('fsdp'), may hold values from -0.125 to 0.125
- gain1: bfloat16 [512], P('fsdp'), may hold values from 0.25 to 1.75
- shift1: bfloat16 [512], P('fsdp'), may hold values from -3 to 3
- diff_weight: bfloat16 [4608, 512], P('fsdp'), may hold values from -0.09375 to 0.09375
- pooled_weight: bfloat16 [512, 512], P('fsdp'), may hold values from -0.25 to 0.25
- spatial_weight: bfloat16 [4608, 512], P('fsdp'), may hold values from -0.09375 to 0.09375
- gain2: bfloat16 [512], P('fsdp'), may hold values from 0.25 to 1.75
- shift2: bfloat16 [512], P('fsdp'), may hold values from -3 to 3
- expand_weight: bfloat16 [512, 2048], P('fsdp'), may hold values from -0.25 to 0.25
- gain3: bfloat16 [2048], P('fsdp'), may hold values from 0.25 to 1.75
- shift3: bfloat16 [2048], P('fsdp'), may hold values from -3 to 3
- class_weight: bfloat16 [2048, 174], P('fsdp'), may hold values from -0.125 to 0.125
- video_cotangent: float32 [32, 174], P(('fsdp', 'rep')), may hold values from -6 to 6
Outputs:
- video_logits: float32 [32, 174], P(('fsdp', 'rep'))
- clips_grad: bfloat16 [96, 392, 2048], P(('fsdp', 'rep'))
- grad_reduce: float32 [2048, 512], P('fsdp')
- grad_gain1: float32 [512], P('fsdp')
- grad_shift1: float32 [512], P('fsdp')
- grad_diff: float32 [4608, 512], P('fsdp')
- grad_pooled: float32 [512, 512], P('fsdp')
- grad_spatial: float32 [4608, 512], P('fsdp')
- grad_gain2: float32 [512], P('fsdp')
- grad_shift2: float32 [512], P('fsdp')
- grad_expand: float32 [512, 2048], P('fsdp')
- grad_gain3: float32 [2048], P('fsdp')
- grad_shift3: float32 [2048], P('fsdp')
- grad_class: float32 [2048, 174], P('fsdp')
Inputs may be any that keep to these rules, and one draw needn't show every extreme that they name: `view_ids`: every video 0 to 31 owns 1 to 3 clip slots, some video exactly 3; the other slots are empty and hold 32. `seg_order`: each row is a permutation of the 8 segments.
All inputs are finite; a program needn't handle non-finite values.
Results may differ from a plain program's by a relative error of at most 0.018.
Values may be sent and summed in bfloat16 or wider, within the bound.
No kernel may reach another device: no remote copies, remote signals or barrier semaphores. Data moves between devices by JAX's collectives and lax.ppermute only.
A program may use at most 256 MiB of HBM per device.

v0:
```python
import jax
import jax.numpy as jnp
from jax import lax
from jax.sharding import PartitionSpec as P

D = 2048
MID = 512
SEGS = 8
SIDE = 7
FRAME_ROWS = 392


epsilon = 1e-05
highest = lax.Precision.HIGHEST


def patches(field):
    extent = field.shape[1]
    padded = jnp.pad(field, ((0, 0), (1, 1), (1, 1), (0, 0)))
    pieces = [
        padded[:, row_offset : row_offset + extent, column_offset : column_offset + extent, :]
        for row_offset in range(3)
        for column_offset in range(3)
    ]
    joined = jnp.concatenate(pieces, axis=3)
    return joined.reshape(-1, joined.shape[3])


def flipped(kernel):
    outputs = kernel.shape[1]
    taps = kernel.reshape(9, -1, outputs)[::-1]
    return jnp.swapaxes(taps, 1, 2).reshape(-1, taps.shape[1])


def temporal_mix(order):
    length = order.shape[1]
    stations = jnp.arange(length, dtype=jnp.int32)
    places = (order[:, :, None] == stations[None, None, :]).astype(jnp.float32)
    current = places[:, :-1, :]
    upcoming = places[:, 1:, :]
    return jnp.sum(
        current[:, :, :, None] * (upcoming[:, :, None, :] - current[:, :, None, :]), axis=1
    )


def silu_slope(values):
    sigma_part = jax.nn.sigmoid(values)
    return sigma_part * (1.0 + values * (1.0 - sigma_part))


def moments(values, alive_rows):
    total_sum, weight_sum = lax.psum(
        (jnp.sum(alive_rows * values, axis=0), jnp.sum(alive_rows)), ("fsdp", "rep")
    )
    center = total_sum / weight_sum
    deviation = values - center
    spread = (
        lax.psum(jnp.sum(alive_rows * deviation * deviation, axis=0), ("fsdp", "rep")) / weight_sum
    )
    return (center, lax.rsqrt(spread + epsilon), weight_sum)


def norm_back(grad_out, normed, alive_rows, gain, scale, weight_sum):
    shift_grad, gain_grad = lax.psum(
        (jnp.sum(alive_rows * grad_out, axis=0), jnp.sum(alive_rows * grad_out * normed, axis=0)),
        ("fsdp", "rep"),
    )
    grad_in = (
        gain * scale * (grad_out - alive_rows * (shift_grad + normed * gain_grad) / weight_sum)
    )
    return (grad_in, gain_grad, shift_grad)


def local(
    clips_in,
    view_ids,
    seg_order,
    reduce_weight,
    gain1,
    shift1,
    diff_weight,
    pooled_weight,
    spatial_weight,
    gain2,
    shift2,
    expand_weight,
    gain3,
    shift3,
    class_weight,
    video_cotangent,
):
    clip_count = clips_in.shape[0]
    planes = clip_count * SEGS
    pixels = SIDE * SIDE
    videos_all = video_cotangent.shape[0] * lax.axis_size("fsdp") * lax.axis_size("rep")
    alive_clips = (view_ids < videos_all).astype(jnp.float32)
    alive_rows = jnp.repeat(alive_clips, FRAME_ROWS)[:, None]
    members = (view_ids[:, None] == jnp.arange(videos_all, dtype=jnp.int32)[None, :]).astype(
        jnp.float32
    )
    mixing_table = temporal_mix(seg_order)
    shards = (
        reduce_weight,
        gain1,
        shift1,
        diff_weight,
        pooled_weight,
        spatial_weight,
        gain2,
        shift2,
        expand_weight,
        gain3,
        shift3,
        class_weight,
    )
    gathered = (
        lax.all_gather(shards[0], "fsdp", axis=0, tiled=True),
        lax.all_gather(shards[1], "fsdp", axis=0, tiled=True),
        lax.all_gather(shards[2], "fsdp", axis=0, tiled=True),
        lax.all_gather(shards[3], "fsdp", axis=0, tiled=True),
        lax.all_gather(shards[4], "fsdp", axis=0, tiled=True),
        lax.all_gather(shards[5], "fsdp", axis=0, tiled=True),
        lax.all_gather(shards[6], "fsdp", axis=0, tiled=True),
        lax.all_gather(shards[7], "fsdp", axis=0, tiled=True),
        lax.all_gather(shards[8], "fsdp", axis=0, tiled=True),
        lax.all_gather(shards[9], "fsdp", axis=0, tiled=True),
        lax.all_gather(shards[10], "fsdp", axis=0, tiled=True),
        lax.all_gather(shards[11], "fsdp", axis=0, tiled=True),
    )
    (
        w_reduce,
        g_one,
        s_one,
        w_diff,
        w_pooled,
        w_spatial,
        g_two,
        s_two,
        w_expand,
        g_three,
        s_three,
        w_class,
    ) = gathered
    flat_in = clips_in.reshape(-1, D)
    first_out = jnp.dot(flat_in, w_reduce, preferred_element_type=jnp.float32)
    center_one, scale_one, weight_sum = moments(first_out, alive_rows)
    normed_one = (first_out - center_one) * scale_one
    pre_one = normed_one * g_one.astype(jnp.float32) + s_one.astype(jnp.float32)
    hidden_one = jax.nn.silu(pre_one).reshape(clip_count, SEGS, pixels, MID)
    difference = jnp.einsum("cji,cipn->cjpn", mixing_table, hidden_one, precision=highest).astype(
        jnp.bfloat16
    )
    summary = (
        jnp.mean(difference.astype(jnp.float32), axis=2).astype(jnp.bfloat16).reshape(planes, MID)
    )
    difference_patches = patches(difference.reshape(planes, SIDE, SIDE, MID))
    local_term = jnp.dot(difference_patches, w_diff, preferred_element_type=jnp.float32).reshape(
        planes, pixels, MID
    )
    global_term = jnp.dot(summary, w_pooled, preferred_element_type=jnp.float32)
    gating = jax.nn.sigmoid(local_term + global_term[:, None, :]).reshape(
        clip_count, SEGS, pixels, MID
    )
    boosted = (hidden_one * (1.0 + gating)).astype(jnp.bfloat16)
    boosted_patches = patches(boosted.reshape(planes, SIDE, SIDE, MID))
    second_out = jnp.dot(boosted_patches, w_spatial, preferred_element_type=jnp.float32)
    center_two, scale_two, weight_sum = moments(second_out, alive_rows)
    normed_two = (second_out - center_two) * scale_two
    pre_two = normed_two * g_two.astype(jnp.float32) + s_two.astype(jnp.float32)
    hidden_two = jax.nn.silu(pre_two).astype(jnp.bfloat16)
    third_out = jnp.dot(hidden_two, w_expand, preferred_element_type=jnp.float32)
    center_three, scale_three, weight_sum = moments(third_out, alive_rows)
    normed_three = (third_out - center_three) * scale_three
    summed = (
        normed_three * g_three.astype(jnp.float32)
        + s_three.astype(jnp.float32)
        + flat_in.astype(jnp.float32)
    )
    outcome = jax.nn.silu(summed)
    pooled = jnp.mean(outcome.reshape(clip_count, FRAME_ROWS, D), axis=1).astype(jnp.bfloat16)
    clip_logits = jnp.dot(pooled, w_class, preferred_element_type=jnp.float32)
    video_sums = jnp.dot(members.T, clip_logits, precision=highest)
    video_total, video_count = (
        lax.psum_scatter(video_sums, ("fsdp", "rep"), scatter_dimension=0, tiled=True),
        lax.psum_scatter(
            jnp.sum(members, axis=0), ("fsdp", "rep"), scatter_dimension=0, tiled=True
        ),
    )
    video_logits = video_total / video_count[:, None]
    backward_weights = (
        lax.all_gather(shards[0], "fsdp", axis=0, tiled=True),
        lax.all_gather(shards[1], "fsdp", axis=0, tiled=True),
        lax.all_gather(shards[2], "fsdp", axis=0, tiled=True),
        lax.all_gather(shards[3], "fsdp", axis=0, tiled=True),
        lax.all_gather(shards[4], "fsdp", axis=0, tiled=True),
        lax.all_gather(shards[5], "fsdp", axis=0, tiled=True),
        lax.all_gather(shards[6], "fsdp", axis=0, tiled=True),
        lax.all_gather(shards[7], "fsdp", axis=0, tiled=True),
        lax.all_gather(shards[8], "fsdp", axis=0, tiled=True),
        lax.all_gather(shards[9], "fsdp", axis=0, tiled=True),
        lax.all_gather(shards[10], "fsdp", axis=0, tiled=True),
        lax.all_gather(shards[11], "fsdp", axis=0, tiled=True),
    )
    (
        w_reduce,
        g_one,
        s_one,
        w_diff,
        w_pooled,
        w_spatial,
        g_two,
        s_two,
        w_expand,
        g_three,
        s_three,
        w_class,
    ) = backward_weights
    video_share = video_cotangent / video_count[:, None]
    every_share = lax.all_gather(video_share, ("fsdp", "rep"), axis=0, tiled=True)
    logit_grad = jnp.dot(members, every_share, precision=highest).astype(jnp.bfloat16)
    grad_class = jnp.dot(pooled.T, logit_grad, preferred_element_type=jnp.float32)
    pooled_grad = jnp.dot(logit_grad, w_class.T, preferred_element_type=jnp.float32)
    summed_grad = (
        pooled_grad[:, None, :] / FRAME_ROWS * silu_slope(summed).reshape(clip_count, FRAME_ROWS, D)
    ).reshape(-1, D)
    third_grad, gain_three_grad, shift_three_grad = norm_back(
        summed_grad, normed_three, alive_rows, g_three.astype(jnp.float32), scale_three, weight_sum
    )
    third_low = third_grad.astype(jnp.bfloat16)
    grad_expand = jnp.dot(hidden_two.T, third_low, preferred_element_type=jnp.float32)
    pre_two_grad = jnp.dot(third_low, w_expand.T, preferred_element_type=jnp.float32) * silu_slope(
        pre_two
    )
    second_grad, gain_two_grad, shift_two_grad = norm_back(
        pre_two_grad, normed_two, alive_rows, g_two.astype(jnp.float32), scale_two, weight_sum
    )
    second_low = second_grad.astype(jnp.bfloat16)
    grad_spatial = jnp.dot(boosted_patches.T, second_low, preferred_element_type=jnp.float32)
    boosted_grad = jnp.dot(
        patches(second_low.reshape(planes, SIDE, SIDE, MID)),
        flipped(w_spatial),
        preferred_element_type=jnp.float32,
    ).reshape(clip_count, SEGS, pixels, MID)
    hidden_one_grad = boosted_grad * (1.0 + gating)
    gate_grad = (
        (boosted_grad * hidden_one * gating * (1.0 - gating))
        .astype(jnp.bfloat16)
        .reshape(planes, pixels, MID)
    )
    grad_diff = jnp.dot(
        difference_patches.T, gate_grad.reshape(-1, MID), preferred_element_type=jnp.float32
    )
    gate_sums = jnp.sum(gate_grad.astype(jnp.float32), axis=1)
    grad_pooled = jnp.dot(summary.astype(jnp.float32).T, gate_sums, precision=highest)
    difference_grad = jnp.dot(
        patches(gate_grad.reshape(planes, SIDE, SIDE, MID)),
        flipped(w_diff),
        preferred_element_type=jnp.float32,
    ).reshape(planes, pixels, MID)
    summary_grad = jnp.dot(gate_sums, w_pooled.astype(jnp.float32).T, precision=highest)
    difference_grad = (difference_grad + summary_grad[:, None, :] / pixels).reshape(
        clip_count, SEGS, pixels, MID
    )
    hidden_one_grad = hidden_one_grad + jnp.einsum(
        "cji,cjpn->cipn", mixing_table, difference_grad, precision=highest
    )
    pre_one_grad = hidden_one_grad.reshape(-1, MID) * silu_slope(pre_one)
    first_grad, gain_one_grad, shift_one_grad = norm_back(
        pre_one_grad, normed_one, alive_rows, g_one.astype(jnp.float32), scale_one, weight_sum
    )
    first_low = first_grad.astype(jnp.bfloat16)
    grad_reduce = jnp.dot(flat_in.T, first_low, preferred_element_type=jnp.float32)
    input_grad = jnp.dot(first_low, w_reduce.T, preferred_element_type=jnp.float32) + summed_grad
    clips_grad = input_grad.astype(jnp.bfloat16).reshape(clip_count, FRAME_ROWS, D)
    partial_grads = (grad_reduce, grad_diff, grad_pooled, grad_spatial, grad_expand, grad_class)
    shard_sums = (
        lax.psum_scatter(partial_grads[0], "fsdp", scatter_dimension=0, tiled=True),
        lax.psum_scatter(partial_grads[1], "fsdp", scatter_dimension=0, tiled=True),
        lax.psum_scatter(partial_grads[2], "fsdp", scatter_dimension=0, tiled=True),
        lax.psum_scatter(partial_grads[3], "fsdp", scatter_dimension=0, tiled=True),
        lax.psum_scatter(partial_grads[4], "fsdp", scatter_dimension=0, tiled=True),
        lax.psum_scatter(partial_grads[5], "fsdp", scatter_dimension=0, tiled=True),
    )
    reduced = lax.psum(
        (shard_sums[0], shard_sums[1], shard_sums[2], shard_sums[3], shard_sums[4], shard_sums[5]),
        "rep",
    )
    shard_index = lax.axis_index("fsdp")
    fsdp_count = lax.axis_size("fsdp")

    def own_piece(vector):
        piece_length = vector.shape[0] // fsdp_count
        return lax.dynamic_slice_in_dim(vector, shard_index * piece_length, piece_length)

    return (
        video_logits,
        clips_grad,
        reduced[0],
        own_piece(gain_one_grad),
        own_piece(shift_one_grad),
        reduced[1],
        reduced[2],
        reduced[3],
        own_piece(gain_two_grad),
        own_piece(shift_two_grad),
        reduced[4],
        own_piece(gain_three_grad),
        own_piece(shift_three_grad),
        reduced[5],
    )


def solution(mesh):
    placed = (
        P(("fsdp", "rep"), None, None),
        P(("fsdp", "rep")),
        P(("fsdp", "rep"), None),
        P("fsdp", None),
        P("fsdp"),
        P("fsdp"),
        P("fsdp", None),
        P("fsdp", None),
        P("fsdp", None),
        P("fsdp"),
        P("fsdp"),
        P("fsdp", None),
        P("fsdp"),
        P("fsdp"),
        P("fsdp", None),
        P(("fsdp", "rep"), None),
    )
    return jax.shard_map(
        local,
        mesh=mesh,
        in_specs=placed,
        out_specs=(
            P(("fsdp", "rep"), None),
            P(("fsdp", "rep"), None, None),
            P("fsdp", None),
            P("fsdp"),
            P("fsdp"),
            P("fsdp", None),
            P("fsdp", None),
            P("fsdp", None),
            P("fsdp"),
            P("fsdp"),
            P("fsdp", None),
            P("fsdp"),
            P("fsdp"),
            P("fsdp", None),
        ),
        check_vma=False,
    )
```

profile of v0, /device:TPU:0, one launch (start us, length us, event | category | flops | bytes accessed | tf_op | source)
XLA Modules:
  0.0 1466.7 jit_solution(17218942985243043548)
XLA Ops:
  18.7 23.2 %all-reduce.16 = (bf16[512]{0:T(512)(128)(2,1)S(1)}, bf16[512]{0:T(512)(128)(2,1)S(1)}, bf16[512]{0:T(512)(128)(2,1)S(1)}, bf16[512]{0:T(512)(128)(2,1)S(1)}) all-reduce(bf16[512]{0:T(512)(128)(2,1)S(1)} %dynamic-update-slice.1, bf16[512]{0:T(512)(128)(2,1)S(1)} %dynamic-update-slice, ...), channel_id=1, replica_groups=mesh['fsdp'=8,'rep'=4] {'fsdp'}, use_global_device_ids=true, to_apply=%add.5 | all-reduce | flops 2048 | bytes 8192
  42.0 16.4 %all-gather.1 = bf16[8,1,256]{2,1,0:T(2,128)(2,1)S(1)} all-gather(bf16[1,1,256]{2,1,0:T(2,128)(2,1)S(1)} %reshape.254), channel_id=1, replica_groups=mesh['fsdp'=8,'rep'=4] {'fsdp'}, dimensions={0}, use_global_device_ids=true | all-gather | bytes 4608 | tf_op jit(solution)/shard_map/all_gather | solution.py:127
  58.4 18.2 %all-gather = bf16[8,1,256]{2,1,0:T(2,128)(2,1)S(1)} all-gather(bf16[1,1,256]{2,1,0:T(2,128)(2,1)S(1)} %reshape.252), channel_id=1, replica_groups=mesh['fsdp'=8,'rep'=4] {'fsdp'}, dimensions={0}, use_global_device_ids=true | all-gather | bytes 4608 | tf_op jit(solution)/shard_map/all_gather | solution.py:126
  77.6 35.4 %all_gather.52 = bf16[512,512]{1,0:T(8,128)(2,1)} all-gather(bf16[64,512]{1,0:T(8,128)(2,1)} %param.23), channel_id=1, replica_groups=mesh['fsdp'=8,'rep'=4] {'fsdp'}, dimensions={0}, use_global_device_ids=true | all-gather | bytes 589824 | tf_op jit(solution)/shard_map/all_gather | solution.py:121
  113.0 33.4 %all_gather.59 = bf16[2048,174]{0,1:T(8,128)(2,1)S(1)} all-gather(bf16[256,174]{0,1:T(8,128)(2,1)S(1)} %copy-done.64), channel_id=1, replica_groups=mesh['fsdp'=8,'rep'=4] {'fsdp'}, dimensions={0}, use_global_device_ids=true | all-gather | bytes 801792 | tf_op jit(solution)/shard_map/all_gather | solution.py:128
  146.5 5.3 multiply_reduce_fusion.6
  151.8 38.8 %all-reduce.14 = (f32[512]{0:T(512)S(1)}, f32[]{:T(128)}) all-reduce(f32[512]{0:T(512)S(1)} %get-tuple-element.144, f32[]{:T(128)} %broadcast_reduce_fusion), channel_id=1, replica_groups=mesh['fsdp'=8,'rep'=4] {'fsdp','rep'}, use_global_device_ids=true, to_apply=%region_1.0 | all-reduce | flops 513 | bytes 4104 | tf_op jit(solution)/shard_map/psum | solution.py:52
  191.6 44.8 %psum.141 = f32[512]{0:T(512)S(1)} all-reduce(f32[512]{0:T(512)S(1)} %fusion.5), channel_id=1, replica_groups=mesh['fsdp'=8,'rep'=4] {'fsdp','rep'}, use_global_device_ids=true, to_apply=%region_5.0 | all-reduce | flops 512 | bytes 4096 | tf_op jit(solution)/shard_map/psum | solution.py:58
  239.8 3.2 reshape.228
  243.1 3.4 reshape.227
  246.5 5.1 convert_reduce_fusion.1
  268.0 13.0 broadcast_add_fusion
  281.0 3.7 add.208
  284.7 3.3 copy.157
  289.7 4.6 pad_slice_fusion.8
  294.3 3.2 concatenate.120
  297.5 3.2 concatenate.121
  300.6 3.2 concatenate.122
  303.8 3.2 concatenate.119
  311.6 4.0 copy-done.60
  315.5 3.2 concatenate.126
  318.7 3.2 concatenate.123
  321.9 3.1 concatenate.124
  325.0 3.2 concatenate.125
  328.2 2.6 constant_dynamic-update-slice_fusion.3
  334.3 12.0 multiply_reduce_fusion.5
  346.3 38.6 %psum.142 = f32[512]{0:T(512)S(1)} all-reduce(f32[512]{0:T(512)S(1)} %get-tuple-element.150), channel_id=1, replica_groups=mesh['fsdp'=8,'rep'=4] {'fsdp','rep'}, use_global_device_ids=true, to_apply=%region_9.10 | all-reduce | flops 512 | bytes 4096 | tf_op jit(solution)/shard_map/psum | solution.py:52
  387.6 41.5 %psum.143 = f32[512]{0:T(512)S(1)} all-reduce(f32[512]{0:T(512)S(1)} %fusion.6), channel_id=1, replica_groups=mesh['fsdp'=8,'rep'=4] {'fsdp','rep'}, use_global_device_ids=true, to_apply=%region_11.12 | all-reduce | flops 512 | bytes 4096 | tf_op jit(solution)/shard_map/psum | solution.py:58
  429.8 8.9 multiply_reduce_fusion.1
  438.7 38.5 %psum.144 = f32[2048]{0:T(1024)S(1)} all-reduce(f32[2048]{0:T(1024)S(1)} %get-tuple-element.152), channel_id=1, replica_groups=mesh['fsdp'=8,'rep'=4] {'fsdp','rep'}, use_global_device_ids=true, to_apply=%region_13.14 | all-reduce | flops 2048 | bytes 16384 | tf_op jit(solution)/shard_map/psum | solution.py:52
  477.9 5.1 fusion
  483.0 41.6 %all-reduce.13 = (f32[2048]{0:T(1024)S(1)}, f32[32]{0:T(128)S(1)}) all-reduce(f32[2048]{0:T(1024)S(1)} %fusion, f32[32]{0:T(128)S(1)} %convert_reduce_fusion.2), channel_id=1, replica_groups=mesh['fsdp'=8,'rep'=4] {'fsdp','rep'}, use_global_device_ids=true, to_apply=%region_15.16 | all-reduce | flops 2080 | bytes 16640 | tf_op jit(solution)/shard_map/psum | solution.py:58
  525.9 39.7 %all-gather.2 = f32[32,1,174]{2,1,0:T(1,128)S(1)} all-gather(f32[1,1,174]{2,1,0:T(1,128)S(1)} %divide_bitcast_fusion), channel_id=1, replica_groups=mesh['fsdp'=8,'rep'=4] {'fsdp','rep'}, dimensions={0}, use_global_device_ids=true | all-gather | bytes 22968 | tf_op jit(solution)/shard_map/all_gather | solution.py:219
  566.6 14.1 multiply_reduce_fusion.2
  580.7 37.0 %all-reduce.12 = (f32[2048]{0:T(1024)S(1)}, f32[2048]{0:T(1024)S(1)}) all-reduce(f32[2048]{0:T(1024)S(1)} %get-tuple-element.71, f32[2048]{0:T(1024)S(1)} %get-tuple-element.70), channel_id=1, replica_groups=mesh['fsdp'=8,'rep'=4] {'fsdp','rep'}, use_global_device_ids=true, to_apply=%region_23.24 | all-reduce | flops 4096 | bytes 32768 | tf_op jit(solution)/shard_map/psum | solution.py:64
  617.7 9.3 multiply_convert_fusion
  627.1 5.3 multiply_reduce_fusion.8
  632.4 41.4 %all-reduce.11 = (f32[512]{0:T(512)S(1)}, f32[512]{0:T(512)S(1)}) all-reduce(f32[512]{0:T(512)S(1)} %get-tuple-element.75, f32[512]{0:T(512)S(1)} %get-tuple-element.74), channel_id=1, replica_groups=mesh['fsdp'=8,'rep'=4] {'fsdp','rep'}, use_global_device_ids=true, to_apply=%region_27.28 | all-reduce | flops 1024 | bytes 8192 | tf_op jit(solution)/shard_map/psum | solution.py:64
  673.7 4.8 multiply_convert_fusion.3
  681.1 3.1 reshape.231
  684.1 4.8 reverse_bitcast_fusion.1
  688.9 6.7 copy.175
  695.6 6.4 pad_slice_fusion
  711.1 8.9 convert_reduce_fusion
  721.6 4.3 reduce_sum.181
  727.5 8.2 fusion.35
  735.8 4.8 reverse_bitcast_fusion
  740.7 6.7 copy.185
  755.8 6.9 convolution_add_fusion
  762.7 3.3 fusion.7
  766.1 3.9 copy_add_fusion
  770.0 3.3 reshape.238
  773.9 4.1 multiply_reduce_fusion.7
  778.0 40.3 %all-reduce.10 = (f32[32,174]{1,0:T(8,128)S(1)}, f32[512]{0:T(512)S(1)}, f32[512]{0:T(512)S(1)}) all-reduce(f32[32,174]{1,0:T(8,128)S(1)} %fusion.28, f32[512]{0:T(512)S(1)} %get-tuple-element.73, f32[512]{0:T(512)S(1)} %get-tuple-element.72), channel_id=2, replica_groups=mesh['fsdp'=8,'rep'=4] {'fsdp','rep'}, use_global_device_ids=true, to_apply=%region_17.18.clone | all-reduce | flops 6592 | bytes 52736
  818.3 3.1 multiply_convert_fusion.2
  822.4 6.9 convolution_bitcast_fusion
  830.6 11.3 fusion.40
  882.3 11.5 fusion.39
  894.2 51.0 %reduce-scatter.15.cloned.1.call-done = f32[64,2048]{1,0:T(8,128)} async-done(((f32[512,2048]{1,0:T(8,128)}), f32[64,2048]{1,0:T(8,128)}) %reduce-scatter.15.cloned.1.call-update) | async-done | bytes 524304 | tf_op jit(solution)/shard_map/reduce_scatter | solution.py:281
  945.2 92.3 %reduce-scatter.7.cloned.1.call-done = f32[256,512]{0,1:T(8,128)} async-done(((f32[2048,512]{0,1:T(8,128)}), f32[256,512]{0,1:T(8,128)}) %reduce-scatter.7.cloned.1.call-update) | async-done | bytes 524304 | tf_op jit(solution)/shard_map/reduce_scatter | solution.py:277
  1037.5 167.1 %reduce-scatter.13.cloned.1.call-done = f32[576,512]{1,0:T(8,128)} async-done(((f32[4608,512]{1,0:T(8,128)}), f32[576,512]{1,0:T(8,128)}) %reduce-scatter.13.cloned.1.call-update) | async-done | bytes 1179664 | tf_op jit(solution)/shard_map/reduce_scatter | solution.py:280
  1204.6 166.3 %reduce-scatter.9.cloned.1.call-done = f32[576,512]{1,0:T(8,128)} async-done(((f32[4608,512]{1,0:T(8,128)}), f32[576,512]{1,0:T(8,128)}) %reduce-scatter.9.cloned.1.call-update) | async-done | bytes 1179664 | tf_op jit(solution)/shard_map/reduce_scatter | solution.py:278
  1377.1 10.0 add_convert_fusion
  1387.1 64.8 %all-reduce.19.cloned.1.call-done = (f32[256,512]{0,1:T(8,128)}, f32[576,512]{1,0:T(8,128)}, f32[64,512]{1,0:T(8,128)}, f32[576,512]{1,0:T(8,128)}, f32[64,2048]{1,0:T(8,128)}, /*index=5*/f32[256,174]{0,1:T(8,128)}) async-done(((f32[256,512]{0,1:T(8,128)}, f32[576,512]{1,0:T(8,128)}, f32[64,512]{1,0:T(8,128)}, f32[576,512]{1,0:T(8,128)}, f32[64,2048]{1,0:T(8,128)}, /*index=5*/f32[256,174]{0,1:T(8,128)}), ...) | async-done | bytes 3717136 | tf_op jit(solution)/shard_map/psum | solution.py:284
  (313 shorter events, 129.5 us)
Async XLA Ops:
  7.2 105.8 %copy-start.64 = (bf16[256,174]{0,1:T(8,128)(2,1)S(1)}, bf16[256,174]{0,1:T(8,128)(2,1)}, u32[]{:S(2)}) copy-start(bf16[256,174]{0,1:T(8,128)(2,1)} %param.30) | copy-start | bytes 267268
  7.2 139.3 %all-gather.8.cloned.1.call-start = ((), (), s32[]{:S(2)}) async-start(), calls=%async_computation.6 | async-start | bytes 2359296 | tf_op jit(solution)/shard_map/all_gather | solution.py:117
  7.9 260.0 %all-gather.10.cloned.1.call-start = ((), (), s32[]{:S(2)}) async-start(), calls=%async_computation.7 | async-start | bytes 5308416 | tf_op jit(solution)/shard_map/all_gather | solution.py:120
  8.7 325.6 %all-gather.12.cloned.1.call-start = ((), (), s32[]{:S(2)}) async-start(), calls=%async_computation.8 | async-start | bytes 5308416 | tf_op jit(solution)/shard_map/all_gather | solution.py:122
  9.4 420.4 %all-gather.14.cloned.1.call-start = ((), (), s32[]{:S(2)}) async-start(), calls=%async_computation.9 | async-start | bytes 2359296 | tf_op jit(solution)/shard_map/all_gather | solution.py:125
  10.0 884.2 %reduce-scatter.11.cloned.1.call-start = ((), (), s32[]{:S(2)}) async-start(), calls=%async_computation.12 | async-start | bytes 1179648 | tf_op jit(solution)/shard_map/reduce_scatter | solution.py:279
  146.5 100.1 %copy-start.62 = (f32[3,8,8]{2,1,0:T(8,128)}, f32[3,8,8]{2,1,0:T(8,128)S(1)}, u32[]{:S(2)}) copy-start(f32[3,8,8]{2,1,0:T(8,128)S(1)} %multiply_reduce_fusion.9) | copy-start | bytes 2308
  253.7 3.4 copy-start.3
  253.7 5.0 copy-start.11
  253.7 8.1 copy-start.9
  253.7 9.6 copy-start.13
  253.7 9.6 copy-start.17
  253.7 9.6 copy-start.7
  253.7 11.2 copy-start.5
  253.7 12.7 copy-start.19
  284.7 3.3 copy-start.2
  311.6 4.0 copy-start.60
  328.2 2.6 copy-start.49
  328.2 3.8 copy-start.50
  330.8 2.3 copy-start.42
  477.9 47.3 %copy-start.68 = (f32[1,174]{1,0:T(1,128)S(1)}, f32[1,174]{1,0:T(1,128)}, u32[]{:S(2)}) copy-start(f32[1,174]{1,0:T(1,128)} %param.31) | copy-start | bytes 2092
  477.9 87.6 %copy-start.70 = (s32[3]{0:T(128)S(1)}, s32[3]{0:T(128)}, u32[]{:S(2)}) copy-start(s32[3]{0:T(128)} %param.17) | copy-start | bytes 40
  617.7 9.3 copy-start.65
  617.7 9.3 copy-start.66
  617.7 9.4 copy-start.23
  617.7 9.4 copy-start.69
  627.1 5.3 copy-start.51
  706.9 2.7 slice-start
  708.8 2.3 copy-start.22
  721.6 172.6 %reduce-scatter.17.cloned.1.call-start = ((), (), s32[]{:S(2)}) async-start(), calls=%async_computation.15 | async-start | bytes 1622016 | tf_op jit(solution)/shard_map/reduce_scatter | solution.py:282
  727.5 217.7 %reduce-scatter.15.cloned.1.call-start = ((), (), s32[]{:S(2)}) async-start(), calls=%async_computation.14 | async-start | bytes 4718592 | tf_op jit(solution)/shard_map/reduce_scatter | solution.py:281
  735.8 301.7 %reduce-scatter.7.cloned.1.call-start = ((), (), s32[]{:S(2)}) async-start(), calls=%async_computation.10 | async-start | bytes 4718592 | tf_op jit(solution)/shard_map/reduce_scatter | solution.py:277
  752.7 2.1 slice-start.2
  753.6 2.2 slice-start.3
  755.8 6.9 copy-start.63
  755.8 10.2 copy-start.56
  762.7 3.4 copy-start.55
  773.9 44.4 %copy-start.67 = (f32[512]{0:T(512)S(1)}, f32[512]{0:T(512)}, u32[]{:S(2)}) copy-start(f32[512]{0:T(512)} %get-tuple-element.97) | copy-start | bytes 6148
  829.3 375.3 %reduce-scatter.13.cloned.1.call-start = ((), (), s32[]{:S(2)}) async-start(), calls=%async_computation.13 | async-start | bytes 10616832 | tf_op jit(solution)/shard_map/reduce_scatter | solution.py:280
  841.9 4.3 copy-start.18
  841.9 529.0 %reduce-scatter.9.cloned.1.call-start = ((), (), s32[]{:S(2)}) async-start(), calls=%async_computation.11 | async-start | bytes 10616832 | tf_op jit(solution)/shard_map/reduce_scatter | solution.py:278
  844.7 3.1 copy-start.14
  846.2 3.0 copy-start.12
  847.7 3.1 copy-start.10
  849.2 3.1 copy-start.8
  850.8 3.1 copy-start.6
  852.3 3.0 copy-start.4
  853.8 3.0 copy-start.28
  855.3 3.0 copy-start.29
  868.5 4.0 copy-start.45
  870.0 3.7 copy-start.44
  872.5 2.3 copy-start.43
  873.7 2.4 copy-start.38
  874.8 2.4 copy-start.41
  876.0 2.4 copy-start.40
  877.2 2.4 copy-start.39
  878.4 2.3 copy-start.37
  879.6 2.4 copy-start.1
  893.8 483.3 %copy-start.26 = (bf16[1176,512]{1,0:T(8,128)(2,1)S(1)}, bf16[1176,512]{1,0:T(8,128)(2,1)}, u32[]{:S(2)}) copy-start(bf16[1176,512]{1,0:T(8,128)(2,1)} %copy-done.25) | copy-start | bytes 3612676
  893.8 558.1 %all-reduce.19.cloned.1.call-start = ((), (), s32[]{:S(2)}) async-start(), calls=%async_computation.16 | async-start | bytes 7438336 | tf_op jit(solution)/shard_map/psum | solution.py:284
  1451.9 4.6 copy-start.61
  1451.9 5.2 copy-start.57
  1454.1 4.1 copy-start.58
  1456.5 2.5 copy-start.59
  (22 other events, 32.3 us)
Sparse Core Ops, SparseCore 0:
  10.2 52.4 all-gather.7
  64.8 93.0 all-gather.9
  160.1 80.6 all-gather.11
  242.8 47.5 all-gather.13
  721.7 63.4 reduce-scatter.10
  788.9 65.4 reduce-scatter.16
  858.4 86.7 reduce-scatter.14
  949.4 88.0 reduce-scatter.6
  1041.5 163.0 reduce-scatter.12
  1208.4 162.4 reduce-scatter.8
  1373.9 77.9 all-reduce.18
where the time goes:
time: 1470 us
  waiting for transfers between devices  544 us (37%)
  blocking collectives  529 us (36%)
  local copies, waits for them, and re-layouts  190 us (13%)
  matrix products  121 us (8%)
  other arithmetic  65 us (4%)
  between operations  15.9 us (1%)
    reduce_scatter x1, waiting for transfers between devices, local(): lax.psum_scatter(partial_grads[3], 'fsdp', scatter_dimension=0, tiled=True)  167 us
    reduce_scatter x1, waiting for transfers between devices, local(): lax.psum_scatter(partial_grads[1], 'fsdp', scatter_dimension=0, tiled=True)  166 us
    psum x3, blocking collectives, moments(): lax.psum(jnp.sum(alive_rows * deviation * deviation, axis=0), ('fsdp', 'r...  128 us
    psum x3, blocking collectives, moments(): lax.psum((jnp.sum(alive_rows * values, axis=0), jnp.sum(alive_rows)), ('f...  116 us
    reduce_scatter x1, waiting for transfers between devices, local(): lax.psum_scatter(partial_grads[0], 'fsdp', scatter_dimension=0, tiled=True)  92.3 us
    psum x2, blocking collectives, norm_back(): lax.psum((jnp.sum(alive_rows * grad_out, axis=0), jnp.sum(alive_rows * gr...  78.3 us
    psum x1, waiting for transfers between devices, local(): lax.psum((shard_sums[0], shard_sums[1], shard_sums[2], shard_sums[3], sha...  64.8 us
    unnamed x207, local copies, waits for them, and re-layouts  64.1 us
  transfers between devices with their start and end apart: 11, of which 5 were waited for; matrix products, arithmetic and copies ran while one was open for 18% of the time, Pallas kernels for 0%

commit v1 on v0

v1 whole, which is shorter than its diff:
```python
import jax
import jax.numpy as jnp
from jax import lax
from jax.sharding import PartitionSpec as P

D = 2048
MID = 512
SEGS = 8
SIDE = 7
FRAME_ROWS = 392
EVERY = ("fsdp", "rep")

epsilon = 1e-05
highest = lax.Precision.HIGHEST
f32 = jnp.float32
bf16 = jnp.bfloat16


def patches(field):
    extent = field.shape[1]
    padded = jnp.pad(field, ((0, 0), (1, 1), (1, 1), (0, 0)))
    pieces = [
        padded[:, row_offset : row_offset + extent, column_offset : column_offset + extent, :]
        for row_offset in range(3)
        for column_offset in range(3)
    ]
    joined = jnp.concatenate(pieces, axis=3)
    return joined.reshape(-1, joined.shape[3])


def flipped(kernel):
    outputs = kernel.shape[1]
    taps = kernel.reshape(9, -1, outputs)[::-1]
    return jnp.swapaxes(taps, 1, 2).reshape(-1, taps.shape[1])


def temporal_mix(order):
    length = order.shape[1]
    stations = jnp.arange(length, dtype=jnp.int32)
    places = (order[:, :, None] == stations[None, None, :]).astype(f32)
    current = places[:, :-1, :]
    upcoming = places[:, 1:, :]
    return jnp.sum(
        current[:, :, :, None] * (upcoming[:, :, None, :] - current[:, :, None, :]), axis=1
    )


def silu_slope(values):
    sigma_part = jax.nn.sigmoid(values)
    return sigma_part * (1.0 + values * (1.0 - sigma_part))


def swap(array, bit):
    count = lax.axis_size("fsdp") * lax.axis_size("rep")
    return lax.ppermute(array, EVERY, [(place, place ^ bit) for place in range(count)])


def in_order(bit, mine, other, axis):
    first = jnp.where(bit == 0, mine, other)
    second = jnp.where(bit == 0, other, mine)
    return jnp.stack([first, second], axis=axis)


def half(array, bit, axis):
    return lax.dynamic_index_in_dim(array, bit, axis=axis, keepdims=False)


class Block:
    def __init__(self):
        place = lax.axis_index("fsdp") * 4 + lax.axis_index("rep")
        self.core = place & 1
        self.x = (place >> 1) & 1
        self.y = (place >> 2) & 1
        self.z0 = (place >> 3) & 1
        self.z1 = (place >> 4) & 1
        self.z = place >> 3

    def gather(self, quarter):
        rows, lanes = quarter.shape
        one, two, three = (swap(quarter, bit) for bit in (8, 16, 24))
        low = in_order(self.z0, quarter, one, 0)
        high = in_order(self.z0, two, three, 0)
        depth = in_order(self.z1, low, high, 0).reshape(4, rows, lanes)
        plane = in_order(self.y, depth, swap(depth, 4), 1)
        plane = in_order(self.x, plane, swap(plane, 2), 2)
        plane = in_order(self.core, plane, swap(plane, 1), 3)
        return plane.reshape(32 * rows, lanes)

    def reduce(self, partial):
        lanes = partial.shape[1]
        rows = partial.shape[0] // 32
        total = partial.reshape(4, 2, 2, 2, rows, lanes)

        def fold(total, bit, mask, axis):
            sent = half(total, 1 - bit, axis).astype(bf16)
            return half(total, bit, axis).astype(f32) + swap(sent, mask).astype(f32)

        total = fold(total, self.core, 1, 3)
        total = fold(total, self.x, 2, 2)
        total = fold(total, self.y, 4, 1)
        arrived = [
            swap(half(total, self.z ^ hop, 0).astype(bf16), 8 * hop).astype(f32)
            for hop in (1, 2, 3)
        ]
        total = half(total, self.z, 0) + arrived[0] + arrived[1] + arrived[2]
        total = total.astype(bf16)
        total = in_order(self.x, total, swap(total, 2), 0)
        total = in_order(self.core, total, swap(total, 1), 1)
        return total.reshape(4 * rows, lanes).astype(f32)


def to_rows(array):
    rows, lanes = array.shape
    return jnp.swapaxes(array.reshape(rows, lanes // 512, 512), 0, 1).reshape(-1, 512)


def from_rows(array, shards, rows, lanes):
    array = array.reshape(shards, lanes // 512, rows, 512)
    return jnp.swapaxes(array, 1, 2).reshape(shards * rows, lanes)


def split_rows(array, sizes):
    shards = array.shape[0] // sum(sizes)
    array = array.reshape(shards, sum(sizes), array.shape[1])
    pieces, start = [], 0
    for size in sizes:
        pieces.append(array[:, start : start + size].reshape(shards * size, -1))
        start += size
    return pieces


def gather_block(shards):
    (reduce_weight, diff_weight, pooled_weight, spatial_weight, expand_weight, class_weight) = shards
    block = Block()
    which = lax.axis_index("rep")

    def own(weight):
        rows = weight.shape[0] // 4
        return lax.dynamic_slice_in_dim(weight, which * rows, rows, axis=0)

    w_reduce = block.gather(own(reduce_weight))
    middle = jnp.concatenate([own(diff_weight), own(pooled_weight)])
    w_diff, w_pooled = split_rows(block.gather(middle), (144, 16))
    w_spatial = block.gather(own(spatial_weight))
    classes = class_weight.shape[1]
    wide = jnp.pad(own(class_weight), ((0, 0), (0, 512 - classes)))
    last = jnp.concatenate([to_rows(own(expand_weight)), wide])
    w_expand, w_class = split_rows(block.gather(last), (64, 64))
    w_expand = from_rows(w_expand, 32, 16, D)
    w_class = w_class[:, :classes]
    return (w_reduce, w_diff, w_pooled, w_spatial, w_expand, w_class)


def reduce_block(grads):
    grad_reduce, grad_diff, grad_pooled, grad_spatial, grad_expand, grad_class = grads
    block = Block()

    def join(arrays):
        pieces = [array.reshape(32, -1, 512) for array in arrays]
        return jnp.concatenate(pieces, axis=1).reshape(-1, 512)

    classes = grad_class.shape[1]
    wide = jnp.pad(grad_class, ((0, 0), (0, 512 - classes)))
    narrow = jnp.swapaxes(grad_expand.reshape(32, 16, 4, 512), 1, 2).reshape(-1, 512)
    last = block.reduce(join([narrow, wide])).reshape(4, 128, 512)
    out_expand = jnp.swapaxes(last[:, :64].reshape(4, 4, 16, 512), 1, 2).reshape(64, D)
    out_class = last[:, 64:].reshape(256, 512)[:, :classes]
    out_spatial = block.reduce(grad_spatial)
    middle = block.reduce(join([grad_diff, grad_pooled])).reshape(4, 160, 512)
    out_diff = middle[:, :144].reshape(576, 512)
    out_pooled = middle[:, 144:].reshape(64, 512)
    out_reduce = block.reduce(grad_reduce)
    return (out_reduce, out_diff, out_pooled, out_spatial, out_expand, out_class)


def gather_any(shards):
    return tuple(lax.all_gather(shard, "fsdp", axis=0, tiled=True) for shard in shards)


def reduce_any(grads):
    sums = tuple(
        lax.psum_scatter(grad, "fsdp", scatter_dimension=0, tiled=True) for grad in grads
    )
    return lax.psum(sums, "rep")


def exchange(payload):
    return lax.all_to_all(payload, EVERY, 0, 0, tiled=True)


def share(vector):
    count = lax.axis_size("fsdp") * lax.axis_size("rep")
    return exchange(jnp.broadcast_to(vector[None], (count, vector.shape[0])))


def local_moments(values, alive_rows, own_count):
    mean = jnp.sum(alive_rows * values, axis=0) / jnp.maximum(own_count, 1.0)
    deviation = values - mean
    return mean, jnp.sum(alive_rows * deviation * deviation, axis=0)


def joint_moments(means, squares, every_count, weight_sum):
    center = jnp.sum(every_count * means, axis=0) / weight_sum
    offset = means - center
    spread = jnp.sum(squares + every_count * offset * offset, axis=0) / weight_sum
    return center, lax.rsqrt(spread + epsilon)


def norm_input_grad(grad_out, normed, alive_rows, gain, scale, weight_sum, shift_grad, gain_grad):
    return gain * scale * (grad_out - alive_rows * (shift_grad + normed * gain_grad) / weight_sum)


def local(
    clips_in,
    view_ids,
    seg_order,
    reduce_weight,
    gain1,
    shift1,
    diff_weight,
    pooled_weight,
    spatial_weight,
    gain2,
    shift2,
    expand_weight,
    gain3,
    shift3,
    class_weight,
    video_cotangent,
):
    fsdp_count = lax.axis_size("fsdp")
    rep_count = lax.axis_size("rep")
    devices = fsdp_count * rep_count
    clip_count = clips_in.shape[0]
    planes = clip_count * SEGS
    pixels = SIDE * SIDE
    own_videos, classes = video_cotangent.shape
    videos_all = own_videos * devices
    on_block = (fsdp_count, rep_count) == (8, 4)

    alive_clips = (view_ids < videos_all).astype(f32)
    alive_rows = jnp.repeat(alive_clips, FRAME_ROWS)[:, None]
    own_count = jnp.sum(alive_clips) * FRAME_ROWS
    members = (view_ids[:, None] == jnp.arange(videos_all, dtype=jnp.int32)[None, :]).astype(f32)
    mixing_table = temporal_mix(seg_order)

    weights = (reduce_weight, diff_weight, pooled_weight, spatial_weight, expand_weight, class_weight)
    gather = gather_block if on_block else gather_any
    w_reduce, w_diff, w_pooled, w_spatial, w_expand, w_class = gather(weights)

    flat_in = clips_in.reshape(-1, D)
    first_out = jnp.dot(flat_in, w_reduce, preferred_element_type=f32)
    own_mean, own_square = local_moments(first_out, alive_rows, own_count)
    vectors = (gain1, shift1, gain2, shift2, gain3, shift3)
    lengths = [vector.shape[0] for vector in vectors]
    payload = [own_mean, own_square, view_ids.astype(f32), video_cotangent.reshape(-1)]
    payload += [vector.astype(f32) for vector in vectors]
    got = share(jnp.concatenate(payload))
    cuts = []
    start = 0
    for piece in payload:
        cuts.append(got[:, start : start + piece.shape[0]])
        start += piece.shape[0]
    every_view = cuts[2].reshape(-1)
    every_alive = (cuts[2] < videos_all).astype(f32)
    every_count = jnp.sum(every_alive, axis=1, keepdims=True) * FRAME_ROWS
    weight_sum = jnp.sum(every_count)
    every_cotangent = cuts[3].reshape(videos_all, classes)
    g_one, s_one, g_two, s_two, g_three, s_three = (
        piece.reshape(fsdp_count, rep_count, -1)[:, 0].reshape(-1) for piece in cuts[4:]
    )
    counts = jnp.sum(
        (every_view[:, None] == jnp.arange(videos_all, dtype=f32)[None, :]).astype(f32), axis=0
    )
    center_one, scale_one = joint_moments(cuts[0], cuts[1], every_count, weight_sum)

    normed_one = (first_out - center_one) * scale_one
    pre_one = normed_one * g_one + s_one
    hidden_one = jax.nn.silu(pre_one).reshape(clip_count, SEGS, pixels, MID)
    difference = jnp.einsum("cji,cipn->cjpn", mixing_table, hidden_one, precision=highest).astype(bf16)
    summary = jnp.mean(difference.astype(f32), axis=2).astype(bf16).reshape(planes, MID)
    difference_patches = patches(difference.reshape(planes, SIDE, SIDE, MID))
    local_term = jnp.dot(difference_patches, w_diff, preferred_element_type=f32).reshape(
        planes, pixels, MID
    )
    global_term = jnp.dot(summary, w_pooled, preferred_element_type=f32)
    gating = jax.nn.sigmoid(local_term + global_term[:, None, :]).reshape(
        clip_count, SEGS, pixels, MID
    )
    boosted = (hidden_one * (1.0 + gating)).astype(bf16)
    boosted_patches = patches(boosted.reshape(planes, SIDE, SIDE, MID))
    second_out = jnp.dot(boosted_patches, w_spatial, preferred_element_type=f32)
    got = share(jnp.concatenate(local_moments(second_out, alive_rows, own_count)))
    center_two, scale_two = joint_moments(got[:, :MID], got[:, MID:], every_count, weight_sum)

    normed_two = (second_out - center_two) * scale_two
    pre_two = normed_two * g_two + s_two
    hidden_two = jax.nn.silu(pre_two).astype(bf16)
    third_out = jnp.dot(hidden_two, w_expand, preferred_element_type=f32)
    got = share(jnp.concatenate(local_moments(third_out, alive_rows, own_count)))
    center_three, scale_three = joint_moments(got[:, :D], got[:, D:], every_count, weight_sum)

    normed_three = (third_out - center_three) * scale_three
    summed = normed_three * g_three + s_three + flat_in.astype(f32)
    outcome = jax.nn.silu(summed)
    pooled = jnp.mean(outcome.reshape(clip_count, FRAME_ROWS, D), axis=1).astype(bf16)
    clip_logits = jnp.dot(pooled, w_class, preferred_element_type=f32)
    video_sums = jnp.dot(members.T, clip_logits, precision=highest)

    every_share = every_cotangent / counts[:, None]
    logit_grad = jnp.dot(members, every_share, precision=highest).astype(bf16)
    grad_class = jnp.dot(pooled.T, logit_grad, preferred_element_type=f32)
    pooled_grad = jnp.dot(logit_grad, w_class.T, preferred_element_type=f32)
    summed_grad = (
        pooled_grad[:, None, :] / FRAME_ROWS * silu_slope(summed).reshape(clip_count, FRAME_ROWS, D)
    ).reshape(-1, D)

    def norm_sums(grad_out, normed):
        return jnp.concatenate(
            [
                jnp.sum(alive_rows * grad_out, axis=0),
                jnp.sum(alive_rows * grad_out * normed, axis=0),
            ]
        )

    sums = norm_sums(summed_grad, normed_three)
    got = exchange(
        jnp.concatenate(
            [
                jnp.broadcast_to(sums[None], (devices, sums.shape[0])),
                video_sums.reshape(devices, own_videos * classes),
            ],
            axis=1,
        )
    )
    got = jnp.sum(got, axis=0)
    shift_three_grad, gain_three_grad = got[:D], got[D : 2 * D]
    video_total = got[2 * D :].reshape(own_videos, classes)
    place = lax.axis_index("fsdp") * rep_count + lax.axis_index("rep")
    own_counts = lax.dynamic_slice_in_dim(counts, place * own_videos, own_videos)
    video_logits = video_total / own_counts[:, None]

    third_low = norm_input_grad(
        summed_grad, normed_three, alive_rows, g_three, scale_three, weight_sum, shift_three_grad, gain_three_grad
    ).astype(bf16)
    grad_expand = jnp.dot(hidden_two.T, third_low, preferred_element_type=f32)
    pre_two_grad = jnp.dot(third_low, w_expand.T, preferred_element_type=f32) * silu_slope(pre_two)
    got = jnp.sum(share(norm_sums(pre_two_grad, normed_two)), axis=0)
    shift_two_grad, gain_two_grad = got[:MID], got[MID:]
    second_low = norm_input_grad(
        pre_two_grad, normed_two, alive_rows, g_two, scale_two, weight_sum, shift_two_grad, gain_two_grad
    ).astype(bf16)
    grad_spatial = jnp.dot(boosted_patches.T, second_low, preferred_element_type=f32)
    boosted_grad = jnp.dot(
        patches(second_low.reshape(planes, SIDE, SIDE, MID)),
        flipped(w_spatial),
        preferred_element_type=f32,
    ).reshape(clip_count, SEGS, pixels, MID)
    hidden_one_grad = boosted_grad * (1.0 + gating)
    gate_grad = (
        (boosted_grad * hidden_one * gating * (1.0 - gating))
        .astype(bf16)
        .reshape(planes, pixels, MID)
    )
    grad_diff = jnp.dot(
        difference_patches.T, gate_grad.reshape(-1, MID), preferred_element_type=f32
    )
    gate_sums = jnp.sum(gate_grad.astype(f32), axis=1)
    grad_pooled = jnp.dot(summary.astype(f32).T, gate_sums, precision=highest)
    difference_grad = jnp.dot(
        patches(gate_grad.reshape(planes, SIDE, SIDE, MID)),
        flipped(w_diff),
        preferred_element_type=f32,
    ).reshape(planes, pixels, MID)
    summary_grad = jnp.dot(gate_sums, w_pooled.astype(f32).T, precision=highest)
    difference_grad = (difference_grad + summary_grad[:, None, :] / pixels).reshape(
        clip_count, SEGS, pixels, MID
    )
    hidden_one_grad = hidden_one_grad + jnp.einsum(
        "cji,cjpn->cipn", mixing_table, difference_grad, precision=highest
    )
    pre_one_grad = hidden_one_grad.reshape(-1, MID) * silu_slope(pre_one)
    got = jnp.sum(share(norm_sums(pre_one_grad, normed_one)), axis=0)
    shift_one_grad, gain_one_grad = got[:MID], got[MID:]
    first_low = norm_input_grad(
        pre_one_grad, normed_one, alive_rows, g_one, scale_one, weight_sum, shift_one_grad, gain_one_grad
    ).astype(bf16)
    grad_reduce = jnp.dot(flat_in.T, first_low, preferred_element_type=f32)
    input_grad = jnp.dot(first_low, w_reduce.T, preferred_element_type=f32) + summed_grad
    clips_grad = input_grad.astype(bf16).reshape(clip_count, FRAME_ROWS, D)

    reduce = reduce_block if on_block else reduce_any
    reduced = reduce((grad_reduce, grad_diff, grad_pooled, grad_spatial, grad_expand, grad_class))
    shard_index = lax.axis_index("fsdp")

    def own_piece(vector):
        piece_length = vector.shape[0] // fsdp_count
        return lax.dynamic_slice_in_dim(vector, shard_index * piece_length, piece_length)

    return (
        video_logits,
        clips_grad,
        reduced[0],
        own_piece(gain_one_grad),
        own_piece(shift_one_grad),
        reduced[1],
        reduced[2],
        reduced[3],
        own_piece(gain_two_grad),
        own_piece(shift_two_grad),
        reduced[4],
        own_piece(gain_three_grad),
        own_piece(shift_three_grad),
        reduced[5],
    )


def solution(mesh):
    clips, weight, vector = P(EVERY, None, None), P("fsdp", None), P("fsdp")
    rows = P(EVERY, None)
    placed = (
        clips, P(EVERY), rows,
        weight, vector, vector,
        weight, weight, weight, vector, vector,
        weight, vector, vector,
        weight, rows,
    )
    return jax.shard_map(
        local,
        mesh=mesh,
        in_specs=placed,
        out_specs=(
            rows, clips,
            weight, vector, vector,
            weight, weight, weight, vector, vector,
            weight, vector, vector,
            weight,
        ),
        check_vma=False,
    )
```

time: 1470 us -> 815 us (0.55)
  blocking collectives: 529 us -> 0 us
  waiting for transfers between devices: 544 us -> 175 us
  local copies, waits for them, and re-layouts: 190 us -> 299 us
  starting transfers between devices: 0.98 us -> 99.8 us
  other arithmetic: 65 us -> 121 us
    reduce_scatter x6 -> x0, waiting for transfers between devices: 477 us -> none  [the longest x1 167 us: local(): lax.psum_scatter(partial_grads[3], 'fsdp', scatter_dimension=0, tiled=True)]
    psum x8 -> x0, blocking collectives: 322 us -> none  [the longest x3 128 us: moments(): lax.psum(jnp.sum(alive_rows * deviation * deviation, axis=0), ('fsdp', 'r...]
    ppermute x0 -> x56, waiting for transfers between devices: none -> 163 us  [swap(): lax.ppermute(array, EVERY, [(place, place ^ bit) for place in range(count)])]
    all_gather x5 -> x0, blocking collectives: 143 us -> none  [the longest x1 39.7 us: local(): lax.all_gather(video_share, ('fsdp', 'rep'), axis=0, tiled=True)]
    ppermute x0 -> x56, starting transfers between devices: none -> 71 us  [swap(): lax.ppermute(array, EVERY, [(place, place ^ bit) for place in range(count)])]
    psum x1 -> x0, waiting for transfers between devices: 64.8 us -> none  [local(): lax.psum((shard_sums[0], shard_sums[1], shard_sums[2], shard_sums[3], sha...]
    unnamed x2 -> x0, blocking collectives: 63.5 us -> none
    dot_general x0 -> x4, local copies, waits for them, and re-layouts: none -> 35.6 us  [the longest x1 14.7 us: local(): jnp.dot(difference_patches.T, gate_grad.reshape(-1, MID), preferred_eleme...]
  transfers between devices with their start and end apart: 11 -> 62, of which waited for: 5 -> 28; matrix products, arithmetic and copies ran while one was open for 18% -> 45% of each run, Pallas kernels for 0% -> 0%
where the time goes in v1:
time: 815 us; the launch traced here: 805 us
  local copies, waits for them, and re-layouts  299 us (37%)
  waiting for transfers between devices  175 us (21%)
  other arithmetic  121 us (15%)
  matrix products  107 us (13%)
  starting transfers between devices  99.8 us (12%)
    ppermute x56, waiting for transfers between devices, swap(): lax.ppermute(array, EVERY, [(place, place ^ bit) for place in range(count)])  163 us
    unnamed x258, local copies, waits for them, and re-layouts  76.1 us
    ppermute x56, starting transfers between devices, swap(): lax.ppermute(array, EVERY, [(place, place ^ bit) for place in range(count)])  71 us
    concatenate x23, local copies, waits for them, and re-layouts, patches(): joined = jnp.concatenate(pieces, axis=3)  57.8 us
    slice x20, local copies, waits for them, and re-layouts, patches(): padded[:, row_offset:row_offset + extent, column_offset:column_offset + e...  32 us
    all_to_all x6, starting transfers between devices, exchange(): return lax.all_to_all(payload, EVERY, 0, 0, tiled=True)  28.8 us
    another operation x49, other arithmetic, in_order(): return jnp.stack([first, second], axis=axis)  26 us
    reduce_sum x2, other arithmetic, norm_sums(): jnp.sum(alive_rows * grad_out, axis=0)  18.4 us
  transfers between devices with their start and end apart: 62, of which 28 were waited for; matrix products, arithmetic and copies ran while one was open for 45% of the time, Pallas kernels for 0%

profile of v1, /device:TPU:0, one launch (start us, length us, event | category | flops | bytes accessed | tf_op | source)
XLA Modules:
  0.0 805.3 jit_solution(16594764265209619715)
XLA Ops:
  1.7 4.1 collective-permute-start.19
  28.5 5.1 collective-permute-done.6
  36.9 5.0 collective-permute-done.8
  45.1 5.3 collective-permute-start.12
  55.5 5.3 collective-permute-done.3
  64.1 7.9 collective-permute-done.9
  76.0 7.3 collective-permute-done.21
  86.1 4.2 collective-permute-done.15
  93.3 5.1 collective-permute-done.10
  107.8 3.8 all-to-all-start
  111.6 14.3 %collective-permute-done.22 = bf16[4,2,144,512]{3,2,1,0:T(8,128)(2,1)} collective-permute-done((bf16[4,2,144,512]{3,2,1,0:T(8,128)(2,1)}, bf16[4,2,144,512]{3,2,1,0:T(8,128)(2,1)}, u32[]{:S(2)}, u32[]{:S(2)}) %collective-permute-start.22) | collective-permute-done | bytes 1179680 | tf_op jit(solution)/shard_map/ppermute | solution.py:55
  129.2 17.4 %collective-permute-done.16 = bf16[4,2,160,512]{3,2,0,1:T(8,128)(2,1)} collective-permute-done((bf16[4,2,160,512]{3,2,0,1:T(8,128)(2,1)}, bf16[4,2,160,512]{3,2,0,1:T(8,128)(2,1)}, u32[]{:S(2)}, u32[]{:S(2)}) %collective-permute-start.16) | collective-permute-done | bytes 1310752 | tf_op jit(solution)/shard_map/ppermute | solution.py:55
  159.9 5.1 convert_reduce_fusion.1
  254.2 13.0 %broadcast_add_fusion = (f32[24,49,512]{2,1,0:T(8,128)S(1)}, f32[24,49,512]{2,1,0:T(8,128)}) fusion(f32[24,512]{1,0:T(8,128)S(1)} %fusion.79, bf16[24,49,4608]{2,1,0:T(8,128)(2,1)} %copy_dynamic-update-slice_fusion.16, bf16[4608,512,1]{1,0,2:T(8,128)(2,1)S(1)} %bitcast.475), kind=kOutput, calls=%fused_computation.154 | convolution fusion | flops 5552074752 | bytes 20422656 | tf_op jit(solution)/shard_map/dot_general | solution.py:283
  274.8 3.9 fusion.7
  278.7 4.6 pad_slice_fusion.8
  322.7 8.7 %multiply_reduce_fusion.4 = (f32[512]{0:T(512)S(1)}, f32[1176,512]{1,0:T(8,128)S(1)}) fusion(f32[1176]{0:T(1024)S(1)} %mul.406, bf16[1176,4608]{1,0:T(8,128)(2,1)} %constant_dynamic-update-slice_fusion, bf16[4608,512]{1,0:T(8,128)(2,1)S(1)} %bitcast.474), kind=kOutput, calls=%fused_computation.101 | convolution fusion | flops 5550267904 | bytes 17971808 | tf_op jit(solution)/shard_map/dot_general | solution.py:292
  332.9 5.5 all-to-all-start.1
  338.4 4.0 fusion.100
  348.1 4.6 multiply_reduce_fusion.1
  357.7 5.6 all-to-all-start.2
  368.9 10.0 %all-to-all-done.2 = f32[32,1,4096]{2,1,0:T(1,128)S(1)} async-done(((f32[32,1,4096]{2,1,0:T(1,128)}), f32[32,1,4096]{2,1,0:T(1,128)S(1)}, u32[]{:S(2)}, u32[]{:S(2)}) %all-to-all-start.2) | async-done | bytes 524320 | tf_op jit(solution)/shard_map/all_to_all | solution.py:188
  380.7 14.0 %multiply_reduce_fusion.2 = (f32[2048]{0:T(1024)S(1)}, f32[2048]{0:T(1024)S(1)}, f32[1176,2048]{1,0:T(8,128)}, f32[1176,2048]{1,0:T(8,128)}) fusion(f32[1176]{0:T(1024)S(1)} %mul.406, f32[2048]{0:T(1024)S(1)} %get-tuple-element.98, f32[1176,2048]{1,0:T(8,128)} %copy-done.2, f32[2048]{0:T(1024)S(1)} %broadcast_divide_fusion, bf16[3,392,2048]{2,1,0:T(8,128)(2,1)} %param.16, ...), kind=kLoop, calls=%fused_computation.16 | loop fusion | flops 45756416 | bytes 33796704 | tf_op jit(solution)/shard_map/reduce_sum | solution.py:321
  394.8 4.3 reduce_sum.283
  407.4 14.7 %copy.438 = bf16[4608,1176]{1,0:T(8,128)(2,1)} copy(bf16[4608,1176]{0,1:T(8,128)(2,1)} %bitcast.478) | data formatting | bytes 21676032 | tf_op jit(solution)/shard_map/dot_general | solution.py:365
  423.4 4.8 reverse_bitcast_fusion
  428.2 6.6 copy.412
  434.8 14.6 %copy.443 = bf16[4608,1176]{1,0:T(8,128)(2,1)} copy(bf16[4608,1176]{0,1:T(8,128)(2,1)} %bitcast.479) | data formatting | bytes 21676032 | tf_op jit(solution)/shard_map/dot_general | solution.py:353
  449.5 6.7 copy.422
  456.2 4.8 rev.7
  464.4 8.9 %multiply_convert_fusion = bf16[1176,2048]{1,0:T(8,128)(2,1)S(1)} fusion(f32[1176,2048]{1,0:T(8,128)} %get-tuple-element.99, f32[1176,2048]{1,0:T(8,128)} %copy-done.2, f32[]{:T(128)} %get-tuple-element.231, f32[2048]{0:T(1024)S(1)} %get-tuple-element.224, f32[2048]{0:T(1024)S(1)} %get-tuple-element.223, f32[2048]{0:T(1024)S(1)} %get-tuple-element.97, ...), kind=kLoop, calls=%fused_computation.9 | loop fusion | flops 21676032 | bytes 24130148 | tf_op jit(solution)/shard_map/convert_element_type | solution.py:345
  473.4 5.1 fusion.95
  478.5 5.3 multiply_reduce_fusion.7
  483.8 6.1 reshape.947
  489.9 5.9 copy.445
  496.5 6.4 all-to-all-start.4
  502.9 3.9 fusion.25
  511.2 3.8 multiply_convert_fusion.2
  526.5 4.6 copy-done.65
  531.1 9.6 %convert_reduce_fusion = (f32[3,8,512]{2,1,0:T(8,128)S(1)}, bf16[3,8,49,512]{3,2,1,0:T(8,128)(2,1)S(1)}, f32[3,8,49,512]{3,2,1,0:T(8,128)S(1)}) fusion(f32[3,8,49,512]{3,2,1,0:T(8,128)S(1)} %bitcast.528, f32[3,8,49,512]{3,2,1,0:T(8,128)S(1)} %copy-done.28, bf16[3,8,49,4608]{3,2,1,0:T(8,128)(2,1)} %copy-done.65, bf16[4608,512,1,1]{1,0,3,2:T(8,128)(2,1)S(1)} %bitcast.522), kind=kOutput, calls=%fused_computation.69 | convolution fusion | flops 5553266688 | bytes 24035328 | tf_op jit(solution)/shard_map/dot_general | solution.py:354
  544.9 4.6 copy-done.66
  557.1 9.3 %convolution_add_fusion = f32[24,49,512]{2,1,0:T(8,128)S(1)} fusion(bf16[24,49,4608]{2,1,0:T(8,128)(2,1)} %copy_dynamic-update-slice_fusion, bf16[4608,512,1]{1,0,2:T(8,128)(2,1)S(1)} %bitcast.519, f32[24,512]{1,0:T(8,128)S(1)} %convolution_multiply_fusion.2), kind=kOutput, calls=%fused_computation.127 | convolution fusion | flops 5549666304 | bytes 18014208 | tf_op jit(solution)/shard_map/dot_general | solution.py:370
  569.8 3.7 copy_add_fusion
  577.0 4.3 multiply_reduce_fusion.6
  582.0 4.3 all-to-all-start.5
  586.3 11.7 %fusion.31 = f32[4,2,2,2,144,512]{5,4,3,2,1,0:T(8,128)} fusion(bf16[4,2,2,2,144,1176]{5,4,3,2,1,0:T(8,128)(2,1)} %bitcast.484, bf16[1176,512]{1,0:T(8,128)(2,1)} %copy-done.17), kind=kOutput, calls=%fused_computation.162 | convolution fusion | flops 5549064192 | bytes 21479424 | tf_op jit(solution)/shard_map/dot_general | solution.py:353
  601.7 4.1 fusion.24
  610.1 6.9 convolution_bitcast_fusion
  617.0 5.5 copy.427
  624.6 13.6 %fusion.109 = f32[32,144,512]{2,1,0:T(8,128)} fusion(bf16[32,144,1176]{2,1,0:T(8,128)(2,1)} %bitcast.483, bf16[1176,512,1]{1,0,2:T(8,128)(2,1)S(1)} %copy-done.63), kind=kOutput, calls=%fused_computation.418 | convolution fusion | flops 5549064192 | bytes 21479424 | tf_op jit(solution)/shard_map/dot_general | solution.py:365
  641.9 10.0 %pad_maximum_fusion = f32[32,160,512]{2,1,0:T(8,128)} fusion(f32[32,16,512]{2,1,0:T(8,128)} %fusion.76, f32[32,144,512]{2,1,0:T(8,128)} %fusion.109), kind=kLoop, calls=%fused_computation.1 | loop fusion | flops 2621440 | bytes 20971520 | tf_op jit(solution)/shard_map/concatenate | solution.py:160
  651.9 4.6 fusion.8
  661.4 4.1 collective-permute-done.26
  670.6 3.7 collective-permute-done.28
  676.4 4.6 add_convert_fusion
  682.2 13.4 %collective-permute-done.30 = bf16[64,512]{1,0:T(8,128)(2,1)S(1)} collective-permute-done((bf16[64,512]{1,0:T(8,128)(2,1)S(1)}, bf16[64,512]{1,0:T(8,128)(2,1)S(1)}, u32[]{:S(2)}, u32[]{:S(2)}) %collective-permute-start.30) | collective-permute-done | bytes 65568 | tf_op jit(solution)/shard_map/ppermute | solution.py:55
  695.8 4.1 bitcast_add_fusion.1
  708.5 8.4 %collective-permute-done.50 = bf16[4,128,512]{2,1,0:T(8,128)(2,1)S(1)} collective-permute-done((bf16[4,128,512]{2,1,0:T(8,128)(2,1)S(1)}, bf16[4,128,512]{2,1,0:T(8,128)(2,1)S(1)}, u32[]{:S(2)}, u32[]{:S(2)}) %collective-permute-start.50) | collective-permute-done | bytes 524320 | tf_op jit(solution)/shard_map/ppermute | solution.py:55
  724.1 7.1 collective-permute-done.52
  735.0 24.3 %collective-permute-done.54 = bf16[128,512]{1,0:T(8,128)(2,1)S(1)} collective-permute-done((bf16[128,512]{1,0:T(8,128)(2,1)S(1)}, bf16[128,512]{1,0:T(8,128)(2,1)S(1)}, u32[]{:S(2)}, u32[]{:S(2)}) %collective-permute-start.54) | collective-permute-done | bytes 131104 | tf_op jit(solution)/shard_map/ppermute | solution.py:55
  770.9 7.4 collective-permute-done.34
  784.7 3.6 collective-permute-done.35
  788.3 7.4 collective-permute-done.36
  796.6 4.6 collective-permute-done.38
  (604 shorter events, 346.9 us)
Async XLA Ops:
  1.7 49.8 %collective-permute-start.19 = (bf16[144,512]{1,0:T(8,128)(2,1)S(1)}, bf16[144,512]{1,0:T(8,128)(2,1)S(1)}, u32[]{:S(2)}, u32[]{:S(2)}) collective-permute-start(bf16[144,512]{1,0:T(8,128)(2,1)S(1)} %constant_dynamic-slice_fusion.2), channel_id=1, source_target_pairs={{0,16},{1,17},{2,18},{3,19},{4,20},{5,21},{6,22},{7,23},{8,24},{9,... | collective-permute-start | bytes 442376 | tf_op jit(solution)/shard_map/ppermute | solution.py:55
  5.8 47.3 %collective-permute-start.20 = (bf16[144,512]{1,0:T(8,128)(2,1)S(1)}, bf16[144,512]{1,0:T(8,128)(2,1)S(1)}, u32[]{:S(2)}, u32[]{:S(2)}) collective-permute-start(bf16[144,512]{1,0:T(8,128)(2,1)S(1)} %constant_dynamic-slice_fusion.2), channel_id=1, source_target_pairs={{0,24},{1,25},{2,26},{3,27},{4,28},{5,29},{6,30},{7,31},{8,16},{9,... | collective-permute-start | bytes 442376 | tf_op jit(solution)/shard_map/ppermute | solution.py:55
  7.1 38.0 %collective-permute-start.18 = (bf16[144,512]{1,0:T(8,128)(2,1)S(1)}, bf16[144,512]{1,0:T(8,128)(2,1)S(1)}, u32[]{:S(2)}, u32[]{:S(2)}) collective-permute-start(bf16[144,512]{1,0:T(8,128)(2,1)S(1)} %constant_dynamic-slice_fusion.2), channel_id=1, source_target_pairs={{0,8},{1,9},{2,10},{3,11},{4,12},{5,13},{6,14},{7,15},{8,0},{9,1},... | collective-permute-start | bytes 442376 | tf_op jit(solution)/shard_map/ppermute | solution.py:55
  8.2 14.9 %collective-permute-start.1 = (bf16[64,512]{1,0:T(8,128)(2,1)S(1)}, bf16[64,512]{1,0:T(8,128)(2,1)S(1)}, u32[]{:S(2)}, u32[]{:S(2)}) collective-permute-start(bf16[64,512]{1,0:T(8,128)(2,1)S(1)} %constant_dynamic-slice_fusion.7), channel_id=1, source_target_pairs={{0,16},{1,17},{2,18},{3,19},{4,20},{5,21},{6,22},{7,23},{8,24},{9,... | collective-permute-start | bytes 196616 | tf_op jit(solution)/shard_map/ppermute | solution.py:55
  11.0 7.7 collective-permute-start
  18.7 6.2 collective-permute-start.2
  23.1 13.7 %collective-permute-start.7 = (bf16[128,512]{1,0:T(8,128)(2,1)S(1)}, bf16[128,512]{1,0:T(8,128)(2,1)S(1)}, u32[]{:S(2)}, u32[]{:S(2)}) collective-permute-start(bf16[128,512]{1,0:T(8,128)(2,1)S(1)} %fusion.62), channel_id=1, source_target_pairs={{0,16},{1,17},{2,18},{3,19},{4,20},{5,21},{6,22},{7,23},{8,24},{9,... | collective-permute-start | bytes 393224 | tf_op jit(solution)/shard_map/ppermute | solution.py:55
  24.9 8.7 %collective-permute-start.6 = (bf16[128,512]{1,0:T(8,128)(2,1)S(1)}, bf16[128,512]{1,0:T(8,128)(2,1)S(1)}, u32[]{:S(2)}, u32[]{:S(2)}) collective-permute-start(bf16[128,512]{1,0:T(8,128)(2,1)S(1)} %fusion.62), channel_id=1, source_target_pairs={{0,8},{1,9},{2,10},{3,11},{4,12},{5,13},{6,14},{7,15},{8,0},{9,1},... | collective-permute-start | bytes 393224 | tf_op jit(solution)/shard_map/ppermute | solution.py:55
  33.6 8.2 %collective-permute-start.8 = (bf16[128,512]{1,0:T(8,128)(2,1)S(1)}, bf16[128,512]{1,0:T(8,128)(2,1)S(1)}, u32[]{:S(2)}, u32[]{:S(2)}) collective-permute-start(bf16[128,512]{1,0:T(8,128)(2,1)S(1)} %fusion.62), channel_id=1, source_target_pairs={{0,24},{1,25},{2,26},{3,27},{4,28},{5,29},{6,30},{7,31},{8,16},{9,... | collective-permute-start | bytes 393224 | tf_op jit(solution)/shard_map/ppermute | solution.py:55
  36.8 16.9 %collective-permute-start.13 = (bf16[160,512]{1,0:T(8,128)(2,1)S(1)}, bf16[160,512]{1,0:T(8,128)(2,1)S(1)}, u32[]{:S(2)}, u32[]{:S(2)}) collective-permute-start(bf16[160,512]{1,0:T(8,128)(2,1)S(1)} %pad_maximum_fusion.28), channel_id=1, source_target_pairs={{0,16},{1,17},{2,18},{3,19},{4,20},{5,21},{6,22},{7,23},{8,24},{9,... | collective-permute-start | bytes 491528 | tf_op jit(solution)/shard_map/ppermute | solution.py:55
  41.8 13.5 %collective-permute-start.14 = (bf16[160,512]{1,0:T(8,128)(2,1)S(1)}, bf16[160,512]{1,0:T(8,128)(2,1)S(1)}, u32[]{:S(2)}, u32[]{:S(2)}) collective-permute-start(bf16[160,512]{1,0:T(8,128)(2,1)S(1)} %pad_maximum_fusion.28), channel_id=1, source_target_pairs={{0,24},{1,25},{2,26},{3,27},{4,28},{5,29},{6,30},{7,31},{8,16},{9,... | collective-permute-start | bytes 491528 | tf_op jit(solution)/shard_map/ppermute | solution.py:55
  45.1 10.2 %collective-permute-start.12 = (bf16[160,512]{1,0:T(8,128)(2,1)S(1)}, bf16[160,512]{1,0:T(8,128)(2,1)S(1)}, u32[]{:S(2)}, u32[]{:S(2)}) collective-permute-start(bf16[160,512]{1,0:T(8,128)(2,1)S(1)} %pad_maximum_fusion.28), channel_id=1, source_target_pairs={{0,8},{1,9},{2,10},{3,11},{4,12},{5,13},{6,14},{7,15},{8,0},{9,1},... | collective-permute-start | bytes 491528 | tf_op jit(solution)/shard_map/ppermute | solution.py:55
  51.4 9.3 %collective-permute-start.3 = (bf16[4,64,512]{2,1,0:T(8,128)(2,1)S(1)}, bf16[4,64,512]{2,1,0:T(8,128)(2,1)S(1)}, u32[]{:S(2)}, u32[]{:S(2)}) collective-permute-start(bf16[4,64,512]{2,1,0:T(8,128)(2,1)S(1)} %bitcast.549), channel_id=1, source_target_pairs={{0,4},{1,5},{2,6},{3,7},{4,0},{5,1},{6,2},{7,3},{8,12},{9,13},{10,... | collective-permute-start | bytes 786440 | tf_op jit(solution)/shard_map/ppermute | solution.py:55
  53.0 19.0 %collective-permute-start.9 = (bf16[4,128,512]{2,1,0:T(8,128)(2,1)S(1)}, bf16[4,128,512]{2,1,0:T(8,128)(2,1)S(1)}, u32[]{:S(2)}, u32[]{:S(2)}) collective-permute-start(bf16[4,128,512]{2,1,0:T(8,128)(2,1)S(1)} %bitcast.533), channel_id=1, source_target_pairs={{0,4},{1,5},{2,6},{3,7},{4,0},{5,1},{6,2},{7,3},{8,12},{9,13},{10,... | collective-permute-start | bytes 1572872 | tf_op jit(solution)/shard_map/ppermute | solution.py:55
  53.7 29.6 %collective-permute-start.21 = (bf16[4,144,512]{2,1,0:T(8,128)(2,1)S(1)}, bf16[4,144,512]{2,1,0:T(8,128)(2,1)S(1)}, u32[]{:S(2)}, u32[]{:S(2)}) collective-permute-start(bf16[4,144,512]{2,1,0:T(8,128)(2,1)S(1)} %bitcast.531), channel_id=1, source_target_pairs={{0,4},{1,5},{2,6},{3,7},{4,0},{5,1},{6,2},{7,3},{8,12},{9,13},{10,... | collective-permute-start | bytes 1769480 | tf_op jit(solution)/shard_map/ppermute | solution.py:55
  60.9 14.9 %collective-permute-start.4 = (bf16[4,2,64,512]{3,2,1,0:T(8,128)(2,1)S(1)}, bf16[4,2,64,512]{3,2,1,0:T(8,128)(2,1)S(1)}, u32[]{:S(2)}, u32[]{:S(2)}) collective-permute-start(bf16[4,2,64,512]{3,2,1,0:T(8,128)(2,1)S(1)} %pad_maximum_fusion.16), channel_id=1, source_target_pairs={{0,2},{1,3},{2,0},{3,1},{4,6},{5,7},{6,4},{7,5},{8,10},{9,11},{10,... | collective-permute-start | bytes 1572872 | tf_op jit(solution)/shard_map/ppermute | solution.py:55
  62.5 27.9 %collective-permute-start.15 = (bf16[4,160,512]{2,1,0:T(8,128)(2,1)S(1)}, bf16[4,160,512]{2,1,0:T(8,128)(2,1)S(1)}, u32[]{:S(2)}, u32[]{:S(2)}) collective-permute-start(bf16[4,160,512]{2,1,0:T(8,128)(2,1)S(1)} %bitcast.530), channel_id=1, source_target_pairs={{0,4},{1,5},{2,6},{3,7},{4,0},{5,1},{6,2},{7,3},{8,12},{9,13},{10,... | collective-permute-start | bytes 1966088 | tf_op jit(solution)/shard_map/ppermute | solution.py:55
  72.2 26.2 %collective-permute-start.10 = (bf16[4,2,128,512]{3,2,1,0:T(8,128)(2,1)S(1)}, bf16[4,2,128,512]{3,2,1,0:T(8,128)(2,1)S(1)}, u32[]{:S(2)}, u32[]{:S(2)}) collective-permute-start(bf16[4,2,128,512]{3,2,1,0:T(8,128)(2,1)S(1)} %pad_maximum_fusion.11), channel_id=1, source_target_pairs={{0,2},{1,3},{2,0},{3,1},{4,6},{5,7},{6,4},{7,5},{8,10},{9,11},{10,... | collective-permute-start | bytes 3145736 | tf_op jit(solution)/shard_map/ppermute | solution.py:55
  76.0 24.1 %collective-permute-start.5 = (bf16[4,2,2,64,512]{4,3,2,1,0:T(8,128)(2,1)S(1)}, bf16[4,2,2,64,512]{4,3,2,1,0:T(8,128)(2,1)S(1)}, u32[]{:S(2)}, u32[]{:S(2)}) collective-permute-start(bf16[4,2,2,64,512]{4,3,2,1,0:T(8,128)(2,1)S(1)} %pad_maximum_fusion.10), channel_id=1, source_target_pairs={{0,1},{1,0},{2,3},{3,2},{4,5},{5,4},{6,7},{7,6},{8,9},{9,8},{10,11... | collective-permute-start | bytes 3145736 | tf_op jit(solution)/shard_map/ppermute | solution.py:55
  84.6 41.2 %collective-permute-start.22 = (bf16[4,2,144,512]{3,2,1,0:T(8,128)(2,1)}, bf16[4,2,144,512]{3,2,1,0:T(8,128)(2,1)}, u32[]{:S(2)}, u32[]{:S(2)}) collective-permute-start(bf16[4,2,144,512]{3,2,1,0:T(8,128)(2,1)} %pad_maximum_fusion.9), channel_id=1, source_target_pairs={{0,2},{1,3},{2,0},{3,1},{4,6},{5,7},{6,4},{7,5},{8,10},{9,11},{10,... | collective-permute-start | bytes 3538952 | tf_op jit(solution)/shard_map/ppermute | solution.py:55
  91.8 54.8 %collective-permute-start.16 = (bf16[4,2,160,512]{3,2,0,1:T(8,128)(2,1)}, bf16[4,2,160,512]{3,2,0,1:T(8,128)(2,1)}, u32[]{:S(2)}, u32[]{:S(2)}) collective-permute-start(bf16[4,2,160,512]{3,2,0,1:T(8,128)(2,1)} %pad_maximum_fusion.8), channel_id=1, source_target_pairs={{0,2},{1,3},{2,0},{3,1},{4,6},{5,7},{6,4},{7,5},{8,10},{9,11},{10,... | collective-permute-start | bytes 3932168 | tf_op jit(solution)/shard_map/ppermute | solution.py:55
  100.0 141.3 %collective-permute-start.11 = (bf16[4,2,2,128,512]{4,3,2,1,0:T(8,128)(2,1)}, bf16[4,2,2,128,512]{4,3,2,1,0:T(8,128)(2,1)}, u32[]{:S(2)}, u32[]{:S(2)}) collective-permute-start(bf16[4,2,2,128,512]{4,3,2,1,0:T(8,128)(2,1)} %pad_maximum_fusion.7), channel_id=1, source_target_pairs={{0,1},{1,0},{2,3},{3,2},{4,5},{5,4},{6,7},{7,6},{8,9},{9,8},{10,11... | collective-permute-start | bytes 6291464 | tf_op jit(solution)/shard_map/ppermute | solution.py:55
  105.8 210.1 %copy-start.3 = (f32[512,1176]{0,1:T(8,128)}, f32[512,1176]{0,1:T(8,128)S(1)}, u32[]{:S(2)}) copy-start(f32[512,1176]{0,1:T(8,128)S(1)} %get-tuple-element.234) | copy-start | bytes 7225348
  107.8 42.6 %all-to-all-start = ((f32[32,1,1969]{2,1,0:T(1,128)}), f32[32,1,1969]{2,1,0:T(1,128)}, u32[]{:S(2)}, u32[]{:S(2)}) async-start(f32[32,1,1969]{2,1,0:T(1,128)} %broadcast_in_dim.15), calls=%async_computation | async-start | bytes 524288 | tf_op jit(solution)/shard_map/all_to_all | solution.py:188
  129.1 116.8 %collective-permute-start.23 = (bf16[4,2,2,144,512]{4,3,2,1,0:T(8,128)(2,1)}, bf16[4,2,2,144,512]{4,3,2,1,0:T(8,128)(2,1)}, u32[]{:S(2)}, u32[]{:S(2)}) collective-permute-start(bf16[4,2,2,144,512]{4,3,2,1,0:T(8,128)(2,1)} %pad_maximum_fusion.5), channel_id=1, source_target_pairs={{0,1},{1,0},{2,3},{3,2},{4,5},{5,4},{6,7},{7,6},{8,9},{9,8},{10,11... | collective-permute-start | bytes 7077896 | tf_op jit(solution)/shard_map/ppermute | solution.py:55
  150.4 100.1 %collective-permute-start.17 = (bf16[4,2,2,160,512]{4,3,0,1,2:T(8,128)(2,1)}, bf16[4,2,2,160,512]{4,3,0,1,2:T(8,128)(2,1)}, u32[]{:S(2)}, u32[]{:S(2)}) collective-permute-start(bf16[4,2,2,160,512]{4,3,0,1,2:T(8,128)(2,1)} %pad_maximum_fusion.4), channel_id=1, source_target_pairs={{0,1},{1,0},{2,3},{3,2},{4,5},{5,4},{6,7},{7,6},{8,9},{9,8},{10,11... | collective-permute-start | bytes 7864328 | tf_op jit(solution)/shard_map/ppermute | solution.py:55
  153.0 163.0 %copy-start.69 = (f32[512]{0:T(512)}, f32[512]{0:T(512)S(1)}, u32[]{:S(2)}) copy-start(f32[512]{0:T(512)S(1)} %broadcast_divide_fusion.3) | copy-start | bytes 6148
  332.9 13.7 %all-to-all-start.1 = ((f32[32,1,1024]{2,1,0:T(1,128)}), f32[32,1,1024]{2,1,0:T(1,128)S(1)}, u32[]{:S(2)}, u32[]{:S(2)}) async-start(f32[32,1,1024]{2,1,0:T(1,128)} %broadcast_in_dim.16), calls=%async_computation.1 | async-start | bytes 262144 | tf_op jit(solution)/shard_map/all_to_all | solution.py:188
  357.7 21.2 %all-to-all-start.2 = ((f32[32,1,4096]{2,1,0:T(1,128)}), f32[32,1,4096]{2,1,0:T(1,128)S(1)}, u32[]{:S(2)}, u32[]{:S(2)}) async-start(f32[32,1,4096]{2,1,0:T(1,128)} %broadcast_in_dim.17), calls=%async_computation.2 | async-start | bytes 1048576 | tf_op jit(solution)/shard_map/all_to_all | solution.py:188
  400.8 63.2 %all-to-all-start.3 = ((f32[32,1,4270]{2,1,0:T(1,128)}), f32[32,1,4270]{2,1,0:T(1,128)S(1)}, u32[]{:S(2)}, u32[]{:S(2)}) async-start(f32[32,1,4270]{2,1,0:T(1,128)} %all_to_all.38), calls=%async_computation.3 | async-start | bytes 1114112 | tf_op jit(solution)/shard_map/all_to_all | solution.py:188
  496.5 14.6 %all-to-all-start.4 = ((f32[32,1,1024]{2,1,0:T(1,128)}), f32[32,1,1024]{2,1,0:T(1,128)S(1)}, u32[]{:S(2)}, u32[]{:S(2)}) async-start(f32[32,1,1024]{2,1,0:T(1,128)} %broadcast_in_dim.19), calls=%async_computation.4 | async-start | bytes 262144 | tf_op jit(solution)/shard_map/all_to_all | solution.py:188
  508.0 150.2 %collective-permute-start.48 = (bf16[4,2,2,128,512]{4,3,2,1,0:T(8,128)(2,1)}, bf16[4,2,2,128,512]{4,3,2,1,0:T(8,128)(2,1)}, u32[]{:S(2)}, u32[]{:S(2)}) collective-permute-start(bf16[4,2,2,128,512]{4,3,2,1,0:T(8,128)(2,1)} %fusion.25), channel_id=1, source_target_pairs={{0,1},{1,0},{2,3},{3,2},{4,5},{5,4},{6,7},{7,6},{8,9},{9,8},{10,11... | collective-permute-start | bytes 6291464 | tf_op jit(solution)/shard_map/ppermute | solution.py:55
  582.0 23.9 %all-to-all-start.5 = ((f32[32,1,1024]{2,1,0:T(1,128)}), f32[32,1,1024]{2,1,0:T(1,128)S(1)}, u32[]{:S(2)}, u32[]{:S(2)}) async-start(f32[32,1,1024]{2,1,0:T(1,128)} %broadcast_in_dim.20), calls=%async_computation.5 | async-start | bytes 262144 | tf_op jit(solution)/shard_map/all_to_all | solution.py:188
  605.7 90.0 %collective-permute-start.40 = (bf16[4,2,2,144,512]{4,3,2,1,0:T(8,128)(2,1)}, bf16[4,2,2,144,512]{4,3,2,1,0:T(8,128)(2,1)}, u32[]{:S(2)}, u32[]{:S(2)}) collective-permute-start(bf16[4,2,2,144,512]{4,3,2,1,0:T(8,128)(2,1)} %fusion.24), channel_id=1, source_target_pairs={{0,1},{1,0},{2,3},{3,2},{4,5},{5,4},{6,7},{7,6},{8,9},{9,8},{10,11... | collective-permute-start | bytes 7077896 | tf_op jit(solution)/shard_map/ppermute | solution.py:55
  624.2 15.4 %collective-permute-start.24 = (bf16[4,2,2,64,512]{4,3,2,1,0:T(8,128)(2,1)S(1)}, bf16[4,2,2,64,512]{4,3,2,1,0:T(8,128)(2,1)S(1)}, u32[]{:S(2)}, u32[]{:S(2)}) collective-permute-start(bf16[4,2,2,64,512]{4,3,2,1,0:T(8,128)(2,1)S(1)} %fusion.34), channel_id=1, source_target_pairs={{0,1},{1,0},{2,3},{3,2},{4,5},{5,4},{6,7},{7,6},{8,9},{9,8},{10,11... | collective-permute-start | bytes 3145736 | tf_op jit(solution)/shard_map/ppermute | solution.py:55
  640.1 16.4 %collective-permute-start.25 = (bf16[4,2,64,512]{3,2,1,0:T(8,128)(2,1)S(1)}, bf16[4,2,64,512]{3,2,1,0:T(8,128)(2,1)S(1)}, u32[]{:S(2)}, u32[]{:S(2)}) collective-permute-start(bf16[4,2,64,512]{3,2,1,0:T(8,128)(2,1)S(1)} %fusion.41), channel_id=1, source_target_pairs={{0,2},{1,3},{2,0},{3,1},{4,6},{5,7},{6,4},{7,5},{8,10},{9,11},{10,... | collective-permute-start | bytes 1572872 | tf_op jit(solution)/shard_map/ppermute | solution.py:55
  656.4 47.7 %collective-permute-start.32 = (bf16[4,2,2,160,512]{4,3,0,1,2:T(8,128)(2,1)}, bf16[4,2,2,160,512]{4,3,0,1,2:T(8,128)(2,1)}, u32[]{:S(2)}, u32[]{:S(2)}) collective-permute-start(bf16[4,2,2,160,512]{4,3,0,1,2:T(8,128)(2,1)} %fusion.8), channel_id=1, source_target_pairs={{0,1},{1,0},{2,3},{3,2},{4,5},{5,4},{6,7},{7,6},{8,9},{9,8},{10,11... | collective-permute-start | bytes 7864328 | tf_op jit(solution)/shard_map/ppermute | solution.py:55
  656.7 8.8 %collective-permute-start.26 = (bf16[4,64,512]{2,1,0:T(8,128)(2,1)S(1)}, bf16[4,64,512]{2,1,0:T(8,128)(2,1)S(1)}, u32[]{:S(2)}, u32[]{:S(2)}) collective-permute-start(bf16[4,64,512]{2,1,0:T(8,128)(2,1)S(1)} %fusion.51), channel_id=1, source_target_pairs={{0,4},{1,5},{2,6},{3,7},{4,0},{5,1},{6,2},{7,3},{8,12},{9,13},{10,... | collective-permute-start | bytes 786440 | tf_op jit(solution)/shard_map/ppermute | solution.py:55
  665.6 4.6 collective-permute-start.27
  667.2 7.2 collective-permute-start.28
  669.6 6.2 collective-permute-start.29
  670.2 30.3 %collective-permute-start.49 = (bf16[4,2,128,512]{3,2,1,0:T(8,128)(2,1)S(1)}, bf16[4,2,128,512]{3,2,1,0:T(8,128)(2,1)}, u32[]{:S(2)}, u32[]{:S(2)}) collective-permute-start(bf16[4,2,128,512]{3,2,1,0:T(8,128)(2,1)S(1)} %fusion.35), channel_id=1, source_target_pairs={{0,2},{1,3},{2,0},{3,1},{4,6},{5,7},{6,4},{7,5},{8,10},{9,11},{10,... | collective-permute-start | bytes 3145736 | tf_op jit(solution)/shard_map/ppermute | solution.py:55
  675.8 19.9 %collective-permute-start.30 = (bf16[64,512]{1,0:T(8,128)(2,1)S(1)}, bf16[64,512]{1,0:T(8,128)(2,1)S(1)}, u32[]{:S(2)}, u32[]{:S(2)}) collective-permute-start(bf16[64,512]{1,0:T(8,128)(2,1)S(1)} %fusion.68), channel_id=1, source_target_pairs={{0,2},{1,3},{2,0},{3,1},{4,6},{5,7},{6,4},{7,5},{8,10},{9,11},{10,... | collective-permute-start | bytes 196616 | tf_op jit(solution)/shard_map/ppermute | solution.py:55
  695.7 25.5 %collective-permute-start.31 = (bf16[2,64,512]{2,1,0:T(8,128)(2,1)S(1)}, bf16[2,64,512]{2,1,0:T(8,128)(2,1)S(1)}, u32[]{:S(2)}, u32[]{:S(2)}) collective-permute-start(bf16[2,64,512]{2,1,0:T(8,128)(2,1)S(1)} %pad_maximum_fusion.31), channel_id=1, source_target_pairs={{0,1},{1,0},{2,3},{3,2},{4,5},{5,4},{6,7},{7,6},{8,9},{9,8},{10,11... | collective-permute-start | bytes 393224 | tf_op jit(solution)/shard_map/ppermute | solution.py:55
  700.0 32.1 %collective-permute-start.41 = (bf16[4,2,144,512]{3,2,1,0:T(8,128)(2,1)S(1)}, bf16[4,2,144,512]{3,2,1,0:T(8,128)(2,1)S(1)}, u32[]{:S(2)}, u32[]{:S(2)}) collective-permute-start(bf16[4,2,144,512]{3,2,1,0:T(8,128)(2,1)S(1)} %fusion.33), channel_id=1, source_target_pairs={{0,2},{1,3},{2,0},{3,1},{4,6},{5,7},{6,4},{7,5},{8,10},{9,11},{10,... | collective-permute-start | bytes 3538952 | tf_op jit(solution)/shard_map/ppermute | solution.py:55
  702.6 14.3 %collective-permute-start.50 = (bf16[4,128,512]{2,1,0:T(8,128)(2,1)S(1)}, bf16[4,128,512]{2,1,0:T(8,128)(2,1)S(1)}, u32[]{:S(2)}, u32[]{:S(2)}) collective-permute-start(bf16[4,128,512]{2,1,0:T(8,128)(2,1)S(1)} %fusion.42), channel_id=1, source_target_pairs={{0,4},{1,5},{2,6},{3,7},{4,0},{5,1},{6,2},{7,3},{8,12},{9,13},{10,... | collective-permute-start | bytes 1572872 | tf_op jit(solution)/shard_map/ppermute | solution.py:55
  707.2 52.3 %collective-permute-start.33 = (bf16[4,2,160,512]{3,2,0,1:T(8,128)(2,1)S(1)}, bf16[4,2,160,512]{3,2,0,1:T(8,128)(2,1)S(1)}, u32[]{:S(2)}, u32[]{:S(2)}) collective-permute-start(bf16[4,2,160,512]{3,2,0,1:T(8,128)(2,1)S(1)} %fusion.29), channel_id=1, source_target_pairs={{0,2},{1,3},{2,0},{3,1},{4,6},{5,7},{6,4},{7,5},{8,10},{9,11},{10,... | collective-permute-start | bytes 3932168 | tf_op jit(solution)/shard_map/ppermute | solution.py:55
  717.2 6.9 collective-permute-start.51
  718.1 13.0 %collective-permute-start.52 = (bf16[128,512]{1,0:T(8,128)(2,1)S(1)}, bf16[128,512]{1,0:T(8,128)(2,1)S(1)}, u32[]{:S(2)}, u32[]{:S(2)}) collective-permute-start(bf16[128,512]{1,0:T(8,128)(2,1)S(1)} %get-tuple-element.165), channel_id=1, source_target_pairs={{0,16},{1,17},{2,18},{3,19},{4,20},{5,21},{6,22},{7,23},{8,24},{9,... | collective-permute-start | bytes 393224 | tf_op jit(solution)/shard_map/ppermute | solution.py:55
  721.2 10.0 %collective-permute-start.53 = (bf16[128,512]{1,0:T(8,128)(2,1)S(1)}, bf16[128,512]{1,0:T(8,128)(2,1)S(1)}, u32[]{:S(2)}, u32[]{:S(2)}) collective-permute-start(bf16[128,512]{1,0:T(8,128)(2,1)S(1)} %get-tuple-element.164), channel_id=1, source_target_pairs={{0,24},{1,25},{2,26},{3,27},{4,28},{5,29},{6,30},{7,31},{8,16},{9,... | collective-permute-start | bytes 393224 | tf_op jit(solution)/shard_map/ppermute | solution.py:55
  731.2 28.1 %collective-permute-start.54 = (bf16[128,512]{1,0:T(8,128)(2,1)S(1)}, bf16[128,512]{1,0:T(8,128)(2,1)S(1)}, u32[]{:S(2)}, u32[]{:S(2)}) collective-permute-start(bf16[128,512]{1,0:T(8,128)(2,1)S(1)} %fusion.54), channel_id=1, source_target_pairs={{0,2},{1,3},{2,0},{3,1},{4,6},{5,7},{6,4},{7,5},{8,10},{9,11},{10,... | collective-permute-start | bytes 393224 | tf_op jit(solution)/shard_map/ppermute | solution.py:55
  733.5 31.2 %collective-permute-start.42 = (bf16[4,144,512]{2,1,0:T(8,128)(2,1)}, bf16[4,144,512]{2,1,0:T(8,128)(2,1)}, u32[]{:S(2)}, u32[]{:S(2)}) collective-permute-start(bf16[4,144,512]{2,1,0:T(8,128)(2,1)} %fusion.40), channel_id=1, source_target_pairs={{0,4},{1,5},{2,6},{3,7},{4,0},{5,1},{6,2},{7,3},{8,12},{9,13},{10,... | collective-permute-start | bytes 1769480 | tf_op jit(solution)/shard_map/ppermute | solution.py:55
  759.4 3.0 collective-permute-start.55
  760.9 17.4 %collective-permute-start.34 = (bf16[4,160,512]{2,1,0:T(8,128)(2,1)}, bf16[4,160,512]{2,1,0:T(8,128)(2,1)}, u32[]{:S(2)}, u32[]{:S(2)}) collective-permute-start(bf16[4,160,512]{2,1,0:T(8,128)(2,1)} %fusion.39), channel_id=1, source_target_pairs={{0,4},{1,5},{2,6},{3,7},{4,0},{5,1},{6,2},{7,3},{8,12},{9,13},{10,... | collective-permute-start | bytes 1966088 | tf_op jit(solution)/shard_map/ppermute | solution.py:55
  766.5 17.2 %collective-permute-start.43 = (bf16[144,512]{1,0:T(8,128)(2,1)S(1)}, bf16[144,512]{1,0:T(8,128)(2,1)S(1)}, u32[]{:S(2)}, u32[]{:S(2)}) collective-permute-start(bf16[144,512]{1,0:T(8,128)(2,1)S(1)} %get-tuple-element.156), channel_id=1, source_target_pairs={{0,8},{1,9},{2,10},{3,11},{4,12},{5,13},{6,14},{7,15},{8,0},{9,1},... | collective-permute-start | bytes 442376 | tf_op jit(solution)/shard_map/ppermute | solution.py:55
  767.3 16.8 %collective-permute-start.44 = (bf16[144,512]{1,0:T(8,128)(2,1)S(1)}, bf16[144,512]{1,0:T(8,128)(2,1)S(1)}, u32[]{:S(2)}, u32[]{:S(2)}) collective-permute-start(bf16[144,512]{1,0:T(8,128)(2,1)S(1)} %get-tuple-element.158), channel_id=1, source_target_pairs={{0,16},{1,17},{2,18},{3,19},{4,20},{5,21},{6,22},{7,23},{8,24},{9,... | collective-permute-start | bytes 442376 | tf_op jit(solution)/shard_map/ppermute | solution.py:55
  770.5 13.7 %collective-permute-start.45 = (bf16[144,512]{1,0:T(8,128)(2,1)S(1)}, bf16[144,512]{1,0:T(8,128)(2,1)S(1)}, u32[]{:S(2)}, u32[]{:S(2)}) collective-permute-start(bf16[144,512]{1,0:T(8,128)(2,1)S(1)} %get-tuple-element.157), channel_id=1, source_target_pairs={{0,24},{1,25},{2,26},{3,27},{4,28},{5,29},{6,30},{7,31},{8,16},{9,... | collective-permute-start | bytes 442376 | tf_op jit(solution)/shard_map/ppermute | solution.py:55
  779.7 8.6 %collective-permute-start.35 = (bf16[160,512]{1,0:T(8,128)(2,1)S(1)}, bf16[160,512]{1,0:T(8,128)(2,1)S(1)}, u32[]{:S(2)}, u32[]{:S(2)}) collective-permute-start(bf16[160,512]{1,0:T(8,128)(2,1)S(1)} %get-tuple-element.133), channel_id=1, source_target_pairs={{0,8},{1,9},{2,10},{3,11},{4,12},{5,13},{6,14},{7,15},{8,0},{9,1},... | collective-permute-start | bytes 491528 | tf_op jit(solution)/shard_map/ppermute | solution.py:55
  780.6 15.2 %collective-permute-start.36 = (bf16[160,512]{1,0:T(8,128)(2,1)S(1)}, bf16[160,512]{1,0:T(8,128)(2,1)S(1)}, u32[]{:S(2)}, u32[]{:S(2)}) collective-permute-start(bf16[160,512]{1,0:T(8,128)(2,1)S(1)} %get-tuple-element.135), channel_id=1, source_target_pairs={{0,16},{1,17},{2,18},{3,19},{4,20},{5,21},{6,22},{7,23},{8,24},{9,... | collective-permute-start | bytes 491528 | tf_op jit(solution)/shard_map/ppermute | solution.py:55
  783.7 12.1 %collective-permute-start.37 = (bf16[160,512]{1,0:T(8,128)(2,1)S(1)}, bf16[160,512]{1,0:T(8,128)(2,1)S(1)}, u32[]{:S(2)}, u32[]{:S(2)}) collective-permute-start(bf16[160,512]{1,0:T(8,128)(2,1)S(1)} %get-tuple-element.134), channel_id=1, source_target_pairs={{0,24},{1,25},{2,26},{3,27},{4,28},{5,29},{6,30},{7,31},{8,16},{9,... | collective-permute-start | bytes 491528 | tf_op jit(solution)/shard_map/ppermute | solution.py:55
  784.2 12.3 %collective-permute-start.46 = (bf16[144,512]{1,0:T(8,128)(2,1)S(1)}, bf16[144,512]{1,0:T(8,128)(2,1)S(1)}, u32[]{:S(2)}, u32[]{:S(2)}) collective-permute-start(bf16[144,512]{1,0:T(8,128)(2,1)S(1)} %fusion.48), channel_id=1, source_target_pairs={{0,2},{1,3},{2,0},{3,1},{4,6},{5,7},{6,4},{7,5},{8,10},{9,11},{10,... | collective-permute-start | bytes 442376 | tf_op jit(solution)/shard_map/ppermute | solution.py:55
  795.9 5.4 collective-permute-start.38
  796.6 4.8 collective-permute-start.47
  801.3 1.7 collective-permute-start.39
  (105 other events, 1501.9 us)

commit v2 on v1

v2 whole, which is shorter than its diff:
```python
import jax
import jax.numpy as jnp
from jax import lax
from jax.experimental import pallas as pl
from jax.experimental.pallas import tpu as pltpu
from jax.sharding import PartitionSpec as P

D = 2048
MID = 512
EVERY = ("fsdp", "rep")

epsilon = 1e-05
f32 = jnp.float32
bf16 = jnp.bfloat16

SEGS = 8
SIDE = 7
PIXELS = SIDE * SIDE
FRAME_ROWS = SEGS * PIXELS
WIDE = SIDE + 1
VMEM_LIMIT = 58 * 2**20


class Grid:
    def __init__(self, clips):
        self.clips = clips
        self.planes = clips * SEGS
        self.rows = SIDE * WIDE * self.planes
        self.lead = -(-((WIDE + 1) * self.planes) // 16) * 16
        self.total = self.rows + 2 * self.lead
        self.offsets = [
            (WIDE * dy + dx) * self.planes for dy in (-1, 0, 1) for dx in (-1, 0, 1)
        ]

    @classmethod
    def of(cls, total):
        clips = 1
        while cls(clips).total < total:
            clips += 1
        return cls(clips)

    def tap(self, even, odd, tap, start, count):
        offset = self.offsets[tap]
        if offset % 16 == 0:
            return even[pl.ds(self.lead + start + offset, count), :]
        return odd[pl.ds(self.lead + start + offset - 8, count), :]

    def clear_edges(self, field):
        zeros = jnp.zeros((self.lead, MID), f32)
        field[pl.ds(0, self.lead), :] = zeros
        field[pl.ds(self.lead + self.rows, self.lead), :] = zeros
        field[pl.ds(self.total, 8), :] = zeros[:8]

    def pack(self, field, even, odd):
        step = self.total // 7

        @pl.loop(0, 7)
        def _(i):
            start = pl.multiple_of(i * step, 16)
            even[pl.ds(start, step), :] = field[pl.ds(start, step), :].astype(bf16)
            odd[pl.ds(start, step), :] = field[pl.ds(start + 8, step), :].astype(bf16)


def sigmoid(values):
    return 0.5 * jnp.tanh(0.5 * values) + 0.5


def quarters(ref, rows=slice(None)):
    return jnp.concatenate([ref[block, rows, :] for block in range(4)], axis=1)


def put_quarters(ref, rows, value):
    for block in range(4):
        ref[block, rows, :] = value[:, block * 128 : (block + 1) * 128]


def clip_pixel(clip, pixel):
    return pl.ds(clip * FRAME_ROWS + pixel, SEGS, stride=PIXELS)


def send_out(payload, low, high):
    count, _, lanes = payload.shape
    for row in range(4):
        for at, vector in ((row, low), (row + 4, high)):
            payload[:, at, :] = jnp.broadcast_to(
                vector[:, row * lanes : (row + 1) * lanes], (count, lanes)
            )


def received(got, at):
    return jnp.concatenate([got[:, row, :] for row in range(at, at + 4)], axis=1)


def joint_moments(got, counts):
    count = counts[...]
    population = jnp.sum(count, axis=0, keepdims=True)
    means, squares = received(got, 0), received(got, 4)
    center = jnp.sum(count * means, axis=0, keepdims=True) / population
    offset = means - center
    spread = jnp.sum(squares + count * offset * offset, axis=0, keepdims=True) / population
    return center, lax.rsqrt(spread + epsilon)


def own_moments(alive, means, squares):
    clips = len(means)
    alive_sum = sum(alive[clip] for clip in range(clips))
    mean = sum(alive[clip] * means[clip] for clip in range(clips)) / jnp.maximum(alive_sum, 1.0)
    square = 0.0
    for clip in range(clips):
        offset = means[clip] - mean
        square = square + alive[clip] * (squares[clip] + FRAME_ROWS * offset * offset)
    return mean, square


def clip_moments(values):
    mean = jnp.sum(values, axis=0, keepdims=True) * (1.0 / FRAME_ROWS)
    offset = values - mean
    return mean, jnp.sum(offset * offset, axis=0, keepdims=True)


def joint_sums(got, counts):
    population = jnp.sum(counts[...], axis=0, keepdims=True)
    total = jnp.sum(got[...], axis=0)
    low = jnp.concatenate([total[row : row + 1] for row in range(4)], axis=1)
    high = jnp.concatenate([total[row : row + 1] for row in range(4, 8)], axis=1)
    return low, high, low / population, high / population


def contract_rows(left, right):
    return lax.dot_general(left, right, (((0,), (0,)), ((), ())), preferred_element_type=f32)


def contract_lanes(left, right):
    return lax.dot_general(left, right, (((1,), (1,)), ((), ())), preferred_element_type=f32)


def dot(left, right):
    return jnp.dot(left, right, preferred_element_type=f32)


def first_kernel(alive, clips_in, w_reduce, first, payload, means, squares):
    clip = pl.program_id(0)
    first[0] = dot(clips_in[0], w_reduce[...])
    mean, square = clip_moments(first[0])
    means[clip] = mean
    squares[clip] = square

    @pl.when(clip == pl.num_programs(0) - 1)
    def _():
        count = means.shape[0]
        mean, square = own_moments(
            alive, [means[i] for i in range(count)], [squares[i] for i in range(count)]
        )
        send_out(payload, mean, square)


def gate_kernel(
    got, counts, first, gain, shift, following, later, w_diff, w_pooled,
    norm, hidden, gating, diff_even, diff_odd, boost_even, boost_odd, summary,
    natural, field, weight, sem,
):
    grid = Grid(first.shape[0])
    fetch = pltpu.make_async_copy(w_diff, weight, sem)
    fetch.start()
    center, scale = joint_moments(got, counts)
    norm[0:1] = center
    norm[1:2] = scale
    ratio = scale * gain[...]
    for clip in range(grid.clips):

        @pl.loop(0, SIDE)
        def _(part):
            rows = pl.ds(pl.multiple_of(part * 56, 8), 56)
            pre = (first[clip, rows, :] - center) * ratio + shift[...]
            value = pre * sigmoid(pre)
            put_quarters(natural, pl.ds(pl.multiple_of(clip * FRAME_ROWS + part * 56, 8), 56), value)

    grid.clear_edges(field)
    zeros = jnp.zeros((grid.planes, MID), f32)

    def spread_row(y, totals):
        base = pl.multiple_of(y * (WIDE * grid.planes), 8)
        totals = list(totals)
        for x in range(SIDE):
            for clip in range(grid.clips):
                at = base + x * grid.planes + clip * SEGS
                own = quarters(natural, clip_pixel(clip, y * SIDE + x))
                index = following[pl.ds(clip * SEGS, SEGS), :]
                after = jnp.concatenate(
                    [
                        jnp.take_along_axis(own[:, b * 128 : (b + 1) * 128], index, axis=0)
                        for b in range(4)
                    ],
                    axis=1,
                )
                step = (after - own) * later[pl.ds(clip * SEGS, SEGS), 0:1]
                step = step.astype(bf16).astype(f32)
                hidden[pl.ds(at, SEGS), :] = own
                field[pl.ds(grid.lead + at, SEGS), :] = step
                totals[clip] = totals[clip] + step
        edge = base + SIDE * grid.planes
        hidden[pl.ds(edge, grid.planes), :] = zeros
        field[pl.ds(grid.lead + edge, grid.planes), :] = zeros
        return tuple(totals)

    totals = lax.fori_loop(0, SIDE, spread_row, (zeros[:SEGS],) * grid.clips)
    mean = (jnp.concatenate(totals, axis=0) * (1.0 / PIXELS)).astype(bf16)
    summary[...] = mean.astype(f32)
    pooled_term = dot(mean, w_pooled[...])
    grid.pack(field, diff_even, diff_odd)
    fetch.wait()
    part = grid.rows // 2
    for start in (0, part):
        total = None
        for tap in range(9):
            term = dot(grid.tap(diff_even, diff_odd, tap, start, part), weight[pl.ds(tap * MID, MID), :])
            total = term if total is None else total + term
        gating[pl.ds(start, part), :] = total

    def boost(pixel):
        rows = pl.ds(pl.multiple_of(pixel * grid.planes, 8), grid.planes)
        gate = sigmoid(gating[rows, :] + pooled_term)
        gating[rows, :] = gate
        value = hidden[rows, :] * (1.0 + gate)
        field[pl.ds(pl.multiple_of(grid.lead + pixel * grid.planes, 8), grid.planes), :] = value

    pl.loop(0, SIDE * WIDE)(boost)
    grid.pack(field, boost_even, boost_odd)


def spatial_kernel(
    alive, boost_even, boost_odd, w_spatial, second, payload, natural, field
):
    grid = Grid(second.shape[0])
    part = grid.rows // 2
    for start in (0, part):
        total = None
        for tap in range(9):
            term = dot(grid.tap(boost_even, boost_odd, tap, start, part), w_spatial[pl.ds(tap * MID, MID), :])
            total = term if total is None else total + term
        field[pl.ds(start, part), :] = total
    to_natural(grid, lambda at, clip: field[pl.ds(at, SEGS), :], natural)
    means, squares = [], []
    for clip in range(grid.clips):
        second[clip] = quarters(natural, pl.ds(clip * FRAME_ROWS, FRAME_ROWS))
        mean, square = clip_moments(second[clip])
        means.append(mean)
        squares.append(square)
    mean, square = own_moments(alive, means, squares)
    send_out(payload, mean, square)


def to_natural(grid, tile, natural):
    @pl.loop(0, SIDE)
    def _(y):
        for x in range(SIDE):
            for clip in range(grid.clips):
                at = pl.multiple_of(y * (WIDE * grid.planes), 8) + x * grid.planes + clip * SEGS
                put_quarters(natural, clip_pixel(clip, y * SIDE + x), tile(at, clip))


def expand_kernel(
    alive, got, counts, second, gain, shift, w_expand, norm, hidden, third, payload, means, squares
):
    clip = pl.program_id(0)
    center, scale = joint_moments(got, counts)

    @pl.when(clip == 0)
    def _():
        norm[0:1] = center
        norm[1:2] = scale

    ratio = scale * gain[...]
    pre = (second[0] - center) * ratio + shift[...]
    hidden[0] = (pre * sigmoid(pre)).astype(bf16)
    third[0] = dot(hidden[0], w_expand[...])
    mean, square = clip_moments(third[0])
    means[clip] = mean
    squares[clip] = square

    @pl.when(clip == pl.num_programs(0) - 1)
    def _():
        count = means.shape[0]
        mean, square = own_moments(
            alive, [means[i] for i in range(count)], [squares[i] for i in range(count)]
        )
        send_out(payload, mean, square)


def outcome_kernel(
    alive, got, counts, third, clips_in, gain, shift, logit_grad, w_class, members,
    norm, normed, summed_grad, payload, video_sums, grad_class,
    pooled_grad, sums, pooled, moments,
):
    clip = pl.program_id(0)

    @pl.when(clip == 0)
    def _():
        center, scale = joint_moments(got, counts)
        norm[0:1] = center
        norm[1:2] = scale
        moments[0:1] = center
        moments[1:2] = scale
        pooled_grad[...] = contract_lanes(logit_grad[...], w_class[...]) * (1.0 / FRAME_ROWS)
        sums[...] = jnp.zeros_like(sums)
        pooled[...] = jnp.zeros_like(pooled)

    weight = alive[clip]
    for lane in range(0, D, 512):
        lanes = pl.ds(lane, 512)
        center, scale = moments[0:1, lanes], moments[1:2, lanes]
        g, s = gain[:, lanes], shift[:, lanes]
        slope_grad = pooled_grad[pl.ds(clip, 1), lanes]

        def piece(start, count, carry):
            rows = pl.ds(start, count)
            value = (third[0, rows, lanes] - center) * scale
            total = value * g + s + clips_in[0, rows, lanes].astype(f32)
            sigma = sigmoid(total)
            out = total * sigma
            grad = slope_grad * (sigma + out * (1.0 - sigma))
            normed[0, rows, lanes] = value.astype(bf16)
            summed_grad[0, rows, lanes] = grad.astype(bf16)
            eights = lambda v: jnp.sum(v.reshape(count // 8, 8, 512), axis=0)
            return (
                carry[0] + eights(grad),
                carry[1] + eights(grad * value),
                carry[2] + eights(out),
            )

        zero = jnp.zeros((8, 512), f32)
        carry = lax.fori_loop(
            0, FRAME_ROWS // 16, lambda i, c: piece(pl.multiple_of(i * 16, 16), 16, c), (zero,) * 3
        )
        tail = FRAME_ROWS - FRAME_ROWS % 16
        if tail < FRAME_ROWS:
            carry = piece(tail, FRAME_ROWS - tail, carry)
        low, high, mean = (jnp.sum(v, axis=0, keepdims=True) for v in carry)
        sums[0:1, lanes] = sums[0:1, lanes] + weight * low
        sums[1:2, lanes] = sums[1:2, lanes] + weight * high
        pooled[pl.ds(clip, 1), lanes] = mean * (1.0 / FRAME_ROWS)

    @pl.when(clip == pl.num_programs(0) - 1)
    def _():
        send_out(payload, sums[0:1], sums[1:2])
        rounded = pooled[...].astype(bf16)
        logits = dot(rounded, w_class[...])
        total = 0.0
        for i in range(clips_of(members)):
            total = total + members[:, i : i + 1] * logits[i : i + 1]
        video_sums[...] = total
        grad_class[...] = contract_rows(rounded, logit_grad[...]).astype(grad_class.dtype)


def clips_of(members):
    return members.shape[1]


def third_kernel(
    alive, got, counts, normed, summed_grad, gain, norm_three, hidden, w_expand, second, norm_two, gain_two, shift_two,
    grad_expand, pre_grad, payload, grads, total, sums, low, columns,
):
    clip = pl.program_id(0)

    @pl.when(clip == 0)
    def _():
        total[...] = jnp.zeros_like(total)
        columns[...] = jnp.zeros_like(columns)
        sums[...] = jnp.zeros_like(sums)
        shift_grad, gain_grad, shift_share, gain_share = joint_sums(got, counts)
        grads[0:1] = shift_grad
        grads[1:2] = gain_grad
        columns[1:2] = shift_share
        columns[2:3] = gain_share

    weight = alive[clip]
    ratio = gain[...] * norm_three[1:2]
    for lane in range(0, D, 512):
        lanes = pl.ds(lane, 512)
        shift_share, gain_share = columns[1:2, lanes] * weight, columns[2:3, lanes] * weight
        r = ratio[:, lane : lane + 512]

        def piece(start, count, carry):
            rows = pl.ds(start, count)
            value = summed_grad[0, rows, lanes].astype(f32) - (
                shift_share + normed[0, rows, lanes].astype(f32) * gain_share
            )
            value = (r * value).astype(bf16)
            low[rows, lanes] = value
            return carry + jnp.sum(value.astype(f32).reshape(count // 8, 8, 512), axis=0)

        carry = lax.fori_loop(
            0,
            FRAME_ROWS // 16,
            lambda i, c: piece(pl.multiple_of(i * 16, 16), 16, c),
            jnp.zeros((8, 512), f32),
        )
        tail = FRAME_ROWS - FRAME_ROWS % 16
        if tail < FRAME_ROWS:
            carry = piece(tail, FRAME_ROWS - tail, carry)
        columns[0:1, lanes] = columns[0:1, lanes] + jnp.sum(carry, axis=0, keepdims=True)
    grad_out = low[pl.ds(0, FRAME_ROWS), :]
    total[...] = total[...] + contract_rows(hidden[0], grad_out)
    back = contract_lanes(grad_out, w_expand[...])
    value = (second[0] - norm_two[0:1]) * norm_two[1:2]
    pre = value * gain_two[...] + shift_two[...]
    sigma = sigmoid(pre)
    grad = back * (sigma * (1.0 + pre * (1.0 - sigma)))
    pre_grad[0] = grad
    sums[0:1] = sums[0:1] + weight * jnp.sum(grad, axis=0, keepdims=True)
    sums[1:2] = sums[1:2] + weight * jnp.sum(grad * value, axis=0, keepdims=True)

    @pl.when(clip == pl.num_programs(0) - 1)
    def _():
        send_out(payload, sums[0:1], sums[1:2])
        mean = usual_silu(shift_two[...], gain_two[...])
        offset = outer(mean, columns[0:1])
        grad_expand[...] = (total[...] - offset).astype(grad_expand.dtype)


def usual_silu(shift, gain):
    silu = lambda v: v * sigmoid(v)
    wide = 3.0**0.5 * gain
    return (2.0 / 3.0) * silu(shift) + (silu(shift + wide) + silu(shift - wide)) * (1.0 / 6.0)


def outer(column, row):
    return jnp.swapaxes(jnp.broadcast_to(column, (8, column.shape[1])), 0, 1)[:, 0:1] * row


def to_grid(grid, natural, put):
    @pl.loop(0, SIDE)
    def _(y):
        base = pl.multiple_of(y * (WIDE * grid.planes), 8)
        for x in range(SIDE):
            for clip in range(grid.clips):
                put(base + x * grid.planes + clip * SEGS, clip, quarters(natural, clip_pixel(clip, y * SIDE + x)))
        put(base + SIDE * grid.planes, None, jnp.zeros((grid.planes, MID), f32))


def second_kernel(
    alive, got, counts, pre_grad, second, norm_two, gain_two, gain_one, shift_one, boost_even, boost_odd,
    grads, low_even, low_odd, grad_spatial, natural, field,
):
    grid = Grid(pre_grad.shape[0])
    shift_grad, gain_grad, shift_share, gain_share = joint_sums(got, counts)
    grads[0:1] = shift_grad
    grads[1:2] = gain_grad
    center, scale = norm_two[0:1], norm_two[1:2]
    ratio = gain_two[...] * scale
    columns = jnp.zeros((8, MID), f32)
    for clip in range(grid.clips):
        weight = alive[clip]

        def piece(part, columns):
            rows = pl.ds(pl.multiple_of(part * 56, 8), 56)
            value = (second[clip, rows, :] - center) * scale
            grad = ratio * (pre_grad[clip, rows, :] - weight * (shift_share + value * gain_share))
            grad = grad.astype(bf16).astype(f32)
            put_quarters(natural, pl.ds(pl.multiple_of(clip * FRAME_ROWS + part * 56, 8), 56), grad)
            return columns + jnp.sum(grad.reshape(7, 8, MID), axis=0)

        columns = lax.fori_loop(0, SIDE, piece, columns)
    columns = jnp.sum(columns, axis=0, keepdims=True)
    grid.clear_edges(field)

    def put(at, clip, value):
        field[pl.ds(grid.lead + at, value.shape[0]), :] = value

    to_grid(grid, natural, put)
    grid.pack(field, low_even, low_odd)
    offset = outer(1.5 * usual_silu(shift_one[...], gain_one[...]), columns)
    grad_out = low_even[pl.ds(grid.lead, grid.rows), :]
    for tap in range(9):
        term = contract_rows(grid.tap(boost_even, boost_odd, tap, 0, grid.rows), grad_out)
        grad_spatial[pl.ds(tap * MID, MID), :] = (term - offset).astype(grad_spatial.dtype)


def boost_back_kernel(
    low_even, low_odd, w_spatial, hidden, gating, summary, w_pooled,
    hidden_grad, gate_even, gate_odd, grad_pooled, summary_grad, field,
):
    grid = Grid(hidden.shape[0] // (SIDE * WIDE * SEGS))
    part = grid.rows // 2
    for start in (0, part):
        total = None
        for tap in range(9):
            term = contract_lanes(
                grid.tap(low_even, low_odd, 8 - tap, start, part), w_spatial[pl.ds(tap * MID, MID), :]
            )
            total = term if total is None else total + term
        hidden_grad[pl.ds(start, part), :] = total
    grid.clear_edges(field)

    def piece(pixel, total):
        rows = pl.ds(pl.multiple_of(pixel * grid.planes, 8), grid.planes)
        grad, gate = hidden_grad[rows, :], gating[rows, :]
        hidden_grad[rows, :] = grad * (1.0 + gate)
        gate_grad = (grad * hidden[rows, :] * gate * (1.0 - gate)).astype(bf16).astype(f32)
        field[pl.ds(pl.multiple_of(grid.lead + pixel * grid.planes, 8), grid.planes), :] = gate_grad
        return total + gate_grad

    gate_sums = lax.fori_loop(0, SIDE * WIDE, piece, jnp.zeros((grid.planes, MID), f32))
    grid.pack(field, gate_even, gate_odd)
    high = gate_sums.astype(bf16)
    low = (gate_sums - high.astype(f32)).astype(bf16)
    mean = summary[...].astype(bf16)
    grad_pooled[...] = (contract_rows(mean, high) + contract_rows(mean, low)).astype(grad_pooled.dtype)
    back = contract_lanes(high, w_pooled[...]) + contract_lanes(low, w_pooled[...])
    summary_grad[...] = back * (1.0 / PIXELS)


def diff_kernel(diff_even, diff_odd, gate_even, grad_diff):
    grid = Grid.of(gate_even.shape[0])
    grad_out = gate_even[pl.ds(grid.lead, grid.rows), :]
    for tap in range(9):
        term = contract_rows(grid.tap(diff_even, diff_odd, tap, 0, grid.rows), grad_out)
        grad_diff[pl.ds(tap * MID, MID), :] = term.astype(grad_diff.dtype)


def diff_back_kernel(
    alive, gate_even, gate_odd, w_diff, summary_grad, hidden_grad, first, norm_one, gain, shift, before, earlier, later,
    pre_grad, payload, natural, field,
):
    grid = Grid(first.shape[0])
    part = grid.rows // 2
    for start in (0, part):
        total = None
        for tap in range(9):
            term = contract_lanes(
                grid.tap(gate_even, gate_odd, 8 - tap, start, part), w_diff[pl.ds(tap * MID, MID), :]
            )
            total = term if total is None else total + term
        field[pl.ds(start, part), :] = total

    def tile(at, clip):
        planes = pl.ds(clip * SEGS, SEGS)
        grad = field[pl.ds(at, SEGS), :] + summary_grad[planes, :]
        index = before[planes, :]
        back = jnp.concatenate(
            [
                jnp.take_along_axis(grad[:, b * 128 : (b + 1) * 128], index, axis=0)
                for b in range(4)
            ],
            axis=1,
        )
        own = hidden_grad[pl.ds(at, SEGS), :]
        return own + back * earlier[planes, 0:1] - grad * later[planes, 0:1]

    to_natural(grid, tile, natural)
    center, scale = norm_one[0:1], norm_one[1:2]
    low = jnp.zeros((8, MID), f32)
    high = jnp.zeros((8, MID), f32)
    for clip in range(grid.clips):
        weight = alive[clip]

        def piece(step, carry):
            rows = pl.ds(pl.multiple_of(step * 56, 8), 56)
            value = (first[clip, rows, :] - center) * scale
            pre = value * gain[...] + shift[...]
            sigma = sigmoid(pre)
            grad = quarters(natural, pl.ds(pl.multiple_of(clip * FRAME_ROWS + step * 56, 8), 56))
            grad = grad * (sigma * (1.0 + pre * (1.0 - sigma)))
            pre_grad[clip, rows, :] = grad
            eights = lambda v: jnp.sum(v.reshape(7, 8, MID), axis=0) * weight
            return carry[0] + eights(grad), carry[1] + eights(grad * value)

        low, high = lax.fori_loop(0, SIDE, piece, (low, high))
    send_out(payload, jnp.sum(low, axis=0, keepdims=True), jnp.sum(high, axis=0, keepdims=True))


def reduce_kernel(
    alive, got, counts, pre_grad, first, norm_one, gain, clips_in, grads, low, grad_reduce, total
):
    clip = pl.program_id(0)
    shift_grad, gain_grad, shift_share, gain_share = joint_sums(got, counts)

    @pl.when(clip == 0)
    def _():
        total[...] = jnp.zeros_like(total)
        grads[0:1] = shift_grad
        grads[1:2] = gain_grad

    center, scale = norm_one[0:1], norm_one[1:2]
    value = (first[0] - center) * scale
    grad = pre_grad[0] - alive[clip] * (shift_share + value * gain_share)
    low[0] = (gain[...] * scale * grad).astype(bf16)
    total[...] = total[...] + contract_rows(clips_in[0], low[0])

    @pl.when(clip == pl.num_programs(0) - 1)
    def _():
        grad_reduce[...] = total[...].astype(grad_reduce.dtype)


def input_kernel(low, w_reduce, summed_grad, clips_grad):
    back = contract_lanes(low[0], w_reduce[...])
    clips_grad[0] = (back + summed_grad[0].astype(f32)).astype(bf16)


def swap(array, bit):
    count = lax.axis_size("fsdp") * lax.axis_size("rep")
    return lax.ppermute(array, EVERY, [(place, place ^ bit) for place in range(count)])


def in_order(bit, mine, other, axis):
    first = jnp.where(bit == 0, mine, other)
    second = jnp.where(bit == 0, other, mine)
    return jnp.stack([first, second], axis=axis)


def half(array, bit, axis):
    return lax.dynamic_index_in_dim(array, bit, axis=axis, keepdims=False)


class Block:
    def __init__(self):
        self.which = lax.axis_index("rep")
        place = lax.axis_index("fsdp") * 4 + self.which
        self.core = place & 1
        self.x = (place >> 1) & 1
        self.y = (place >> 2) & 1
        self.z0 = (place >> 3) & 1
        self.z1 = (place >> 4) & 1
        self.z = place >> 3

    def own(self, weight):
        rows = weight.shape[0] // 4
        return lax.dynamic_slice_in_dim(weight, self.which * rows, rows, axis=0)

    def gather(self, quarter):
        rows, lanes = quarter.shape
        one, two, three = (swap(quarter, bit) for bit in (8, 16, 24))
        low = in_order(self.z0, quarter, one, 0)
        high = in_order(self.z0, two, three, 0)
        depth = in_order(self.z1, low, high, 0).reshape(4, rows, lanes)
        plane = in_order(self.y, depth, swap(depth, 4), 1)
        plane = in_order(self.x, plane, swap(plane, 2), 2)
        plane = in_order(self.core, plane, swap(plane, 1), 3)
        return plane.reshape(32, rows, lanes)

    def reduce(self, partial):
        _, rows, lanes = partial.shape
        total = partial.reshape(4, 2, 2, 2, rows, lanes)

        def fold(total, bit, mask, axis):
            there = swap(half(total, 1 - bit, axis), mask)
            return (half(total, bit, axis).astype(f32) + there.astype(f32)).astype(bf16)

        total = fold(total, self.core, 1, 3)
        total = fold(total, self.x, 2, 2)
        total = fold(total, self.y, 4, 1)
        arrived = [swap(half(total, self.z ^ hop, 0), 8 * hop) for hop in (1, 2, 3)]
        total = half(total, self.z, 0).astype(f32)
        for there in arrived:
            total = total + there.astype(f32)
        return total

    def spread(self, total):
        rows, lanes = total.shape
        total = total.astype(bf16)
        total = in_order(self.x, total, swap(total, 2), 0)
        total = in_order(self.core, total, swap(total, 1), 1)
        return total.reshape(4, rows, lanes).astype(f32)


def gather_block(reduce_weight, diff_weight, pooled_weight, spatial_weight, expand_weight, class_weight):
    block = Block()
    w_reduce = block.gather(block.own(reduce_weight)).reshape(-1, MID)
    middle = block.gather(jnp.concatenate([block.own(diff_weight), block.own(pooled_weight)]))
    w_diff = middle[:, :144].reshape(-1, MID)
    w_pooled = middle[:, 144:].reshape(-1, MID)
    w_spatial = block.gather(block.own(spatial_weight)).reshape(-1, MID)
    expand = block.own(expand_weight)
    wide = block.own(pad_classes(class_weight))
    last = block.gather(
        jnp.concatenate(
            [expand[:, 512 * i : 512 * (i + 1)] for i in range(4)]
            + [jnp.concatenate([wide[:32], wide[32:]], axis=1)]
        )
    )
    w_expand = jnp.concatenate([last[:, 16 * i : 16 * (i + 1)] for i in range(4)], axis=2)
    w_class = jnp.concatenate([last[:, 64:, :256], last[:, 64:, 256:]], axis=1)
    return w_reduce, w_diff, w_pooled, w_spatial, w_expand.reshape(-1, D), w_class.reshape(D, 256)


def pad_classes(array):
    return jnp.pad(array, ((0, 0), (0, 256 - array.shape[1])))


def reduce_block(grad_reduce, grad_diff, grad_pooled, grad_spatial, grad_expand, grad_class, video_sums):
    block = Block()
    parts = lambda array: array.reshape(32, -1, array.shape[-1])
    expand = parts(grad_expand)
    wide = parts(grad_class)
    last = jnp.concatenate(
        [expand[:, :, 512 * i : 512 * (i + 1)] for i in range(4)]
        + [
            jnp.concatenate([wide[:, :32], wide[:, 32:]], axis=2),
            jnp.pad(video_sums.astype(bf16)[:, None, :], ((0, 0), (0, 15), (0, 256))),
        ],
        axis=1,
    )
    last = block.reduce(last)
    video_total = last[96:97, :256]
    last = block.spread(last[:96])
    out_expand = jnp.concatenate([last[:, 16 * i : 16 * (i + 1)] for i in range(4)], axis=2)
    out_class = jnp.concatenate([last[:, 64:, :256], last[:, 64:, 256:]], axis=1)
    out_spatial = block.spread(block.reduce(parts(grad_spatial)))
    middle = jnp.concatenate([parts(grad_diff), parts(grad_pooled)], axis=1)
    middle = block.spread(block.reduce(middle))
    out_reduce = block.spread(block.reduce(parts(grad_reduce)))
    flat = lambda array: array.reshape(-1, array.shape[-1])
    return (
        flat(out_reduce), flat(middle[:, :144]), flat(middle[:, 144:]), flat(out_spatial),
        flat(out_expand), flat(out_class), video_total,
    )


def gather_any(*shards):
    gathered = [lax.all_gather(shard, "fsdp", axis=0, tiled=True) for shard in shards]
    gathered[5] = pad_classes(gathered[5])
    return gathered


def reduce_any(*grads):
    sums = tuple(
        lax.psum_scatter(grad.astype(f32), "fsdp", scatter_dimension=0, tiled=True)
        for grad in grads[:6]
    )
    videos = lax.psum_scatter(grads[6], EVERY, scatter_dimension=0, tiled=True)
    return *lax.psum(sums, "rep"), videos


def exchange(payload):
    return lax.all_to_all(payload, EVERY, 0, 0, tiled=True)


SCALARS = pl.BlockSpec(memory_space=pltpu.SMEM)
WHOLE = pl.BlockSpec(memory_space=pltpu.VMEM)
ANY = pl.BlockSpec(memory_space=pl.ANY)


def each_clip(shape):
    return pl.BlockSpec((1, *shape[1:]), lambda clip: (clip, 0, 0))


def shaped(shape, dtype=f32):
    return jax.ShapeDtypeStruct(tuple(shape), dtype)


def call(kernel, name, ins, outs, scratch=(), clips=None):
    return pl.pallas_call(
        kernel,
        out_shape=[shape for shape, _ in outs],
        grid=(clips,) if clips else (),
        in_specs=[spec for _, spec in ins],
        out_specs=[spec for _, spec in outs],
        scratch_shapes=list(scratch),
        compiler_params=pltpu.CompilerParams(vmem_limit_bytes=VMEM_LIMIT),
        name=name,
    )(*[array for array, _ in ins])


def local(
    clips_in,
    view_ids,
    seg_order,
    reduce_weight,
    gain1,
    shift1,
    diff_weight,
    pooled_weight,
    spatial_weight,
    gain2,
    shift2,
    expand_weight,
    gain3,
    shift3,
    class_weight,
    video_cotangent,
):
    fsdp_count = lax.axis_size("fsdp")
    rep_count = lax.axis_size("rep")
    devices = fsdp_count * rep_count
    clips = clips_in.shape[0]
    own_videos, classes = video_cotangent.shape
    videos_all = own_videos * devices
    on_block = (fsdp_count, rep_count) == (8, 4)
    grid = Grid(clips)
    planes = grid.planes

    vectors = (gain1, shift1, gain2, shift2, gain3, shift3)
    early = [view_ids.astype(f32), video_cotangent.reshape(-1)]
    early += [vector.astype(f32) for vector in vectors]
    early = jnp.concatenate(early)
    room = -(-early.shape[0] // 1024) * 1024
    early = jnp.pad(early, (0, room - early.shape[0])).reshape(1, 8, room // 8)
    got = exchange(jnp.broadcast_to(early, (devices, 8, room // 8))).reshape(devices, room)
    every_view = got[:, :clips]
    every_alive = (every_view < videos_all).astype(f32)
    counts = jnp.sum(every_alive, axis=1, keepdims=True) * FRAME_ROWS
    start = clips + own_videos * classes
    every_cotangent = got[:, clips:start].reshape(videos_all, classes)
    params = []
    for vector in vectors:
        params.append(got[::rep_count, start : start + vector.shape[0]].reshape(1, -1))
        start += vector.shape[0]
    g_one, s_one, g_two, s_two, g_three, s_three = params
    video_list = jnp.arange(videos_all, dtype=jnp.int32)
    video_count = jnp.sum(
        (every_view.reshape(1, -1) == video_list.astype(f32)[:, None]).astype(f32), axis=1
    )
    members = (video_list[:, None] == view_ids[None, :]).astype(f32)
    alive = (view_ids < videos_all).astype(f32)
    every_share = every_cotangent / video_count[:, None]
    logit_grad = jnp.sum(members[:, :, None] * every_share[:, None, :], axis=0)
    logit_grad = jnp.pad(logit_grad.astype(bf16), ((0, 8 - clips), (0, 256 - classes)))

    stations = jnp.arange(SEGS, dtype=jnp.int32)
    places = (seg_order[:, :, None] == stations).astype(jnp.int32)
    place = jnp.sum(places * stations[None, :, None], axis=1)
    is_last, is_first = place == SEGS - 1, place == 0
    at = lambda wanted: jnp.sum(
        (jnp.clip(wanted, 0, SEGS - 1)[:, :, None] == stations).astype(jnp.int32)
        * seg_order[:, None, :],
        axis=2,
    )
    lanes = lambda array: jnp.broadcast_to(array.reshape(planes, 1), (planes, 128))
    following = lanes(at(place + 1))
    before = lanes(at(place - 1))
    later = lanes(1.0 - is_last.astype(f32))
    earlier = lanes(1.0 - is_first.astype(f32))

    gather = gather_block if on_block else gather_any
    w_reduce, w_diff, w_pooled, w_spatial, w_expand, w_class = gather(
        reduce_weight, diff_weight, pooled_weight, spatial_weight, expand_weight, class_weight
    )

    tall = (clips, FRAME_ROWS, MID)
    tall_wide = (clips, FRAME_ROWS, D)
    narrow_note = shaped((devices, 8, MID // 4))
    wide_note = shaped((devices, 8, D // 4))
    packed = shaped((grid.total, MID), bf16)
    in_grid = shaped((grid.rows, MID))
    natural = pltpu.VMEM((4, clips * FRAME_ROWS, 128), f32)
    field = pltpu.VMEM((grid.total + 8, MID), f32)
    alive_in = (alive, SCALARS)
    counts_in = (counts, WHOLE)
    whole = lambda *arrays: [(array, WHOLE) for array in arrays]
    per_clip = lambda *arrays: [(array, each_clip(array.shape)) for array in arrays]
    vector_scratch = [pltpu.VMEM((clips, 1, MID), f32)] * 2

    first, note = call(
        first_kernel, "first", [alive_in, *per_clip(clips_in), *whole(w_reduce)],
        [*per_clip(shaped(tall)), *whole(narrow_note)], vector_scratch, clips,
    )
    got = exchange(note)
    norm_one, hidden, gating, diff_even, diff_odd, boost_even, boost_odd, summary = call(
        gate_kernel, "gate",
        [*whole(got, counts, first, g_one, s_one, following, later), (w_diff, ANY), (w_pooled, WHOLE)],
        whole(shaped((2, MID)), in_grid, in_grid, packed, packed, packed, packed, shaped((planes, MID))),
        [natural, field, pltpu.VMEM((9 * MID, MID), bf16), pltpu.SemaphoreType.DMA],
    )
    second, note = call(
        spatial_kernel, "spatial", [alive_in, *whole(boost_even, boost_odd, w_spatial)],
        whole(shaped(tall), narrow_note), [natural, field],
    )
    got = exchange(note)
    norm_two, hidden_two, third, note = call(
        expand_kernel, "expand",
        [alive_in, *whole(got, counts), *per_clip(second), *whole(g_two, s_two, w_expand)],
        [*whole(shaped((2, MID))), *per_clip(shaped(tall, bf16), shaped(tall_wide)), *whole(wide_note)],
        [pltpu.VMEM((clips, 1, D), f32)] * 2, clips,
    )
    got = exchange(note)
    norm_three, normed, summed_grad, note, video_sums, grad_class = call(
        outcome_kernel, "outcome",
        [
            alive_in, *whole(got, counts), *per_clip(third, clips_in),
            *whole(g_three, s_three, logit_grad, w_class, members),
        ],
        [
            *whole(shaped((2, D))), *per_clip(shaped(tall_wide, bf16), shaped(tall_wide, bf16)),
            *whole(wide_note, shaped((videos_all, 256)), shaped((D, 256), bf16)),
        ],
        [pltpu.VMEM((8, D), f32), pltpu.VMEM((2, D), f32), pltpu.VMEM((8, D), f32), pltpu.VMEM((2, D), f32)],
        clips,
    )
    got = exchange(note)
    grad_expand, pre_two_grad, note, grads_three = call(
        third_kernel, "third",
        [
            alive_in, *whole(got, counts), *per_clip(normed, summed_grad), *whole(g_three, norm_three),
            *per_clip(hidden_two), *whole(w_expand), *per_clip(second), *whole(norm_two, g_two, s_two),
        ],
        [*whole(shaped((MID, D), bf16)), *per_clip(shaped(tall)), *whole(narrow_note, shaped((2, D)))],
        [
            pltpu.VMEM((MID, D), f32), pltpu.VMEM((2, MID), f32),
            pltpu.VMEM((FRAME_ROWS, D), bf16), pltpu.VMEM((3, D), f32),
        ],
        clips,
    )
    got = exchange(note)
    grads_two, low_even, low_odd, grad_spatial = call(
        second_kernel, "second",
        [alive_in, *whole(got, counts, pre_two_grad, second, norm_two, g_two, g_one, s_one, boost_even, boost_odd)],
        whole(shaped((2, MID)), packed, packed, shaped((9 * MID, MID), bf16)), [natural, field],
    )
    hidden_grad, gate_even, gate_odd, grad_pooled, summary_grad = call(
        boost_back_kernel, "boost_back",
        whole(low_even, low_odd, w_spatial, hidden, gating, summary, w_pooled),
        whole(in_grid, packed, packed, shaped((MID, MID), bf16), shaped((planes, MID))), [field],
    )
    (grad_diff,) = call(
        diff_kernel, "diff", whole(diff_even, diff_odd, gate_even), whole(shaped((9 * MID, MID), bf16))
    )
    pre_one_grad, note = call(
        diff_back_kernel, "diff_back",
        [
            alive_in,
            *whole(gate_even, gate_odd, w_diff, summary_grad, hidden_grad, first, norm_one, g_one, s_one),
            *whole(before, earlier, later),
        ],
        whole(shaped(tall), narrow_note), [natural, field],
    )
    got = exchange(note)
    grads_one, low, grad_reduce = call(
        reduce_kernel, "reduce",
        [
            alive_in, *whole(got, counts), *per_clip(pre_one_grad, first), *whole(norm_one, g_one),
            *per_clip(clips_in),
        ],
        [*whole(shaped((2, MID))), *per_clip(shaped(tall, bf16)), *whole(shaped((D, MID), bf16))],
        [pltpu.VMEM((D, MID), f32)], clips,
    )
    (clips_grad,) = call(
        input_kernel, "input", [*per_clip(low), *whole(w_reduce), *per_clip(summed_grad)],
        per_clip(shaped(tall_wide, bf16)), (), clips,
    )

    reduce = reduce_block if on_block else reduce_any
    *reduced, video_total = reduce(
        grad_reduce, grad_diff, grad_pooled, grad_spatial, grad_expand, grad_class, video_sums
    )
    place = lax.axis_index("fsdp") * rep_count + lax.axis_index("rep")
    own_counts = lax.dynamic_slice_in_dim(video_count, place * own_videos, own_videos)
    video_logits = video_total[:, :classes] / own_counts[:, None]

    def own_piece(grads, row):
        length = grads.shape[1] // fsdp_count
        return lax.dynamic_slice(grads, (row, lax.axis_index("fsdp") * length), (1, length))[0]

    return (
        video_logits,
        clips_grad,
        reduced[0],
        own_piece(grads_one, 1),
        own_piece(grads_one, 0),
        reduced[1],
        reduced[2],
        reduced[3],
        own_piece(grads_two, 1),
        own_piece(grads_two, 0),
        reduced[4],
        own_piece(grads_three, 1),
        own_piece(grads_three, 0),
        reduced[5][:, :classes],
    )


def solution(mesh):
    clips, weight, vector = P(EVERY, None, None), P("fsdp", None), P("fsdp")
    rows = P(EVERY, None)
    placed = (
        clips, P(EVERY), rows,
        weight, vector, vector,
        weight, weight, weight, vector, vector,
        weight, vector, vector,
        weight, rows,
    )
    return jax.shard_map(
        local,
        mesh=mesh,
        in_specs=placed,
        out_specs=(
            rows, clips,
            weight, vector, vector,
            weight, weight, weight, vector, vector,
            weight, vector, vector,
            weight,
        ),
        check_vma=False,
    )
```

time: 815 us -> 566 us (0.69)
  local copies, waits for them, and re-layouts: 299 us -> 54 us
  Pallas kernels: 0 us -> 158 us
  matrix products: 107 us -> 0 us
  other arithmetic: 121 us -> 47 us
  waiting for transfers between devices: 175 us -> 200 us
    pallas_call x0 -> x12, Pallas kernels: none -> 158 us  [call(): pl.pallas_call(kernel, out_shape=[shape for shape, _ in outs], grid=(clip...]
    dot_general x21 -> x0, matrix products: 107 us -> none  [the longest x1 13.6 us: local(): jnp.dot(difference_patches.T, gate_grad.reshape(-1, MID), preferred_eleme...]
    unnamed x258 -> x69, local copies, waits for them, and re-layouts: 76.1 us -> 14 us
    concatenate x24 -> x2, local copies, waits for them, and re-layouts: 57.9 us -> 4.14 us  [the longest x1 4.1 us: local(): early = jnp.concatenate(early)]
    dot_general x4 -> x0, local copies, waits for them, and re-layouts: 35.6 us -> none  [the longest x1 14.7 us: local(): jnp.dot(difference_patches.T, gate_grad.reshape(-1, MID), preferred_eleme...]
    all_to_all x6 -> x7, waiting for transfers between devices: 11.8 us -> 46.8 us  [exchange(): return lax.all_to_all(payload, EVERY, 0, 0, tiled=True)]
    slice x37 -> x17, local copies, waits for them, and re-layouts: 38.4 us -> 9.01 us  [the longest x1 2.56 us: gather_block(): w_diff = middle[:, :144].reshape(-1, MID)]
    reduce_sum x19 -> x4, other arithmetic: 27.9 us -> 1.96 us  [the longest x1 0.92 us: local(): jnp.sum((jnp.clip(wanted, 0, SEGS - 1)[:, :, None] == stations).astype(jn...]
  transfers between devices with their start and end apart: 62 -> 63, of which waited for: 28 -> 30; matrix products, arithmetic and copies ran while one was open for 45% -> 15% of each run, Pallas kernels for 0% -> 5%
where the time goes in v2:
time: 566 us; the launch traced here: 559 us
  waiting for transfers between devices  200 us (35%)
  Pallas kernels  158 us (28%)
  starting transfers between devices  97.7 us (17%)
  local copies, waits for them, and re-layouts  54 us (10%)
  other arithmetic  47 us (8%)
    pallas_call x12, Pallas kernels, call(): pl.pallas_call(kernel, out_shape=[shape for shape, _ in outs], grid=(clip...  158 us
    ppermute x56, waiting for transfers between devices, swap(): lax.ppermute(array, EVERY, [(place, place ^ bit) for place in range(count)])  153 us
    ppermute x56, starting transfers between devices, swap(): lax.ppermute(array, EVERY, [(place, place ^ bit) for place in range(count)])  69.6 us
    all_to_all x7, waiting for transfers between devices, exchange(): return lax.all_to_all(payload, EVERY, 0, 0, tiled=True)  46.8 us
    all_to_all x7, starting transfers between devices, exchange(): return lax.all_to_all(payload, EVERY, 0, 0, tiled=True)  28.1 us
    another operation x49, other arithmetic, in_order(): return jnp.stack([first, second], axis=axis)  21.9 us
    unnamed x69, local copies, waits for them, and re-layouts  14 us
  transfers between devices with their start and end apart: 63, of which 30 were waited for; matrix products, arithmetic and copies ran while one was open for 15% of the time, Pallas kernels for 5%

profile of v2, /device:TPU:0, one launch (start us, length us, event | category | flops | bytes accessed | tf_op | source)
XLA Modules:
  0.0 558.5 jit_solution(1236286435658286587)
XLA Ops:
  4.6 4.1 collective-permute-start.19
  11.2 2.8 collective-permute-start.1
  15.3 4.1 concatenate.150
  20.1 3.6 all-to-all-start.1
  27.3 3.7 collective-permute-start.2
  33.5 4.1 collective-permute-start.14
  38.5 3.8 collective-permute-start.8
  42.4 5.8 %collective-permute-done.12 = bf16[144,512]{1,0:T(8,128)(2,1)S(1)} collective-permute-done((bf16[144,512]{1,0:T(8,128)(2,1)S(1)}, bf16[144,512]{1,0:T(8,128)(2,1)S(1)}, u32[]{:S(2)}, u32[]{:S(2)}) %collective-permute-start.12) | collective-permute-done | bytes 147488 | tf_op jit(solution)/shard_map/ppermute | solution.py:602
  51.6 6.1 %collective-permute-done.7 = bf16[160,512]{1,0:T(8,128)(2,1)S(1)} collective-permute-done((bf16[160,512]{1,0:T(8,128)(2,1)S(1)}, bf16[160,512]{1,0:T(8,128)(2,1)S(1)}, u32[]{:S(2)}, u32[]{:S(2)}) %collective-permute-start.7) | collective-permute-done | bytes 163872 | tf_op jit(solution)/shard_map/ppermute | solution.py:602
  62.1 4.9 collective-permute-done.21
  68.7 11.0 %collective-permute-done.15 = bf16[4,144,512]{2,1,0:T(8,128)(2,1)S(1)} collective-permute-done((bf16[4,144,512]{2,1,0:T(8,128)(2,1)S(1)}, bf16[4,144,512]{2,1,0:T(8,128)(2,1)S(1)}, u32[]{:S(2)}, u32[]{:S(2)}) %collective-permute-start.15) | collective-permute-done | bytes 589856 | tf_op jit(solution)/shard_map/ppermute | solution.py:602
  81.4 11.0 %collective-permute-done.9 = bf16[4,160,512]{2,1,0:T(8,128)(2,1)S(1)} collective-permute-done((bf16[4,160,512]{2,1,0:T(8,128)(2,1)S(1)}, bf16[4,160,512]{2,1,0:T(8,128)(2,1)S(1)}, u32[]{:S(2)}, u32[]{:S(2)}) %collective-permute-start.9) | collective-permute-done | bytes 655392 | tf_op jit(solution)/shard_map/ppermute | solution.py:602
  97.4 20.2 %collective-permute-done.16 = bf16[4,2,144,512]{3,2,1,0:T(8,128)(2,1)S(1)} collective-permute-done((bf16[4,2,144,512]{3,2,1,0:T(8,128)(2,1)S(1)}, bf16[4,2,144,512]{3,2,1,0:T(8,128)(2,1)S(1)}, u32[]{:S(2)}, u32[]{:S(2)}) %collective-permute-start.16) | collective-permute-done | bytes 1179680 | tf_op jit(solution)/shard_map/ppermute | solution.py:602
  120.0 24.0 %collective-permute-done.10 = bf16[4,2,160,512]{3,2,0,1:T(8,128)(2,1)S(1)} collective-permute-done((bf16[4,2,160,512]{3,2,0,1:T(8,128)(2,1)S(1)}, bf16[4,2,160,512]{3,2,0,1:T(8,128)(2,1)S(1)}, u32[]{:S(2)}, u32[]{:S(2)}) %collective-permute-start.10) | collective-permute-done | bytes 1310752 | tf_op jit(solution)/shard_map/ppermute | solution.py:602
  153.7 7.1 %first.1 = (f32[3,392,512]{2,1,0:T(8,128)}, f32[32,8,128]{2,1,0:T(8,128)}) custom-call(f32[3]{0:T(128)} %compare_convert_fusion.alive, bf16[3,392,2048]{2,1,0:T(8,128)(2,1)} %clips_in.5, bf16[2048,512]{1,0:T(8,128)(2,1)} %bitcast.306), custom_call_target="tpu_custom_call" | custom-call | tf_op jit(solution)/shard_map/first/pallas_call | solution.py:752
  160.8 6.1 %all-to-all-start = ((f32[32,8,128]{2,1,0:T(8,128)}), f32[32,8,128]{2,1,0:T(8,128)S(1)}, u32[]{:S(2)}, u32[]{:S(2)}) async-start(f32[32,8,128]{2,1,0:T(8,128)} %get-tuple-element.54), calls=%async_computation | async-start | bytes 262144 | tf_op jit(solution)/shard_map/all_to_all | solution.py:735
  171.2 2.0 select_bitcast_fusion.3
  173.2 2.6 pad_maximum_fusion.1
  175.8 2.1 select_bitcast_fusion.1
  179.0 2.6 slice.160
  183.7 17.1 %gate.1 = (f32[2,512]{1,0:T(2,128)}, f32[1344,512]{1,0:T(8,128)}, f32[1344,512]{1,0:T(8,128)}, bf16[1792,512]{1,0:T(8,128)(2,1)}, bf16[1792,512]{1,0:T(8,128)(2,...) custom-call(f32[32,8,128]{2,1,0:T(8,128)} %copy-done.19, f32[32,1]{1,0:T(8,128)} %copy.153.counts, ...), custom_call_target="tpu_custom_call" | custom-call | tf_op jit(solution)/shard_map/gate/pallas_call | solution.py:752
  200.8 12.1 %spatial.1 = (f32[3,392,512]{2,1,0:T(8,128)}, f32[32,8,128]{2,1,0:T(8,128)}) custom-call(f32[3]{0:T(128)} %compare_convert_fusion.alive, bf16[1792,512]{1,0:T(8,128)(2,1)} %get-tuple-element.56.boost_even, bf16[1792,512]{1,0:T(8,128)(2,1)} %get-tuple-element.57.boost_odd, bf16[4608,512]{1,0:T(8,128)(2,1)} %bitcast.297), custom_call_target="tpu_custom_call" | custom-call | tf_op jit(solution)/shard_map/spatial/pallas_call | solution.py:752
  212.9 5.9 %all-to-all-start.2 = ((f32[32,8,128]{2,1,0:T(8,128)}), f32[32,8,128]{2,1,0:T(8,128)S(1)}, u32[]{:S(2)}, u32[]{:S(2)}) async-start(f32[32,8,128]{2,1,0:T(8,128)} %get-tuple-element.58), calls=%async_computation.2 | async-start | bytes 262144 | tf_op jit(solution)/shard_map/all_to_all | solution.py:735
  218.9 3.1 pad_maximum_fusion.6
  222.0 5.1 all-to-all-done.2.got
  227.7 8.8 %expand.1 = (f32[2,512]{1,0:T(2,128)}, bf16[3,392,512]{2,1,0:T(8,128)(2,1)}, f32[3,392,2048]{2,1,0:T(8,128)}, f32[32,8,512]{2,1,0:T(8,128)}) custom-call(f32[3]{0:T(128)} %compare_convert_fusion.alive, f32[32,8,128]{2,1,0:T(8,128)} %copy-done.22, f32[32,1]{1,0:T(8,128)} %copy.153.counts, f32[3,392,512]{2,1,0:T(8,128)} %get-tuple-element.59.second, ...), custom_call_target="tpu_custom_call" | custom-call | tf_op jit(solution)/shard_map/expand/pallas_call | solution.py:752
  236.5 3.8 all-to-all-start.3
  244.1 11.8 %all-to-all-done.3.got = f32[32,8,512]{2,1,0:T(8,128)} async-done(((f32[32,8,512]{2,1,0:T(8,128)}), f32[32,8,512]{2,1,0:T(8,128)}, u32[]{:S(2)}, u32[]{:S(2)}) %all-to-all-start.3) | async-done | bytes 524320 | tf_op jit(solution)/shard_map/all_to_all | solution.py:735
  255.8 17.2 %outcome.1 = (f32[2,2048]{1,0:T(2,128)}, bf16[3,392,2048]{2,1,0:T(8,128)(2,1)}, bf16[3,392,2048]{2,1,0:T(8,128)(2,1)}, f32[32,8,512]{2,1,0:T(8,128)}, f32[32,256]{1,0:T(8,128)}, /*index=5*/bf16[2048,256]{1,0:T(8,128)(2,1)}) custom-call(f32[3]{0:T(128)} %compare_convert_fusion.alive, f32[32,8,512]{2,1,0:T(8,128)} %all-to-all-done.3.got, ...), custom_call_target="tpu_custom_call" | custom-call | tf_op jit(solution)/shard_map/outcome/pallas_call | solution.py:752
  273.0 3.0 all-to-all-start.4
  276.2 15.4 %all-to-all-done.4.got = f32[32,8,512]{2,1,0:T(8,128)S(1)} async-done(((f32[32,8,512]{2,1,0:T(8,128)}), f32[32,8,512]{2,1,0:T(8,128)S(1)}, u32[]{:S(2)}, u32[]{:S(2)}) %all-to-all-start.4) | async-done | bytes 524320 | tf_op jit(solution)/shard_map/all_to_all | solution.py:735
  292.3 18.6 %third.1 = (bf16[512,2048]{1,0:T(8,128)(2,1)}, f32[3,392,512]{2,1,0:T(8,128)}, f32[32,8,128]{2,1,0:T(8,128)}, f32[2,2048]{1,0:T(2,128)}) custom-call(f32[3]{0:T(128)} %compare_convert_fusion.alive, f32[32,8,512]{2,1,0:T(8,128)} %copy-done.13, f32[32,1]{1,0:T(8,128)} %copy.153.counts, bf16[3,392,2048]{2,1,0:T(8,128)(2,1)} %get-tuple-element.63.normed, ...), custom_call_target="tpu_custom_call" | custom-call | tf_op jit(solution)/shard_map/third/pallas_call | solution.py:752
  310.9 3.1 all-to-all-start.5
  315.0 7.2 %all-to-all-done.5.got = f32[32,8,128]{2,1,0:T(8,128)S(1)} async-done(((f32[32,8,128]{2,1,0:T(8,128)}), f32[32,8,128]{2,1,0:T(8,128)S(1)}, u32[]{:S(2)}, u32[]{:S(2)}) %all-to-all-start.5) | async-done | bytes 131104 | tf_op jit(solution)/shard_map/all_to_all | solution.py:735
  322.9 15.2 %second.1 = (f32[2,512]{1,0:T(2,128)}, bf16[1792,512]{1,0:T(8,128)(2,1)}, bf16[1792,512]{1,0:T(8,128)(2,1)}, bf16[4608,512]{1,0:T(8,128)(2,1)}) custom-call(f32[3]{0:T(128)} %compare_convert_fusion.alive, f32[32,8,128]{2,1,0:T(8,128)} %copy-done.21, f32[32,1]{1,0:T(8,128)} %copy.153.counts, f32[3,392,512]{2,1,0:T(8,128)} %get-tuple-element.72.pre_grad, ...), custom_call_target="tpu_custom_call" | custom-call | tf_op jit(solution)/shard_map/second/pallas_call | solution.py:752
  338.1 16.4 %boost_back.1 = (f32[1344,512]{1,0:T(8,128)}, bf16[1792,512]{1,0:T(8,128)(2,1)}, bf16[1792,512]{1,0:T(8,128)(2,1)}, bf16[512,512]{1,0:T(8,128)(2,1)}, f32[24,512]{1,0:T(8,128)}) custom-call(bf16[1792,512]{1,0:T(8,128)(2,1)} %get-tuple-element.73.low_even, bf16[1792,512]{1,0:T(8,128)(2,1)} %get-tuple-element.74.low_odd, bf16[4608,512]{1,0:T(8,128)(2,1)} %bitcast.298, ...), custom_call_target="tpu_custom_call" | custom-call | tf_op jit(solution)/shard_map/boost_back/pallas_call | solution.py:752
  355.8 15.6 %diff_back.1 = (f32[3,392,512]{2,1,0:T(8,128)}, f32[32,8,128]{2,1,0:T(8,128)}) custom-call(f32[3]{0:T(128)} %compare_convert_fusion.alive, bf16[1792,512]{1,0:T(8,128)(2,1)} %get-tuple-element.78.gate_even, bf16[1792,512]{1,0:T(8,128)(2,1)} %get-tuple-element.79.gate_odd, bf16[4608,512]{1,0:T(8,128)(2,1)} %bitcast.300, ...), custom_call_target="tpu_custom_call" | custom-call | tf_op jit(solution)/shard_map/diff_back/pallas_call | solution.py:752
  371.4 2.6 all-to-all-start.6
  374.8 7.3 %all-to-all-done.6.got = f32[32,8,128]{2,1,0:T(8,128)S(1)} async-done(((f32[32,8,128]{2,1,0:T(8,128)}), f32[32,8,128]{2,1,0:T(8,128)S(1)}, u32[]{:S(2)}, u32[]{:S(2)}) %all-to-all-start.6) | async-done | bytes 131104 | tf_op jit(solution)/shard_map/all_to_all | solution.py:735
  382.8 9.2 %reduce.1 = (f32[2,512]{1,0:T(2,128)}, bf16[3,392,512]{2,1,0:T(8,128)(2,1)}, bf16[2048,512]{1,0:T(8,128)(2,1)}) custom-call(f32[3]{0:T(128)} %compare_convert_fusion.alive, f32[32,8,128]{2,1,0:T(8,128)} %copy-done.20, f32[32,1]{1,0:T(8,128)} %copy.153.counts, f32[3,392,512]{2,1,0:T(8,128)} %get-tuple-element.84.pre_grad, ...), custom_call_target="tpu_custom_call" | custom-call | tf_op jit(solution)/shard_map/reduce/pallas_call | solution.py:752
  399.8 3.4 dynamic-slice_bitcast_fusion
  403.2 12.3 %diff.1 = bf16[4608,512]{1,0:T(8,128)(2,1)} custom-call(bf16[1792,512]{1,0:T(8,128)(2,1)} %get-tuple-element.88.diff_even, bf16[1792,512]{1,0:T(8,128)(2,1)} %get-tuple-element.89.diff_odd, bf16[1792,512]{1,0:T(8,128)(2,1)} %get-tuple-element.78.gate_even), custom_call_target="tpu_custom_call" | custom-call | tf_op jit(solution)/shard_map/diff/pallas_call | solution.py:752
  416.8 2.7 fusion.4
  421.4 3.0 collective-permute-done.32
  426.3 2.7 collective-permute-start.35
  429.0 2.1 fusion.2
  436.1 2.0 collective-permute-done.36
  439.5 8.2 %input.1 = bf16[3,392,2048]{2,1,0:T(8,128)(2,1)} custom-call(bf16[3,392,512]{2,1,0:T(8,128)(2,1)} %get-tuple-element.85.low, bf16[2048,512]{1,0:T(8,128)(2,1)} %bitcast.307, bf16[3,392,2048]{2,1,0:T(8,128)(2,1)} %get-tuple-element.64.summed_grad), custom_call_target="tpu_custom_call" | custom-call | tf_op jit(solution)/shard_map/input/pallas_call | solution.py:752
  450.0 6.0 %collective-permute-done.25 = bf16[4,2,112,512]{3,2,1,0:T(8,128)(2,1)S(1)} collective-permute-done((bf16[4,2,112,512]{3,2,1,0:T(8,128)(2,1)}, bf16[4,2,112,512]{3,2,1,0:T(8,128)(2,1)S(1)}, u32[]{:S(2)}, u32[]{:S(2)}) %collective-permute-start.25) | collective-permute-done | bytes 917536 | tf_op jit(solution)/shard_map/ppermute | solution.py:602
  456.8 3.1 fusion.1
  460.7 5.1 collective-permute-done.26
  466.0 2.1 collective-permute-start.27
  470.5 2.6 fusion
  473.1 2.1 collective-permute-done.28
  476.6 3.0 collective-permute-start.54
  479.8 11.2 %collective-permute-done.54 = bf16[96,512]{1,0:T(8,128)(2,1)S(1)} collective-permute-done((bf16[96,512]{1,0:T(8,128)(2,1)S(1)}, bf16[96,512]{1,0:T(8,128)(2,1)S(1)}, u32[]{:S(2)}, u32[]{:S(2)}) %collective-permute-start.54) | collective-permute-done | bytes 98336 | tf_op jit(solution)/shard_map/ppermute | solution.py:602
  496.5 18.3 %collective-permute-done.39 = bf16[4,2,160,512]{3,2,0,1:T(8,128)(2,1)S(1)} collective-permute-done((bf16[4,2,160,512]{3,2,0,1:T(8,128)(2,1)S(1)}, bf16[4,2,160,512]{3,2,0,1:T(8,128)(2,1)S(1)}, u32[]{:S(2)}, u32[]{:S(2)}) %collective-permute-start.39) | collective-permute-done | bytes 1310752 | tf_op jit(solution)/shard_map/ppermute | solution.py:602
  521.7 2.7 collective-permute-start.49
  529.0 4.2 collective-permute-start.41
  533.4 2.3 collective-permute-start.43
  535.7 2.4 collective-permute-done.50
  538.1 2.0 collective-permute-start.52
  540.1 8.8 %collective-permute-done.42 = bf16[160,512]{1,0:T(8,128)(2,1)S(1)} collective-permute-done((bf16[160,512]{1,0:T(8,128)(2,1)S(1)}, bf16[160,512]{1,0:T(8,128)(2,1)S(1)}, u32[]{:S(2)}, u32[]{:S(2)}) %collective-permute-start.42) | collective-permute-done | bytes 163872 | tf_op jit(solution)/shard_map/ppermute | solution.py:602
  551.0 3.4 collective-permute-done.44
  (303 shorter events, 110.9 us)
Async XLA Ops:
  0.6 25.7 %copy-start = (bf16[576,512]{1,0:T(8,128)(2,1)S(1)}, bf16[576,512]{1,0:T(8,128)(2,1)}, u32[]{:S(2)}) copy-start(bf16[576,512]{1,0:T(8,128)(2,1)} %param.22) | copy-start | bytes 1769476
  4.6 33.2 %collective-permute-start.19 = (bf16[96,512]{1,0:T(8,128)(2,1)S(1)}, bf16[96,512]{1,0:T(8,128)(2,1)S(1)}, u32[]{:S(2)}, u32[]{:S(2)}) collective-permute-start(bf16[96,512]{1,0:T(8,128)(2,1)S(1)} %maximum_dynamic-update-slice_fusion.1), channel_id=1, source_target_pairs={{0,16},{1,17},{2,18},{3,19},{4,20},{5,21},{6,22},{7,23},{8,24},{9,... | collective-permute-start | bytes 294920 | tf_op jit(solution)/shard_map/ppermute | solution.py:602
  8.7 29.7 %collective-permute-start.20 = (bf16[96,512]{1,0:T(8,128)(2,1)S(1)}, bf16[96,512]{1,0:T(8,128)(2,1)S(1)}, u32[]{:S(2)}, u32[]{:S(2)}) collective-permute-start(bf16[96,512]{1,0:T(8,128)(2,1)S(1)} %maximum_dynamic-update-slice_fusion.1), channel_id=1, source_target_pairs={{0,24},{1,25},{2,26},{3,27},{4,28},{5,29},{6,30},{7,31},{8,16},{9,... | collective-permute-start | bytes 294920 | tf_op jit(solution)/shard_map/ppermute | solution.py:602
  10.1 27.7 %collective-permute-start.18 = (bf16[96,512]{1,0:T(8,128)(2,1)S(1)}, bf16[96,512]{1,0:T(8,128)(2,1)S(1)}, u32[]{:S(2)}, u32[]{:S(2)}) collective-permute-start(bf16[96,512]{1,0:T(8,128)(2,1)S(1)} %maximum_dynamic-update-slice_fusion.1), channel_id=1, source_target_pairs={{0,8},{1,9},{2,10},{3,11},{4,12},{5,13},{6,14},{7,15},{8,0},{9,1},... | collective-permute-start | bytes 294920 | tf_op jit(solution)/shard_map/ppermute | solution.py:602
  11.2 20.7 %collective-permute-start.1 = (bf16[64,512]{1,0:T(8,128)(2,1)S(1)}, bf16[64,512]{1,0:T(8,128)(2,1)S(1)}, u32[]{:S(2)}, u32[]{:S(2)}) collective-permute-start(bf16[64,512]{1,0:T(8,128)(2,1)S(1)} %constant_dynamic-slice_fusion.6), channel_id=1, source_target_pairs={{0,16},{1,17},{2,18},{3,19},{4,20},{5,21},{6,22},{7,23},{8,24},{9,... | collective-permute-start | bytes 196616 | tf_op jit(solution)/shard_map/ppermute | solution.py:602
  14.0 13.3 %collective-permute-start = (bf16[64,512]{1,0:T(8,128)(2,1)S(1)}, bf16[64,512]{1,0:T(8,128)(2,1)S(1)}, u32[]{:S(2)}, u32[]{:S(2)}) collective-permute-start(bf16[64,512]{1,0:T(8,128)(2,1)S(1)} %constant_dynamic-slice_fusion.6), channel_id=1, source_target_pairs={{0,8},{1,9},{2,10},{3,11},{4,12},{5,13},{6,14},{7,15},{8,0},{9,1},... | collective-permute-start | bytes 196616 | tf_op jit(solution)/shard_map/ppermute | solution.py:602
  20.1 126.9 %all-to-all-start.1 = ((f32[32,8,128]{2,1,0:T(8,128)}), f32[32,8,128]{2,1,0:T(8,128)S(1)}, u32[]{:S(2)}, u32[]{:S(2)}) async-start(f32[32,8,128]{2,1,0:T(8,128)} %broadcast_in_dim.19), calls=%async_computation.1 | async-start | bytes 262144 | tf_op jit(solution)/shard_map/all_to_all | solution.py:735
  27.3 6.2 %collective-permute-start.2 = (bf16[64,512]{1,0:T(8,128)(2,1)S(1)}, bf16[64,512]{1,0:T(8,128)(2,1)S(1)}, u32[]{:S(2)}, u32[]{:S(2)}) collective-permute-start(bf16[64,512]{1,0:T(8,128)(2,1)S(1)} %constant_dynamic-slice_fusion.6), channel_id=1, source_target_pairs={{0,24},{1,25},{2,26},{3,27},{4,28},{5,29},{6,30},{7,31},{8,16},{9,... | collective-permute-start | bytes 196616 | tf_op jit(solution)/shard_map/ppermute | solution.py:602
  31.9 17.5 %collective-permute-start.13 = (bf16[144,512]{1,0:T(8,128)(2,1)S(1)}, bf16[144,512]{1,0:T(8,128)(2,1)S(1)}, u32[]{:S(2)}, u32[]{:S(2)}) collective-permute-start(bf16[144,512]{1,0:T(8,128)(2,1)S(1)} %constant_dynamic-slice_fusion.3), channel_id=1, source_target_pairs={{0,16},{1,17},{2,18},{3,19},{4,20},{5,21},{6,22},{7,23},{8,24},{9,... | collective-permute-start | bytes 442376 | tf_op jit(solution)/shard_map/ppermute | solution.py:602
  33.5 17.3 %collective-permute-start.14 = (bf16[144,512]{1,0:T(8,128)(2,1)S(1)}, bf16[144,512]{1,0:T(8,128)(2,1)S(1)}, u32[]{:S(2)}, u32[]{:S(2)}) collective-permute-start(bf16[144,512]{1,0:T(8,128)(2,1)S(1)} %constant_dynamic-slice_fusion.3), channel_id=1, source_target_pairs={{0,24},{1,25},{2,26},{3,27},{4,28},{5,29},{6,30},{7,31},{8,16},{9,... | collective-permute-start | bytes 442376 | tf_op jit(solution)/shard_map/ppermute | solution.py:602
  37.7 10.4 %collective-permute-start.12 = (bf16[144,512]{1,0:T(8,128)(2,1)S(1)}, bf16[144,512]{1,0:T(8,128)(2,1)S(1)}, u32[]{:S(2)}, u32[]{:S(2)}) collective-permute-start(bf16[144,512]{1,0:T(8,128)(2,1)S(1)} %constant_dynamic-slice_fusion.3), channel_id=1, source_target_pairs={{0,8},{1,9},{2,10},{3,11},{4,12},{5,13},{6,14},{7,15},{8,0},{9,1},... | collective-permute-start | bytes 442376 | tf_op jit(solution)/shard_map/ppermute | solution.py:602
  37.9 19.9 %collective-permute-start.7 = (bf16[160,512]{1,0:T(8,128)(2,1)S(1)}, bf16[160,512]{1,0:T(8,128)(2,1)S(1)}, u32[]{:S(2)}, u32[]{:S(2)}) collective-permute-start(bf16[160,512]{1,0:T(8,128)(2,1)S(1)} %pad_maximum_fusion.30), channel_id=1, source_target_pairs={{0,16},{1,17},{2,18},{3,19},{4,20},{5,21},{6,22},{7,23},{8,24},{9,... | collective-permute-start | bytes 491528 | tf_op jit(solution)/shard_map/ppermute | solution.py:602
  38.5 20.7 %collective-permute-start.8 = (bf16[160,512]{1,0:T(8,128)(2,1)S(1)}, bf16[160,512]{1,0:T(8,128)(2,1)S(1)}, u32[]{:S(2)}, u32[]{:S(2)}) collective-permute-start(bf16[160,512]{1,0:T(8,128)(2,1)S(1)} %pad_maximum_fusion.30), channel_id=1, source_target_pairs={{0,24},{1,25},{2,26},{3,27},{4,28},{5,29},{6,30},{7,31},{8,16},{9,... | collective-permute-start | bytes 491528 | tf_op jit(solution)/shard_map/ppermute | solution.py:602
  48.2 11.0 %collective-permute-start.6 = (bf16[160,512]{1,0:T(8,128)(2,1)S(1)}, bf16[160,512]{1,0:T(8,128)(2,1)S(1)}, u32[]{:S(2)}, u32[]{:S(2)}) collective-permute-start(bf16[160,512]{1,0:T(8,128)(2,1)S(1)} %pad_maximum_fusion.30), channel_id=1, source_target_pairs={{0,8},{1,9},{2,10},{3,11},{4,12},{5,13},{6,14},{7,15},{8,0},{9,1},... | collective-permute-start | bytes 491528 | tf_op jit(solution)/shard_map/ppermute | solution.py:602
  49.4 11.0 %collective-permute-start.3 = (bf16[4,64,512]{2,1,0:T(8,128)(2,1)S(1)}, bf16[4,64,512]{2,1,0:T(8,128)(2,1)S(1)}, u32[]{:S(2)}, u32[]{:S(2)}) collective-permute-start(bf16[4,64,512]{2,1,0:T(8,128)(2,1)S(1)} %bitcast.332), channel_id=1, source_target_pairs={{0,4},{1,5},{2,6},{3,7},{4,0},{5,1},{6,2},{7,3},{8,12},{9,13},{10,... | collective-permute-start | bytes 786440 | tf_op jit(solution)/shard_map/ppermute | solution.py:602
  50.9 16.2 %collective-permute-start.21 = (bf16[4,96,512]{2,1,0:T(8,128)(2,1)S(1)}, bf16[4,96,512]{2,1,0:T(8,128)(2,1)S(1)}, u32[]{:S(2)}, u32[]{:S(2)}) collective-permute-start(bf16[4,96,512]{2,1,0:T(8,128)(2,1)S(1)} %bitcast.327), channel_id=1, source_target_pairs={{0,4},{1,5},{2,6},{3,7},{4,0},{5,1},{6,2},{7,3},{8,12},{9,13},{10,... | collective-permute-start | bytes 1179656 | tf_op jit(solution)/shard_map/ppermute | solution.py:602
  57.7 22.0 %collective-permute-start.15 = (bf16[4,144,512]{2,1,0:T(8,128)(2,1)S(1)}, bf16[4,144,512]{2,1,0:T(8,128)(2,1)S(1)}, u32[]{:S(2)}, u32[]{:S(2)}) collective-permute-start(bf16[4,144,512]{2,1,0:T(8,128)(2,1)S(1)} %bitcast.320), channel_id=1, source_target_pairs={{0,4},{1,5},{2,6},{3,7},{4,0},{5,1},{6,2},{7,3},{8,12},{9,13},{10,... | collective-permute-start | bytes 1769480 | tf_op jit(solution)/shard_map/ppermute | solution.py:602
  59.5 33.0 %collective-permute-start.9 = (bf16[4,160,512]{2,1,0:T(8,128)(2,1)S(1)}, bf16[4,160,512]{2,1,0:T(8,128)(2,1)S(1)}, u32[]{:S(2)}, u32[]{:S(2)}) collective-permute-start(bf16[4,160,512]{2,1,0:T(8,128)(2,1)S(1)} %bitcast.319), channel_id=1, source_target_pairs={{0,4},{1,5},{2,6},{3,7},{4,0},{5,1},{6,2},{7,3},{8,12},{9,13},{10,... | collective-permute-start | bytes 1966088 | tf_op jit(solution)/shard_map/ppermute | solution.py:602
  60.6 33.7 %collective-permute-start.4 = (bf16[4,2,64,512]{3,2,1,0:T(8,128)(2,1)S(1)}, bf16[4,2,64,512]{3,2,1,0:T(8,128)(2,1)S(1)}, u32[]{:S(2)}, u32[]{:S(2)}) collective-permute-start(bf16[4,2,64,512]{3,2,1,0:T(8,128)(2,1)S(1)} %pad_maximum_fusion.16), channel_id=1, source_target_pairs={{0,2},{1,3},{2,0},{3,1},{4,6},{5,7},{6,4},{7,5},{8,10},{9,11},{10,... | collective-permute-start | bytes 1572872 | tf_op jit(solution)/shard_map/ppermute | solution.py:602
  67.2 28.2 %collective-permute-start.22 = (bf16[4,2,96,512]{3,2,1,0:T(8,128)(2,1)S(1)}, bf16[4,2,96,512]{3,2,1,0:T(8,128)(2,1)S(1)}, u32[]{:S(2)}, u32[]{:S(2)}) collective-permute-start(bf16[4,2,96,512]{3,2,1,0:T(8,128)(2,1)S(1)} %pad_maximum_fusion.12), channel_id=1, source_target_pairs={{0,2},{1,3},{2,0},{3,1},{4,6},{5,7},{6,4},{7,5},{8,10},{9,11},{10,... | collective-permute-start | bytes 2359304 | tf_op jit(solution)/shard_map/ppermute | solution.py:602
  79.9 37.7 %collective-permute-start.16 = (bf16[4,2,144,512]{3,2,1,0:T(8,128)(2,1)S(1)}, bf16[4,2,144,512]{3,2,1,0:T(8,128)(2,1)S(1)}, u32[]{:S(2)}, u32[]{:S(2)}) collective-permute-start(bf16[4,2,144,512]{3,2,1,0:T(8,128)(2,1)S(1)} %pad_maximum_fusion.9), channel_id=1, source_target_pairs={{0,2},{1,3},{2,0},{3,1},{4,6},{5,7},{6,4},{7,5},{8,10},{9,11},{10,... | collective-permute-start | bytes 3538952 | tf_op jit(solution)/shard_map/ppermute | solution.py:602
  92.7 51.2 %collective-permute-start.10 = (bf16[4,2,160,512]{3,2,0,1:T(8,128)(2,1)S(1)}, bf16[4,2,160,512]{3,2,0,1:T(8,128)(2,1)S(1)}, u32[]{:S(2)}, u32[]{:S(2)}) collective-permute-start(bf16[4,2,160,512]{3,2,0,1:T(8,128)(2,1)S(1)} %pad_maximum_fusion.8), channel_id=1, source_target_pairs={{0,2},{1,3},{2,0},{3,1},{4,6},{5,7},{6,4},{7,5},{8,10},{9,11},{10,... | collective-permute-start | bytes 3932168 | tf_op jit(solution)/shard_map/ppermute | solution.py:602
  95.5 55.3 %collective-permute-start.5 = (bf16[4,2,2,64,512]{4,3,2,1,0:T(8,128)(2,1)}, bf16[4,2,2,64,512]{4,3,2,1,0:T(8,128)(2,1)}, u32[]{:S(2)}, u32[]{:S(2)}) collective-permute-start(bf16[4,2,2,64,512]{4,3,2,1,0:T(8,128)(2,1)} %pad_maximum_fusion.10), channel_id=1, source_target_pairs={{0,1},{1,0},{2,3},{3,2},{4,5},{5,4},{6,7},{7,6},{8,9},{9,8},{10,11... | collective-permute-start | bytes 3145736 | tf_op jit(solution)/shard_map/ppermute | solution.py:602
  96.9 70.1 %collective-permute-start.23 = (bf16[4,2,2,96,512]{4,3,2,1,0:T(8,128)(2,1)}, bf16[4,2,2,96,512]{4,3,2,1,0:T(8,128)(2,1)}, u32[]{:S(2)}, u32[]{:S(2)}) collective-permute-start(bf16[4,2,2,96,512]{4,3,2,1,0:T(8,128)(2,1)} %pad_maximum_fusion.7), channel_id=1, source_target_pairs={{0,1},{1,0},{2,3},{3,2},{4,5},{5,4},{6,7},{7,6},{8,9},{9,8},{10,11... | collective-permute-start | bytes 4718600 | tf_op jit(solution)/shard_map/ppermute | solution.py:602
  120.0 50.3 %collective-permute-start.17 = (bf16[4,2,2,144,512]{4,3,2,1,0:T(8,128)(2,1)}, bf16[4,2,2,144,512]{4,3,2,1,0:T(8,128)(2,1)}, u32[]{:S(2)}, u32[]{:S(2)}) collective-permute-start(bf16[4,2,2,144,512]{4,3,2,1,0:T(8,128)(2,1)} %pad_maximum_fusion.4), channel_id=1, source_target_pairs={{0,1},{1,0},{2,3},{3,2},{4,5},{5,4},{6,7},{7,6},{8,9},{9,8},{10,11... | collective-permute-start | bytes 7077896 | tf_op jit(solution)/shard_map/ppermute | solution.py:602
  146.5 29.4 %collective-permute-start.11 = (bf16[4,2,2,160,512]{4,3,0,1,2:T(8,128)(2,1)}, bf16[4,2,2,160,512]{4,3,0,1,2:T(8,128)(2,1)}, u32[]{:S(2)}, u32[]{:S(2)}) collective-permute-start(bf16[4,2,2,160,512]{4,3,0,1,2:T(8,128)(2,1)} %pad_maximum_fusion.3), channel_id=1, source_target_pairs={{0,1},{1,0},{2,3},{3,2},{4,5},{5,4},{6,7},{7,6},{8,9},{9,8},{10,11... | collective-permute-start | bytes 7864328 | tf_op jit(solution)/shard_map/ppermute | solution.py:602
  160.8 21.6 %all-to-all-start = ((f32[32,8,128]{2,1,0:T(8,128)}), f32[32,8,128]{2,1,0:T(8,128)S(1)}, u32[]{:S(2)}, u32[]{:S(2)}) async-start(f32[32,8,128]{2,1,0:T(8,128)} %get-tuple-element.54), calls=%async_computation | async-start | bytes 262144 | tf_op jit(solution)/shard_map/all_to_all | solution.py:735
  212.9 14.2 %all-to-all-start.2 = ((f32[32,8,128]{2,1,0:T(8,128)}), f32[32,8,128]{2,1,0:T(8,128)S(1)}, u32[]{:S(2)}, u32[]{:S(2)}) async-start(f32[32,8,128]{2,1,0:T(8,128)} %get-tuple-element.58), calls=%async_computation.2 | async-start | bytes 262144 | tf_op jit(solution)/shard_map/all_to_all | solution.py:735
  236.5 19.3 %all-to-all-start.3 = ((f32[32,8,512]{2,1,0:T(8,128)}), f32[32,8,512]{2,1,0:T(8,128)}, u32[]{:S(2)}, u32[]{:S(2)}) async-start(f32[32,8,512]{2,1,0:T(8,128)} %get-tuple-element.60), calls=%async_computation.3 | async-start | bytes 1048576 | tf_op jit(solution)/shard_map/all_to_all | solution.py:735
  273.0 18.5 %all-to-all-start.4 = ((f32[32,8,512]{2,1,0:T(8,128)}), f32[32,8,512]{2,1,0:T(8,128)S(1)}, u32[]{:S(2)}, u32[]{:S(2)}) async-start(f32[32,8,512]{2,1,0:T(8,128)} %get-tuple-element.62), calls=%async_computation.4 | async-start | bytes 1048576 | tf_op jit(solution)/shard_map/all_to_all | solution.py:735
  310.9 11.3 %all-to-all-start.5 = ((f32[32,8,128]{2,1,0:T(8,128)}), f32[32,8,128]{2,1,0:T(8,128)S(1)}, u32[]{:S(2)}, u32[]{:S(2)}) async-start(f32[32,8,128]{2,1,0:T(8,128)} %get-tuple-element.71), calls=%async_computation.5 | async-start | bytes 262144 | tf_op jit(solution)/shard_map/all_to_all | solution.py:735
  371.4 10.8 %all-to-all-start.6 = ((f32[32,8,128]{2,1,0:T(8,128)}), f32[32,8,128]{2,1,0:T(8,128)S(1)}, u32[]{:S(2)}, u32[]{:S(2)}) async-start(f32[32,8,128]{2,1,0:T(8,128)} %get-tuple-element.83), calls=%async_computation.6 | async-start | bytes 262144 | tf_op jit(solution)/shard_map/all_to_all | solution.py:735
  393.5 2.7 collective-permute-start.30
  395.5 30.8 %collective-permute-start.24 = (bf16[4,2,2,112,512]{4,3,2,1,0:T(8,128)(2,1)}, bf16[4,2,2,112,512]{4,3,2,1,0:T(8,128)(2,1)}, u32[]{:S(2)}, u32[]{:S(2)}) collective-permute-start(bf16[4,2,2,112,512]{4,3,2,1,0:T(8,128)(2,1)} %dynamic-slice_bitcast_fusion.1), channel_id=1, source_target_pairs={{0,1},{1,0},{2,3},{3,2},{4,5},{5,4},{6,7},{7,6},{8,9},{9,8},{10,11... | collective-permute-start | bytes 5505032 | tf_op jit(solution)/shard_map/ppermute | solution.py:602
  397.4 18.1 %collective-permute-start.31 = (bf16[4,2,64,512]{3,2,1,0:T(8,128)(2,1)S(1)}, bf16[4,2,64,512]{3,2,1,0:T(8,128)(2,1)S(1)}, u32[]{:S(2)}, u32[]{:S(2)}) collective-permute-start(bf16[4,2,64,512]{3,2,1,0:T(8,128)(2,1)S(1)} %dynamic-slice_bitcast_fusion.8), channel_id=1, source_target_pairs={{0,2},{1,3},{2,0},{3,1},{4,6},{5,7},{6,4},{7,5},{8,10},{9,11},{10,... | collective-permute-start | bytes 1572872 | tf_op jit(solution)/shard_map/ppermute | solution.py:602
  403.1 53.6 %collective-permute-start.46 = (bf16[4,2,2,144,512]{4,3,2,1,0:T(8,128)(2,1)}, bf16[4,2,2,144,512]{4,3,2,1,0:T(8,128)(2,1)}, u32[]{:S(2)}, u32[]{:S(2)}) collective-permute-start(bf16[4,2,2,144,512]{4,3,2,1,0:T(8,128)(2,1)} %dynamic-slice_bitcast_fusion), channel_id=1, source_target_pairs={{0,1},{1,0},{2,3},{3,2},{4,5},{5,4},{6,7},{7,6},{8,9},{9,8},{10,11... | collective-permute-start | bytes 7077896 | tf_op jit(solution)/shard_map/ppermute | solution.py:602
  415.7 8.7 %collective-permute-start.32 = (bf16[4,64,512]{2,1,0:T(8,128)(2,1)S(1)}, bf16[4,64,512]{2,1,0:T(8,128)(2,1)S(1)}, u32[]{:S(2)}, u32[]{:S(2)}) collective-permute-start(bf16[4,64,512]{2,1,0:T(8,128)(2,1)S(1)} %dynamic-slice_bitcast_fusion.10), channel_id=1, source_target_pairs={{0,4},{1,5},{2,6},{3,7},{4,0},{5,1},{6,2},{7,3},{8,12},{9,13},{10,... | collective-permute-start | bytes 786440 | tf_op jit(solution)/shard_map/ppermute | solution.py:602
  421.2 49.3 %collective-permute-start.38 = (bf16[4,2,2,160,512]{4,3,0,1,2:T(8,128)(2,1)}, bf16[4,2,2,160,512]{4,3,0,1,2:T(8,128)(2,1)}, u32[]{:S(2)}, u32[]{:S(2)}) collective-permute-start(bf16[4,2,2,160,512]{4,3,0,1,2:T(8,128)(2,1)} %bitcast.294), channel_id=1, source_target_pairs={{0,1},{1,0},{2,3},{3,2},{4,5},{5,4},{6,7},{7,6},{8,9},{9,8},{10,11... | collective-permute-start | bytes 7864328 | tf_op jit(solution)/shard_map/ppermute | solution.py:602
  424.5 6.5 %collective-permute-start.33 = (bf16[64,512]{1,0:T(8,128)(2,1)S(1)}, bf16[64,512]{1,0:T(8,128)(2,1)S(1)}, u32[]{:S(2)}, u32[]{:S(2)}) collective-permute-start(bf16[64,512]{1,0:T(8,128)(2,1)S(1)} %get-tuple-element.241), channel_id=1, source_target_pairs={{0,8},{1,9},{2,10},{3,11},{4,12},{5,13},{6,14},{7,15},{8,0},{9,1},... | collective-permute-start | bytes 196616 | tf_op jit(solution)/shard_map/ppermute | solution.py:602
  425.2 7.9 %collective-permute-start.34 = (bf16[64,512]{1,0:T(8,128)(2,1)S(1)}, bf16[64,512]{1,0:T(8,128)(2,1)S(1)}, u32[]{:S(2)}, u32[]{:S(2)}) collective-permute-start(bf16[64,512]{1,0:T(8,128)(2,1)S(1)} %get-tuple-element.243), channel_id=1, source_target_pairs={{0,16},{1,17},{2,18},{3,19},{4,20},{5,21},{6,22},{7,23},{8,24},{9,... | collective-permute-start | bytes 196616 | tf_op jit(solution)/shard_map/ppermute | solution.py:602
  426.3 6.7 %collective-permute-start.35 = (bf16[64,512]{1,0:T(8,128)(2,1)S(1)}, bf16[64,512]{1,0:T(8,128)(2,1)S(1)}, u32[]{:S(2)}, u32[]{:S(2)}) collective-permute-start(bf16[64,512]{1,0:T(8,128)(2,1)S(1)} %get-tuple-element.242), channel_id=1, source_target_pairs={{0,24},{1,25},{2,26},{3,27},{4,28},{5,29},{6,30},{7,31},{8,16},{9,... | collective-permute-start | bytes 196616 | tf_op jit(solution)/shard_map/ppermute | solution.py:602
  433.1 5.0 collective-permute-start.36
  435.6 20.4 %collective-permute-start.25 = (bf16[4,2,112,512]{3,2,1,0:T(8,128)(2,1)}, bf16[4,2,112,512]{3,2,1,0:T(8,128)(2,1)S(1)}, u32[]{:S(2)}, u32[]{:S(2)}) collective-permute-start(bf16[4,2,112,512]{3,2,1,0:T(8,128)(2,1)} %dynamic-slice_bitcast_fusion.5), channel_id=1, source_target_pairs={{0,2},{1,3},{2,0},{3,1},{4,6},{5,7},{6,4},{7,5},{8,10},{9,11},{10,... | collective-permute-start | bytes 2752520 | tf_op jit(solution)/shard_map/ppermute | solution.py:602
  438.1 10.9 %collective-permute-start.37 = (bf16[2,64,512]{2,1,0:T(8,128)(2,1)S(1)}, bf16[2,64,512]{2,1,0:T(8,128)(2,1)S(1)}, u32[]{:S(2)}, u32[]{:S(2)}) collective-permute-start(bf16[2,64,512]{2,1,0:T(8,128)(2,1)S(1)} %pad_maximum_fusion.33), channel_id=1, source_target_pairs={{0,1},{1,0},{2,3},{3,2},{4,5},{5,4},{6,7},{7,6},{8,9},{9,8},{10,11... | collective-permute-start | bytes 393224 | tf_op jit(solution)/shard_map/ppermute | solution.py:602
  456.3 9.5 %collective-permute-start.26 = (bf16[4,112,512]{2,1,0:T(8,128)(2,1)S(1)}, bf16[4,112,512]{2,1,0:T(8,128)(2,1)S(1)}, u32[]{:S(2)}, u32[]{:S(2)}) collective-permute-start(bf16[4,112,512]{2,1,0:T(8,128)(2,1)S(1)} %dynamic-slice_bitcast_fusion.9), channel_id=1, source_target_pairs={{0,4},{1,5},{2,6},{3,7},{4,0},{5,1},{6,2},{7,3},{8,12},{9,13},{10,... | collective-permute-start | bytes 1376264 | tf_op jit(solution)/shard_map/ppermute | solution.py:602
  460.0 33.6 %collective-permute-start.47 = (bf16[4,2,144,512]{3,2,1,0:T(8,128)(2,1)S(1)}, bf16[4,2,144,512]{3,2,1,0:T(8,128)(2,1)S(1)}, u32[]{:S(2)}, u32[]{:S(2)}) collective-permute-start(bf16[4,2,144,512]{3,2,1,0:T(8,128)(2,1)S(1)} %dynamic-slice_bitcast_fusion.3), channel_id=1, source_target_pairs={{0,2},{1,3},{2,0},{3,1},{4,6},{5,7},{6,4},{7,5},{8,10},{9,11},{10,... | collective-permute-start | bytes 3538952 | tf_op jit(solution)/shard_map/ppermute | solution.py:602
  466.0 7.1 %collective-permute-start.27 = (bf16[112,512]{1,0:T(8,128)(2,1)S(1)}, bf16[112,512]{1,0:T(8,128)(2,1)S(1)}, u32[]{:S(2)}, u32[]{:S(2)}) collective-permute-start(bf16[112,512]{1,0:T(8,128)(2,1)S(1)} %get-tuple-element.220), channel_id=1, source_target_pairs={{0,8},{1,9},{2,10},{3,11},{4,12},{5,13},{6,14},{7,15},{8,0},{9,1},... | collective-permute-start | bytes 344072 | tf_op jit(solution)/shard_map/ppermute | solution.py:602
  468.0 7.1 %collective-permute-start.28 = (bf16[112,512]{1,0:T(8,128)(2,1)S(1)}, bf16[112,512]{1,0:T(8,128)(2,1)S(1)}, u32[]{:S(2)}, u32[]{:S(2)}) collective-permute-start(bf16[112,512]{1,0:T(8,128)(2,1)S(1)} %get-tuple-element.222), channel_id=1, source_target_pairs={{0,16},{1,17},{2,18},{3,19},{4,20},{5,21},{6,22},{7,23},{8,24},{9,... | collective-permute-start | bytes 344072 | tf_op jit(solution)/shard_map/ppermute | solution.py:602
  469.8 6.7 %collective-permute-start.29 = (bf16[112,512]{1,0:T(8,128)(2,1)S(1)}, bf16[112,512]{1,0:T(8,128)(2,1)S(1)}, u32[]{:S(2)}, u32[]{:S(2)}) collective-permute-start(bf16[112,512]{1,0:T(8,128)(2,1)S(1)} %get-tuple-element.221), channel_id=1, source_target_pairs={{0,24},{1,25},{2,26},{3,27},{4,28},{5,29},{6,30},{7,31},{8,16},{9,... | collective-permute-start | bytes 344072 | tf_op jit(solution)/shard_map/ppermute | solution.py:602
  476.6 14.5 %collective-permute-start.54 = (bf16[96,512]{1,0:T(8,128)(2,1)S(1)}, bf16[96,512]{1,0:T(8,128)(2,1)S(1)}, u32[]{:S(2)}, u32[]{:S(2)}) collective-permute-start(bf16[96,512]{1,0:T(8,128)(2,1)S(1)} %slice.194), channel_id=1, source_target_pairs={{0,2},{1,3},{2,0},{3,1},{4,6},{5,7},{6,4},{7,5},{8,10},{9,11},{10,... | collective-permute-start | bytes 294920 | tf_op jit(solution)/shard_map/ppermute | solution.py:602
  479.8 35.0 %collective-permute-start.39 = (bf16[4,2,160,512]{3,2,0,1:T(8,128)(2,1)S(1)}, bf16[4,2,160,512]{3,2,0,1:T(8,128)(2,1)S(1)}, u32[]{:S(2)}, u32[]{:S(2)}) collective-permute-start(bf16[4,2,160,512]{3,2,0,1:T(8,128)(2,1)S(1)} %dynamic-slice_bitcast_fusion.2), channel_id=1, source_target_pairs={{0,2},{1,3},{2,0},{3,1},{4,6},{5,7},{6,4},{7,5},{8,10},{9,11},{10,... | collective-permute-start | bytes 3932168 | tf_op jit(solution)/shard_map/ppermute | solution.py:602
  491.1 1.5 collective-permute-start.55
  494.8 25.6 %collective-permute-start.48 = (bf16[4,144,512]{2,1,0:T(8,128)(2,1)}, bf16[4,144,512]{2,1,0:T(8,128)(2,1)}, u32[]{:S(2)}, u32[]{:S(2)}) collective-permute-start(bf16[4,144,512]{2,1,0:T(8,128)(2,1)} %dynamic-slice_bitcast_fusion.7), channel_id=1, source_target_pairs={{0,4},{1,5},{2,6},{3,7},{4,0},{5,1},{6,2},{7,3},{8,12},{9,13},{10,... | collective-permute-start | bytes 1769480 | tf_op jit(solution)/shard_map/ppermute | solution.py:602
  516.1 12.7 %collective-permute-start.40 = (bf16[4,160,512]{2,1,0:T(8,128)(2,1)}, bf16[4,160,512]{2,1,0:T(8,128)(2,1)S(1)}, u32[]{:S(2)}, u32[]{:S(2)}) collective-permute-start(bf16[4,160,512]{2,1,0:T(8,128)(2,1)} %dynamic-slice_bitcast_fusion.6), channel_id=1, source_target_pairs={{0,4},{1,5},{2,6},{3,7},{4,0},{5,1},{6,2},{7,3},{8,12},{9,13},{10,... | collective-permute-start | bytes 1966088 | tf_op jit(solution)/shard_map/ppermute | solution.py:602
  521.7 11.6 %collective-permute-start.49 = (bf16[144,512]{1,0:T(8,128)(2,1)S(1)}, bf16[144,512]{1,0:T(8,128)(2,1)S(1)}, u32[]{:S(2)}, u32[]{:S(2)}) collective-permute-start(bf16[144,512]{1,0:T(8,128)(2,1)S(1)} %get-tuple-element.213), channel_id=1, source_target_pairs={{0,8},{1,9},{2,10},{3,11},{4,12},{5,13},{6,14},{7,15},{8,0},{9,1},... | collective-permute-start | bytes 442376 | tf_op jit(solution)/shard_map/ppermute | solution.py:602
  524.4 13.6 %collective-permute-start.50 = (bf16[144,512]{1,0:T(8,128)(2,1)S(1)}, bf16[144,512]{1,0:T(8,128)(2,1)S(1)}, u32[]{:S(2)}, u32[]{:S(2)}) collective-permute-start(bf16[144,512]{1,0:T(8,128)(2,1)S(1)} %get-tuple-element.215), channel_id=1, source_target_pairs={{0,16},{1,17},{2,18},{3,19},{4,20},{5,21},{6,22},{7,23},{8,24},{9,... | collective-permute-start | bytes 442376 | tf_op jit(solution)/shard_map/ppermute | solution.py:602
  525.6 12.4 %collective-permute-start.51 = (bf16[144,512]{1,0:T(8,128)(2,1)S(1)}, bf16[144,512]{1,0:T(8,128)(2,1)S(1)}, u32[]{:S(2)}, u32[]{:S(2)}) collective-permute-start(bf16[144,512]{1,0:T(8,128)(2,1)S(1)} %get-tuple-element.214), channel_id=1, source_target_pairs={{0,24},{1,25},{2,26},{3,27},{4,28},{5,29},{6,30},{7,31},{8,16},{9,... | collective-permute-start | bytes 442376 | tf_op jit(solution)/shard_map/ppermute | solution.py:602
  529.0 11.1 %collective-permute-start.41 = (bf16[160,512]{1,0:T(8,128)(2,1)S(1)}, bf16[160,512]{1,0:T(8,128)(2,1)S(1)}, u32[]{:S(2)}, u32[]{:S(2)}) collective-permute-start(bf16[160,512]{1,0:T(8,128)(2,1)S(1)} %get-tuple-element.206), channel_id=1, source_target_pairs={{0,8},{1,9},{2,10},{3,11},{4,12},{5,13},{6,14},{7,15},{8,0},{9,1},... | collective-permute-start | bytes 491528 | tf_op jit(solution)/shard_map/ppermute | solution.py:602
  533.2 15.7 %collective-permute-start.42 = (bf16[160,512]{1,0:T(8,128)(2,1)S(1)}, bf16[160,512]{1,0:T(8,128)(2,1)S(1)}, u32[]{:S(2)}, u32[]{:S(2)}) collective-permute-start(bf16[160,512]{1,0:T(8,128)(2,1)S(1)} %get-tuple-element.208), channel_id=1, source_target_pairs={{0,16},{1,17},{2,18},{3,19},{4,20},{5,21},{6,22},{7,23},{8,24},{9,... | collective-permute-start | bytes 491528 | tf_op jit(solution)/shard_map/ppermute | solution.py:602
  533.4 15.6 %collective-permute-start.43 = (bf16[160,512]{1,0:T(8,128)(2,1)S(1)}, bf16[160,512]{1,0:T(8,128)(2,1)S(1)}, u32[]{:S(2)}, u32[]{:S(2)}) collective-permute-start(bf16[160,512]{1,0:T(8,128)(2,1)S(1)} %get-tuple-element.207), channel_id=1, source_target_pairs={{0,24},{1,25},{2,26},{3,27},{4,28},{5,29},{6,30},{7,31},{8,16},{9,... | collective-permute-start | bytes 491528 | tf_op jit(solution)/shard_map/ppermute | solution.py:602
  538.1 12.7 %collective-permute-start.52 = (bf16[144,512]{1,0:T(8,128)(2,1)S(1)}, bf16[144,512]{1,0:T(8,128)(2,1)S(1)}, u32[]{:S(2)}, u32[]{:S(2)}) collective-permute-start(bf16[144,512]{1,0:T(8,128)(2,1)S(1)} %fusion.19), channel_id=1, source_target_pairs={{0,2},{1,3},{2,0},{3,1},{4,6},{5,7},{6,4},{7,5},{8,10},{9,11},{10,... | collective-permute-start | bytes 442376 | tf_op jit(solution)/shard_map/ppermute | solution.py:602
  549.0 5.4 collective-permute-start.44
  550.9 3.6 collective-permute-start.53
  554.5 1.7 collective-permute-start.45
  (26 other events, 131.7 us)
